TPU v7x, 256 devices: a whole 4x4x8 slice. The times are simulated.
256 devices in a mesh: tens: 64 (over z, y, core), mat: 4 (over x).
Axes of the slice: x: 4, y: 4, z: 8, core: 2. Of those that a mesh axis runs over, the one named last changes fastest.
Arguments:
- tiles: bfloat16 [2048, 64, 4096], P(('tens', 'mat')), may hold values from -6 to 6
- tile_dest: int32 [2048], P(('tens', 'mat')), may hold values from 0 to 63
- tile_aux: int32 [2048], P(('tens', 'mat')), may hold values from 0 to 1
- tile_row: int32 [2048], P(('tens', 'mat')), may hold values from 0 to 15
- tile_col: int32 [2048], P(('tens', 'mat')), may hold values from 0 to 15
- green_occ: bfloat16 [1024, 1024], P(('tens', 'mat')), may hold values from -0.75 to 0.75
- green_virt: bfloat16 [1024, 1024], P(('tens', 'mat')), may hold values from -0.75 to 0.75
Outputs:
- chi: float32 [8192, 64], P('tens')
All inputs are finite; a program needn't handle non-finite values.
Results may differ from a plain program's by a relative error of at most 0.0041.
Values may be sent and summed in bfloat16 or wider, within the bound.
No kernel may reach another device: no remote copies, remote signals or barrier semaphores. Data moves between devices by JAX's collectives and lax.ppermute only.
A program may use at most 128 MiB of HBM per device.

v0:
```python
import jax
import jax.numpy as jnp
from jax import lax
from jax.experimental import pallas as pl
from jax.experimental.pallas import tpu as pltpu
from jax.sharding import Mesh, PartitionSpec as P

BS = 64
NA = 16
AUX = 2
ZHL = ("z", "h", "l")
TENS = ("z", "h", "l", "c")
ALL = ("z", "h", "l", "c", "x")
NX = 4
F32, BF16 = jnp.float32, jnp.bfloat16
VMEM = pl.BlockSpec(memory_space=pltpu.VMEM)
SMEM = pl.BlockSpec(memory_space=pltpu.SMEM)


def shift(values, k):
    return lax.ppermute(values, "x", [(i, (i + k) % NX) for i in range(NX)])


def nt(a, b):
    return lax.dot_general(a, b, (((1,), (1,)), ((), ())), preferred_element_type=F32)


def eye(n):
    rows = lax.broadcasted_iota(jnp.int32, (n, n), 0)
    return jnp.where(rows == lax.broadcasted_iota(jnp.int32, (n, n), 1), 1.0, 0.0).astype(BF16)


def swap_kernel(t_ref, o_ref, scr):
    wide, narrow = eye(256), eye(128)
    for s in range(16):
        cut = slice(s * 256, s * 256 + 256)
        scr[cut, :] = nt(wide, jnp.concatenate([t_ref[0, :, cut], t_ref[1, :, cut]], axis=0))
    for s in range(16):
        cut = slice(s * 256, s * 256 + 256)
        rows = jnp.concatenate([scr[pl.ds(4 * s + k, BS, stride=BS), :] for k in range(4)], axis=0)
        back = nt(narrow, rows.astype(BF16)).astype(BF16)
        o_ref[0, :, cut] = back[:BS]
        o_ref[1, :, cut] = back[BS:]


def swap(tiles):
    count = tiles.shape[0]
    spec = pl.BlockSpec((2, BS, BS * BS), lambda i: (i, 0, 0))
    return pl.pallas_call(
        swap_kernel,
        grid=(count // 2,),
        out_shape=jax.ShapeDtypeStruct(tiles.shape, tiles.dtype),
        in_specs=[spec],
        out_specs=spec,
        scratch_shapes=[pltpu.VMEM((BS * BS, 128), F32)],
        cost_estimate=pl.CostEstimate(flops=3_000_000_000, bytes_accessed=2 * tiles.size * 2, transcendentals=0),
        compiler_params=pltpu.CompilerParams(vmem_limit_bytes=32 * 1024 * 1024),
        name="swap",
    )(tiles)


def pick_kernel(core_ref, hot_ref, own_ref, other_ref, o_ref):
    core = core_ref[0]
    for side, ref in ((core, own_ref), (1 - core, other_ref)):
        for l in range(2):
            for ih in range(2):
                for arr in range(2):
                    first = (ih * 2 + arr) * NA
                    table = jnp.concatenate([ref[2 * b + l, first:first + NA, :] for b in range(NA)], axis=0)
                    got = jnp.dot(hot_ref[arr], table, preferred_element_type=F32).astype(BF16)
                    for k in range(NX):
                        o_ref[k, l, side, ih, arr] = got[k * NA:(k + 1) * NA]


def tile_kernel(me_ref, t_ref, ts_ref, g0, g1, g2, g3, o_ref, gscr, scr, yz):
    step = pl.program_id(0)
    me = me_ref[0]

    @pl.when(step == 0)
    def _():
        for k, ref in enumerate((g0, g1, g2, g3)):
            start = pl.multiple_of(((me - k + NX) & 3) * 256, 256)
            gscr[pl.ds(start, 256), :] = ref[...].reshape(256, 128).astype(F32)

    m = lax.broadcasted_iota(jnp.int32, (BS, BS), 0)
    place = ((m & 1) << 5) + (((m >> 2) & 3) << 3) + ((m >> 5) << 2) + (((m >> 4) & 1) << 1) + ((m >> 1) & 1)
    order = jnp.where(place == lax.broadcasted_iota(jnp.int32, (BS, BS), 1), 1.0, 0.0).astype(BF16)
    low = lax.broadcasted_iota(jnp.int32, (32, 128), 1) < BS
    low64 = lax.broadcasted_iota(jnp.int32, (BS, 128), 1) < BS

    def halves(arr, q):
        rows = gscr[pl.ds(arr * 16 + step * 2 + q, 32, stride=32), :]
        turned = pltpu.roll(rows, BS, 1)
        both = jnp.concatenate([jnp.where(low, rows, turned), jnp.where(low, turned, rows)], axis=0)
        block = jnp.dot(order, both.astype(BF16), preferred_element_type=F32)
        return jnp.where(low64, block, 0.0), jnp.where(low64, 0.0, block)

    def twice_t(q):
        return jnp.concatenate(halves(1, q), axis=0).T.astype(BF16)

    def four(q):
        left, right = (h.astype(BF16) for h in halves(0, q))
        none = jnp.zeros((BS, 128), BF16)
        return jnp.concatenate([
            jnp.concatenate([jnp.concatenate([left, none], axis=1), jnp.concatenate([right, none], axis=1)], axis=0),
            jnp.concatenate([jnp.concatenate([none, left], axis=1), jnp.concatenate([none, right], axis=1)], axis=0),
        ], axis=0)

    virt = jnp.concatenate([twice_t(0), twice_t(1)], axis=1)
    zero = jnp.zeros((BS, 128), BF16)
    for s in range(16):
        a = t_ref[0, :, s * 256:s * 256 + 128]
        b = t_ref[0, :, s * 256 + 128:s * 256 + 256]
        left = jnp.concatenate([a, zero, b, zero], axis=0)
        right = jnp.concatenate([zero, a, zero, b], axis=0)
        out = nt(virt, jnp.concatenate([left, right], axis=1))
        scr[s * 256:s * 256 + 128, :] = out[:, :128]
        scr[s * 256 + 128:s * 256 + 256, :] = out[:, 128:]
    same, cross = four(0), four(1)
    for s in range(16):
        cut = slice(s * 256, s * 256 + 256)
        yz[:BS, cut] = nt(ts_ref[0, :, cut], same).astype(BF16)
    for s in range(16):
        cut = slice(s * 256, s * 256 + 256)
        yz[BS:, cut] = nt(t_ref[0, :, cut], cross).astype(BF16)
    acc = jnp.zeros((128, 128), F32)
    for s in range(16):
        rows = jnp.concatenate([scr[pl.ds(4 * s + k, BS, stride=BS), :] for k in range(4)], axis=0)
        acc += jnp.dot(yz[:, s * 256:s * 256 + 256], rows.astype(BF16), preferred_element_type=F32)
    turned = acc.T * (1.0 / BS)
    pair = turned[:BS] + pltpu.roll(turned[BS:], BS, 1)
    packed = jnp.where(low, pair[:32], pltpu.roll(pair[32:], BS, 1))
    for k in range(NX):
        o_ref[k, 0] = packed[8 * k:8 * k + 8]


def tile_pairs(me, tiles, swapped, got):
    count = tiles.shape[0]
    tile = pl.BlockSpec((1, BS, BS * BS), lambda i: (i, 0, 0))
    return pl.pallas_call(
        tile_kernel,
        grid=(count,),
        out_shape=jax.ShapeDtypeStruct((NX, count, 8, 128), F32),
        in_specs=[SMEM, tile, tile] + [VMEM] * 4,
        out_specs=pl.BlockSpec((NX, 1, 8, 128), lambda i: (0, i, 0, 0)),
        scratch_shapes=[pltpu.VMEM((1024, 128), F32), pltpu.VMEM((BS * BS, 128), F32), pltpu.VMEM((128, BS * BS), BF16)],
        compiler_params=pltpu.CompilerParams(vmem_limit_bytes=32 * 1024 * 1024),
        name="tile_pairs",
    )(me, tiles, swapped, *got)


def place_kernel(i0, i1, i2, i3, t0, t1, t2, t3, o_ref, total):
    total[...] = jnp.zeros_like(total)
    for info, terms in ((i0, t0), (i1, t1), (i2, t2), (i3, t3)):
        for t in range(terms.shape[0]):
            at = info[2, t]
            total[at] += terms[t]
    o_ref[...] = total[...].reshape(o_ref.shape).astype(BF16)


def place(infos, terms):
    return pl.pallas_call(
        place_kernel,
        out_shape=jax.ShapeDtypeStruct((64, 16, 128), BF16),
        in_specs=[SMEM] * 4 + [VMEM] * 4,
        out_specs=VMEM,
        scratch_shapes=[pltpu.VMEM((128, 8, 128), F32)],
        name="place",
    )(*infos, *terms)


def sum_kernel(s_ref, o_ref):
    o_ref[...] = jnp.sum(s_ref[...].astype(F32), axis=0)


def finish_kernel(me_ref, p0, p1, p2, p3, o_ref, whole):
    me = me_ref[0]
    for k, ref in enumerate((p0, p1, p2, p3)):
        x = (me - k + NX) & 3
        for aux in range(AUX):
            whole[aux, x] = ref[8 * aux:8 * aux + 8]
    for aux in range(AUX):
        rows = whole[aux].reshape(32, 128)
        o_ref[aux * BS:aux * BS + 32, :] = rows[:, :BS]
        o_ref[aux * BS + 32:(aux + 1) * BS, :] = pltpu.roll(rows, BS, 1)[:, :BS]


def shards(tiles, tile_dest, tile_aux, tile_row, tile_col, green_occ, green_virt):
    count = tiles.shape[0]
    x = lax.axis_index("x")
    me = x.reshape(1)
    info = jnp.stack([tile_row, tile_col, tile_dest * AUX + tile_aux])
    infos = [info] + [shift(info, k) for k in range(1, NX)]

    with jax.named_scope("gather_rows"):
        own = jnp.stack([green_occ, green_virt]).reshape(2, 2, 2, NA, BS)
        own = own.transpose(1, 0, 3, 2, 4).reshape(4 * NA, 2 * BS)
        rows = lax.all_to_all(jnp.broadcast_to(own[None], (32, 4 * NA, 2 * BS)), ZHL, 0, 0)
        other = lax.ppermute(rows, "c", [(0, 1), (1, 0)])
    swapped = swap(tiles)

    with jax.named_scope("pick_blocks"):
        r, c = (jnp.stack([i[j] for i in infos]) for j in (0, 1))
        occ = jnp.stack([r * NA + r, r * NA + c], axis=-1)
        virt = jnp.stack([c * NA + c, c * NA + r], axis=-1)
        wanted = jnp.stack([occ, virt]).reshape(2, NX * count * 2)
        hot = (wanted[..., None] == jnp.arange(NA * NA, dtype=jnp.int32)).astype(BF16)
        picked = pl.pallas_call(
            pick_kernel,
            out_shape=jax.ShapeDtypeStruct((NX, 2, 2, 2, 2, NA, 128), BF16),
            in_specs=[SMEM] + [VMEM] * 3,
            out_specs=VMEM,
            name="pick",
        )(lax.axis_index("c").reshape(1), hot, rows, other)
        got = [picked[0]] + [None] * (NX - 1)
        for k in range(1, NX):
            got[NX - k] = shift(picked[k], NX - k)

    pairs = tile_pairs(me, tiles, swapped, got)

    with jax.named_scope("owners"):
        terms = [lax.dynamic_index_in_dim(pairs, x, 0, keepdims=False)]
        for k in range(1, NX):
            terms.append(shift(lax.dynamic_index_in_dim(pairs, (x + k) % NX, 0, keepdims=False), k))
        spread = lax.all_to_all(place(infos, terms), TENS, 0, 0)
        owned = pl.pallas_call(
            sum_kernel, out_shape=jax.ShapeDtypeStruct((16, 128), F32), in_specs=[VMEM], out_specs=VMEM, name="sum",
        )(spread)
        parts = [owned] + [shift(owned, k) for k in range(1, NX)]
        return pl.pallas_call(
            finish_kernel,
            out_shape=jax.ShapeDtypeStruct((AUX * BS, BS), F32),
            in_specs=[SMEM] + [VMEM] * 4,
            out_specs=VMEM,
            scratch_shapes=[pltpu.VMEM((AUX, NX, 8, 128), F32)],
            name="finish",
        )(me, *parts)


def solution(mesh):
    fine = Mesh(mesh.devices.reshape(8, 2, 2, 2, 4), ALL)
    return jax.shard_map(
        shards,
        mesh=fine,
        in_specs=(P(ALL, None, None), P(ALL), P(ALL), P(ALL), P(ALL), P(ALL, None), P(ALL, None)),
        out_specs=P(TENS, None),
        check_vma=False,
    )
```

profile of v0, /device:TPU:1, one launch (start us, length us, event | category | flops | bytes accessed | tf_op | source)
XLA Modules:
  0.0 134.8 jit_solution(17119512875261333146)
XLA Ops:
  0.0 0.7 add_bitcast_fusion
  0.7 0.7 pad_add_fusion.2.i0
  1.4 2.1 %collective-permute-start = (s32[3,8]{1,0:T(4,128)S(1)}, s32[3,8]{1,0:T(4,128)S(1)}, u32[]{:S(2)}, u32[]{:S(2)}) collective-permute-start(s32[3,8]{1,0:T(4,128)S(1)} %pad_add_fusion.2.i0), channel_id=1, source_target_pairs={{0,1},{1,2},{2,3},{3,0},{4,5},{5,6},{6,7},{7,4},{8,9},{9,10},{10,1... | collective-permute-start | bytes 296 | tf_op jit(solution)/shard_map/ppermute | solution.py:21
  3.5 2.5 %collective-permute-start.1 = (s32[3,8]{1,0:T(4,128)S(1)}, s32[3,8]{1,0:T(4,128)S(1)}, u32[]{:S(2)}, u32[]{:S(2)}) collective-permute-start(s32[3,8]{1,0:T(4,128)S(1)} %pad_add_fusion.2.i0), channel_id=1, source_target_pairs={{0,2},{1,3},{2,0},{3,1},{4,6},{5,7},{6,4},{7,5},{8,10},{9,11},{10,... | collective-permute-start | bytes 296 | tf_op jit(solution)/shard_map/ppermute | solution.py:21
  5.9 1.2 collective-permute-start.2
  7.1 0.8 stack.81
  7.9 0.8 stack.82
  8.7 0.1 broadcast_in_dim.8
  8.8 0.9 broadcast_in_dim.9
  9.7 11.2 %all-to-all-start = ((bf16[32,64,128]{2,1,0:T(8,128)(2,1)}), bf16[32,64,128]{2,1,0:T(8,128)(2,1)S(1)}, u32[]{:S(2)}, u32[]{:S(2)}) async-start(bf16[32,64,128]{2,1,0:T(8,128)(2,1)} %broadcast_in_dim.9), calls=%async_computation | async-start | bytes 1048576 | tf_op jit(solution)/shard_map/gather_rows/all_to_all | solution.py:198
  20.9 0.0 collective-permute-done.i1
  20.9 0.0 copy-start.13
  21.0 0.0 collective-permute-done.1.i2
  21.0 0.0 collective-permute-done.2.i3
  21.0 0.0 copy-start.15
  21.0 0.7 multiply_add_fusion.3
  21.7 0.7 multiply_add_fusion.2
  22.4 13.7 %all-to-all-done.own_ref = bf16[32,64,128]{2,1,0:T(8,128)(2,1)S(1)} async-done(((bf16[32,64,128]{2,1,0:T(8,128)(2,1)}), bf16[32,64,128]{2,1,0:T(8,128)(2,1)S(1)}, u32[]{:S(2)}, u32[]{:S(2)}) %all-to-all-start) | async-done | bytes 524320 | tf_op jit(solution)/shard_map/gather_rows/all_to_all | solution.py:198
  36.1 3.7 %collective-permute-start.3 = (bf16[32,64,128]{2,1,0:T(8,128)(2,1)S(1)}, bf16[32,64,128]{2,1,0:T(8,128)(2,1)S(1)}, u32[]{:S(2)}, u32[]{:S(2)}) collective-permute-start(bf16[32,64,128]{2,1,0:T(8,128)(2,1)S(1)} %all-to-all-done.own_ref), channel_id=1, source_target_pairs={{0,4},{4,0},{1,5},{5,1},{2,6},{6,2},{3,7},{7,3},{8,12},{12,8},{9,1... | collective-permute-start | bytes 1572872 | tf_op jit(solution)/shard_map/gather_rows/ppermute | solution.py:199
  39.7 0.1 copy.13
  39.8 0.1 stack.79
  40.0 0.1 copy.12
  40.1 0.1 stack.77
  40.2 0.7 fusion.hot_ref
  40.9 0.4 collective-permute-done.3.other_ref
  41.3 0.8 copy-done.5
  42.1 2.2 %pick.1 = bf16[4,2,2,2,2,16,128]{6,5,4,3,2,1,0:T(8,128)(2,1)} custom-call(s32[1]{0:T(128)} %bitcast.4.core_ref, bf16[2,64,256]{2,1,0:T(8,128)(2,1)} %fusion.hot_ref, bf16[32,64,128]{2,1,0:T(8,128)(2,1)} %copy-done.4, bf16[32,64,128]{2,1,0:T(8,128)(2,1)} %copy-done.5), custom_call_target="tpu_custom_call" | custom-call | tf_op jit(solution)/shard_map/pick_blocks/pick/pallas_call | solution.py:208
  44.3 1.0 slice_bitcast_fusion
  45.2 0.4 collective-permute-start.4
  45.6 0.8 collective-permute-start.5
  46.5 1.7 %collective-permute-start.6 = (bf16[2,2,2,2,16,128]{5,4,3,2,1,0:T(8,128)(2,1)S(1)}, bf16[2,2,2,2,16,128]{5,4,3,2,1,0:T(8,128)(2,1)S(1)}, u32[]{:S(2)}, u32[]{:S(2)}) collective-permute-start(bf16[2,2,2,2,16,128]{5,4,3,2,1,0:T(8,128)(2,1)S(1)} %get-tuple-element.9), channel_id=1, source_target_pairs={{0,3},{1,0},{2,1},{3,2},{4,7},{5,4},{6,5},{7,6},{8,11},{9,8},{10,9... | collective-permute-start | bytes 196616 | tf_op jit(solution)/shard_map/pick_blocks/ppermute | solution.py:21
  48.1 2.2 %copy-done = bf16[8,64,4096]{2,1,0:T(8,128)(2,1)S(1)} copy-done((bf16[8,64,4096]{2,1,0:T(8,128)(2,1)S(1)}, bf16[8,64,4096]{2,1,0:T(8,128)(2,1)}, u32[]{:S(2)}) %copy-start) | copy-done | bytes 4194328
  50.3 8.1 %swap.1.ts_ref = bf16[8,64,4096]{2,1,0:T(8,128)(2,1)S(1)} custom-call(bf16[8,64,4096]{2,1,0:T(8,128)(2,1)S(1)} %copy-done), custom_call_target="tpu_custom_call" | custom-call | flops 3000000000 | bytes 8388608 | tf_op jit(solution)/shard_map/swap/pallas_call | solution.py:49
  58.4 2.0 %copy-done.2 = bf16[8,64,4096]{2,1,0:T(8,128)(2,1)} copy-done((bf16[8,64,4096]{2,1,0:T(8,128)(2,1)}, bf16[8,64,4096]{2,1,0:T(8,128)(2,1)S(1)}, u32[]{:S(2)}) %copy-start.2) | copy-done | bytes 4194328
  60.4 0.0 collective-permute-done.4.g1
  60.4 0.0 collective-permute-done.5.g2
  60.4 0.0 collective-permute-done.6.g3
  60.4 0.0 copy-start.1
  60.4 2.2 %copy-done.1 = bf16[8,64,4096]{2,1,0:T(8,128)(2,1)S(1)} copy-done((bf16[8,64,4096]{2,1,0:T(8,128)(2,1)S(1)}, bf16[8,64,4096]{2,1,0:T(8,128)(2,1)}, u32[]{:S(2)}) %copy-start.1) | copy-done | bytes 4194328
  62.6 2.2 %copy-done.3 = bf16[8,64,4096]{2,1,0:T(8,128)(2,1)S(1)} copy-done((bf16[8,64,4096]{2,1,0:T(8,128)(2,1)S(1)}, bf16[8,64,4096]{2,1,0:T(8,128)(2,1)}, u32[]{:S(2)}) %copy-start.3) | copy-done | bytes 4194328
  64.8 28.7 %tile_pairs.1 = f32[4,8,8,128]{3,2,1,0:T(8,128)S(1)} custom-call(s32[1]{0:T(128)} %bitcast.me_ref, bf16[8,64,4096]{2,1,0:T(8,128)(2,1)S(1)} %copy-done.1, bf16[8,64,4096]{2,1,0:T(8,128)(2,1)S(1)} %copy-done.3, bf16[2,2,2,2,16,128]{5,4,3,2,1,0:T(8,128)(2,1)S(1)} %get-tuple-element.12.g0, bf16[2,2,2,2,16,128]{5,4,3,2,1,0:T(8,128)(2,1)S(1)} %collective-permute-done.4.g1, ...), custom_call_target="tpu_custom_call" | custom-call | tf_op jit(solution)/shard_map/tile_pairs/pallas_call | solution.py:140
  93.4 0.6 dynamic-slice_bitcast_fusion
  94.1 0.5 collective-permute-start.7
  94.5 1.8 %collective-permute-start.8 = (f32[8,8,128]{2,1,0:T(8,128)S(1)}, f32[8,8,128]{2,1,0:T(8,128)S(1)}, u32[]{:S(2)}, u32[]{:S(2)}) collective-permute-start(f32[8,8,128]{2,1,0:T(8,128)S(1)} %get-tuple-element.14), channel_id=1, source_target_pairs={{0,2},{1,3},{2,0},{3,1},{4,6},{5,7},{6,4},{7,5},{8,10},{9,11},{10,... | collective-permute-start | bytes 98312 | tf_op jit(solution)/shard_map/owners/ppermute | solution.py:21
  96.3 2.1 %collective-permute-start.9 = (f32[8,8,128]{2,1,0:T(8,128)S(1)}, f32[8,8,128]{2,1,0:T(8,128)S(1)}, u32[]{:S(2)}, u32[]{:S(2)}) collective-permute-start(f32[8,8,128]{2,1,0:T(8,128)S(1)} %get-tuple-element.13), channel_id=1, source_target_pairs={{0,3},{1,0},{2,1},{3,2},{4,7},{5,4},{6,5},{7,6},{8,11},{9,8},{10,9... | collective-permute-start | bytes 98312 | tf_op jit(solution)/shard_map/owners/ppermute | solution.py:21
  98.4 0.0 collective-permute-done.7.t1
  98.4 0.6 collective-permute-done.8.t2
  98.9 0.5 collective-permute-done.9.t3
  99.4 0.0 copy-done.6
  99.4 0.1 copy-done.7
  99.5 0.5 copy-done.8
  100.0 1.8 %place.1 = bf16[64,16,128]{2,1,0:T(8,128)(2,1)} custom-call(s32[3,8]{1,0:T(4,128)} %copy-done.9, s32[3,8]{1,0:T(4,128)} %copy-done.13, s32[3,8]{1,0:T(4,128)} %copy-done.14, s32[3,8]{1,0:T(4,128)} %copy-done.15, f32[8,8,128]{2,1,0:T(8,128)} %get-tuple-element.16.t0, f32[8,8,128]{2,1,0:T(8,128)} %copy-done.6, f32[8,8,128]{2,1,0:T(8,128)} %copy-done.7, ...), custom_call_target="tpu_custom_call" | custom-call | tf_op jit(solution)/shard_map/owners/place/pallas_call | solution.py:162
  101.8 20.7 %all_to_all.10.s_ref = bf16[64,16,128]{2,1,0:T(8,128)(2,1)} all-to-all(bf16[64,16,128]{2,1,0:T(8,128)(2,1)} %place.1), channel_id=1, replica_groups=mesh['z'=8,'h'=2,'l'=2,'c'=2,'x'=4] {'z','h','l','c'}, dimensions={0} | all-to-all | bytes 524288 | tf_op jit(solution)/shard_map/owners/all_to_all | solution.py:225
  122.4 1.6 %sum.1.p0 = f32[16,128]{1,0:T(8,128)} custom-call(bf16[64,16,128]{2,1,0:T(8,128)(2,1)} %all_to_all.10.s_ref), custom_call_target="tpu_custom_call" | custom-call | tf_op jit(solution)/shard_map/owners/sum/pallas_call | solution.py:226
  124.1 1.1 collective-permute-start.10
  125.1 3.4 %collective-permute-start.11 = (f32[16,128]{1,0:T(8,128)}, f32[16,128]{1,0:T(8,128)S(1)}, u32[]{:S(2)}, u32[]{:S(2)}) collective-permute-start(f32[16,128]{1,0:T(8,128)} %sum.1.p0), channel_id=1, source_target_pairs={{0,2},{1,3},{2,0},{3,1},{4,6},{5,7},{6,4},{7,5},{8,10},{9,11},{10,... | collective-permute-start | bytes 24584 | tf_op jit(solution)/shard_map/owners/ppermute | solution.py:21
  128.5 0.0 collective-permute-start.12
  128.5 0.1 collective-permute-done.10.p1
  128.6 1.3 collective-permute-done.11.p2
  129.8 1.4 %collective-permute-done.12.p3 = f32[16,128]{1,0:T(8,128)S(1)} collective-permute-done((f32[16,128]{1,0:T(8,128)}, f32[16,128]{1,0:T(8,128)S(1)}, u32[]{:S(2)}, u32[]{:S(2)}) %collective-permute-start.12) | collective-permute-done | bytes 8224 | tf_op jit(solution)/shard_map/owners/ppermute | solution.py:21
  131.2 0.0 copy-done.11
  131.2 0.6 copy-done.12
  131.8 1.5 %finish.1 = f32[128,64]{1,0:T(8,128)} custom-call(s32[1]{0:T(128)} %bitcast.me_ref, f32[16,128]{1,0:T(8,128)} %sum.1.p0, f32[16,128]{1,0:T(8,128)} %copy-done.10, f32[16,128]{1,0:T(8,128)} %copy-done.11, f32[16,128]{1,0:T(8,128)} %copy-done.12), custom_call_target="tpu_custom_call" | custom-call | tf_op jit(solution)/shard_map/owners/finish/pallas_call | solution.py:230
  133.3 1.5 %copy.15 = f32[128,64]{0,1:T(8,128)} copy(f32[128,64]{1,0:T(8,128)} %finish.1) | data formatting | bytes 65536 | tf_op jit(solution)/shard_map/owners/finish/pallas_call | solution.py:230
  (28 shorter events, 0.1 us)
Async XLA Ops:
  1.4 57.0 %copy-start.9 = (s32[3,8]{1,0:T(4,128)}, s32[3,8]{1,0:T(4,128)S(1)}, u32[]{:S(2)}) copy-start(s32[3,8]{1,0:T(4,128)S(1)} %pad_add_fusion.2.i0) | copy-start | bytes 292
  1.4 19.6 %collective-permute-start = (s32[3,8]{1,0:T(4,128)S(1)}, s32[3,8]{1,0:T(4,128)S(1)}, u32[]{:S(2)}, u32[]{:S(2)}) collective-permute-start(s32[3,8]{1,0:T(4,128)S(1)} %pad_add_fusion.2.i0), channel_id=1, source_target_pairs={{0,1},{1,2},{2,3},{3,0},{4,5},{5,6},{6,7},{7,4},{8,9},{9,10},{10,1... | collective-permute-start | bytes 296 | tf_op jit(solution)/shard_map/ppermute | solution.py:21
  3.5 17.5 %collective-permute-start.1 = (s32[3,8]{1,0:T(4,128)S(1)}, s32[3,8]{1,0:T(4,128)S(1)}, u32[]{:S(2)}, u32[]{:S(2)}) collective-permute-start(s32[3,8]{1,0:T(4,128)S(1)} %pad_add_fusion.2.i0), channel_id=1, source_target_pairs={{0,2},{1,3},{2,0},{3,1},{4,6},{5,7},{6,4},{7,5},{8,10},{9,11},{10,... | collective-permute-start | bytes 296 | tf_op jit(solution)/shard_map/ppermute | solution.py:21
  5.9 15.1 %collective-permute-start.2 = (s32[3,8]{1,0:T(4,128)S(1)}, s32[3,8]{1,0:T(4,128)S(1)}, u32[]{:S(2)}, u32[]{:S(2)}) collective-permute-start(s32[3,8]{1,0:T(4,128)S(1)} %pad_add_fusion.2.i0), channel_id=1, source_target_pairs={{0,3},{1,0},{2,1},{3,2},{4,7},{5,4},{6,5},{7,6},{8,11},{9,8},{10,9... | collective-permute-start | bytes 296 | tf_op jit(solution)/shard_map/ppermute | solution.py:21
  9.7 26.4 %all-to-all-start = ((bf16[32,64,128]{2,1,0:T(8,128)(2,1)}), bf16[32,64,128]{2,1,0:T(8,128)(2,1)S(1)}, u32[]{:S(2)}, u32[]{:S(2)}) async-start(bf16[32,64,128]{2,1,0:T(8,128)(2,1)} %broadcast_in_dim.9), calls=%async_computation | async-start | bytes 1048576 | tf_op jit(solution)/shard_map/gather_rows/all_to_all | solution.py:198
  20.9 37.5 %copy-start.13 = (s32[3,8]{1,0:T(4,128)}, s32[3,8]{1,0:T(4,128)S(1)}, u32[]{:S(2)}) copy-start(s32[3,8]{1,0:T(4,128)S(1)} %collective-permute-done.i1) | copy-start | bytes 292
  21.0 37.4 %copy-start.14 = (s32[3,8]{1,0:T(4,128)}, s32[3,8]{1,0:T(4,128)S(1)}, u32[]{:S(2)}) copy-start(s32[3,8]{1,0:T(4,128)S(1)} %collective-permute-done.1.i2) | copy-start | bytes 292
  21.0 37.4 %copy-start.15 = (s32[3,8]{1,0:T(4,128)}, s32[3,8]{1,0:T(4,128)S(1)}, u32[]{:S(2)}) copy-start(s32[3,8]{1,0:T(4,128)S(1)} %collective-permute-done.2.i3) | copy-start | bytes 292
  36.1 5.2 %copy-start.4 = (bf16[32,64,128]{2,1,0:T(8,128)(2,1)}, bf16[32,64,128]{2,1,0:T(8,128)(2,1)S(1)}, u32[]{:S(2)}) copy-start(bf16[32,64,128]{2,1,0:T(8,128)(2,1)S(1)} %all-to-all-done.own_ref) | copy-start | bytes 1572868
  36.1 5.2 %collective-permute-start.3 = (bf16[32,64,128]{2,1,0:T(8,128)(2,1)S(1)}, bf16[32,64,128]{2,1,0:T(8,128)(2,1)S(1)}, u32[]{:S(2)}, u32[]{:S(2)}) collective-permute-start(bf16[32,64,128]{2,1,0:T(8,128)(2,1)S(1)} %all-to-all-done.own_ref), channel_id=1, source_target_pairs={{0,4},{4,0},{1,5},{5,1},{2,6},{6,2},{3,7},{7,3},{8,12},{12,8},{9,1... | collective-permute-start | bytes 1572872 | tf_op jit(solution)/shard_map/gather_rows/ppermute | solution.py:199
  41.3 0.8 copy-start.5
  45.2 15.2 %collective-permute-start.4 = (bf16[2,2,2,2,16,128]{5,4,3,2,1,0:T(8,128)(2,1)S(1)}, bf16[2,2,2,2,16,128]{5,4,3,2,1,0:T(8,128)(2,1)S(1)}, u32[]{:S(2)}, u32[]{:S(2)}) collective-permute-start(bf16[2,2,2,2,16,128]{5,4,3,2,1,0:T(8,128)(2,1)S(1)} %get-tuple-element.11), channel_id=1, source_target_pairs={{0,1},{1,2},{2,3},{3,0},{4,5},{5,6},{6,7},{7,4},{8,9},{9,10},{10,1... | collective-permute-start | bytes 196616 | tf_op jit(solution)/shard_map/pick_blocks/ppermute | solution.py:21
  45.6 14.8 %collective-permute-start.5 = (bf16[2,2,2,2,16,128]{5,4,3,2,1,0:T(8,128)(2,1)S(1)}, bf16[2,2,2,2,16,128]{5,4,3,2,1,0:T(8,128)(2,1)S(1)}, u32[]{:S(2)}, u32[]{:S(2)}) collective-permute-start(bf16[2,2,2,2,16,128]{5,4,3,2,1,0:T(8,128)(2,1)S(1)} %get-tuple-element.10), channel_id=1, source_target_pairs={{0,2},{1,3},{2,0},{3,1},{4,6},{5,7},{6,4},{7,5},{8,10},{9,11},{10,... | collective-permute-start | bytes 196616 | tf_op jit(solution)/shard_map/pick_blocks/ppermute | solution.py:21
  46.5 13.9 %collective-permute-start.6 = (bf16[2,2,2,2,16,128]{5,4,3,2,1,0:T(8,128)(2,1)S(1)}, bf16[2,2,2,2,16,128]{5,4,3,2,1,0:T(8,128)(2,1)S(1)}, u32[]{:S(2)}, u32[]{:S(2)}) collective-permute-start(bf16[2,2,2,2,16,128]{5,4,3,2,1,0:T(8,128)(2,1)S(1)} %get-tuple-element.9), channel_id=1, source_target_pairs={{0,3},{1,0},{2,1},{3,2},{4,7},{5,4},{6,5},{7,6},{8,11},{9,8},{10,9... | collective-permute-start | bytes 196616 | tf_op jit(solution)/shard_map/pick_blocks/ppermute | solution.py:21
  48.1 2.2 %copy-start = (bf16[8,64,4096]{2,1,0:T(8,128)(2,1)S(1)}, bf16[8,64,4096]{2,1,0:T(8,128)(2,1)}, u32[]{:S(2)}) copy-start(bf16[8,64,4096]{2,1,0:T(8,128)(2,1)} %t_ref.3) | copy-start | bytes 12582916
  58.4 2.0 %copy-start.2 = (bf16[8,64,4096]{2,1,0:T(8,128)(2,1)}, bf16[8,64,4096]{2,1,0:T(8,128)(2,1)S(1)}, u32[]{:S(2)}) copy-start(bf16[8,64,4096]{2,1,0:T(8,128)(2,1)S(1)} %swap.1.ts_ref) | copy-start | bytes 12582916
  60.4 2.2 %copy-start.1 = (bf16[8,64,4096]{2,1,0:T(8,128)(2,1)S(1)}, bf16[8,64,4096]{2,1,0:T(8,128)(2,1)}, u32[]{:S(2)}) copy-start(bf16[8,64,4096]{2,1,0:T(8,128)(2,1)} %t_ref.3) | copy-start | bytes 12582916
  62.6 2.2 %copy-start.3 = (bf16[8,64,4096]{2,1,0:T(8,128)(2,1)S(1)}, bf16[8,64,4096]{2,1,0:T(8,128)(2,1)}, u32[]{:S(2)}) copy-start(bf16[8,64,4096]{2,1,0:T(8,128)(2,1)} %copy-done.2) | copy-start | bytes 12582916
  94.1 4.3 %collective-permute-start.7 = (f32[8,8,128]{2,1,0:T(8,128)S(1)}, f32[8,8,128]{2,1,0:T(8,128)S(1)}, u32[]{:S(2)}, u32[]{:S(2)}) collective-permute-start(f32[8,8,128]{2,1,0:T(8,128)S(1)} %get-tuple-element.15), channel_id=1, source_target_pairs={{0,1},{1,2},{2,3},{3,0},{4,5},{5,6},{6,7},{7,4},{8,9},{9,10},{10,1... | collective-permute-start | bytes 98312 | tf_op jit(solution)/shard_map/owners/ppermute | solution.py:21
  94.5 4.4 %collective-permute-start.8 = (f32[8,8,128]{2,1,0:T(8,128)S(1)}, f32[8,8,128]{2,1,0:T(8,128)S(1)}, u32[]{:S(2)}, u32[]{:S(2)}) collective-permute-start(f32[8,8,128]{2,1,0:T(8,128)S(1)} %get-tuple-element.14), channel_id=1, source_target_pairs={{0,2},{1,3},{2,0},{3,1},{4,6},{5,7},{6,4},{7,5},{8,10},{9,11},{10,... | collective-permute-start | bytes 98312 | tf_op jit(solution)/shard_map/owners/ppermute | solution.py:21
  96.3 3.1 %collective-permute-start.9 = (f32[8,8,128]{2,1,0:T(8,128)S(1)}, f32[8,8,128]{2,1,0:T(8,128)S(1)}, u32[]{:S(2)}, u32[]{:S(2)}) collective-permute-start(f32[8,8,128]{2,1,0:T(8,128)S(1)} %get-tuple-element.13), channel_id=1, source_target_pairs={{0,3},{1,0},{2,1},{3,2},{4,7},{5,4},{6,5},{7,6},{8,11},{9,8},{10,9... | collective-permute-start | bytes 98312 | tf_op jit(solution)/shard_map/owners/ppermute | solution.py:21
  98.4 1.0 copy-start.6
  98.9 0.6 copy-start.7
  99.4 0.6 copy-start.8
  124.1 4.5 %collective-permute-start.10 = (f32[16,128]{1,0:T(8,128)}, f32[16,128]{1,0:T(8,128)S(1)}, u32[]{:S(2)}, u32[]{:S(2)}) collective-permute-start(f32[16,128]{1,0:T(8,128)} %sum.1.p0), channel_id=1, source_target_pairs={{0,1},{1,2},{2,3},{3,0},{4,5},{5,6},{6,7},{7,4},{8,9},{9,10},{10,1... | collective-permute-start | bytes 24584 | tf_op jit(solution)/shard_map/owners/ppermute | solution.py:21
  125.1 4.7 %collective-permute-start.11 = (f32[16,128]{1,0:T(8,128)}, f32[16,128]{1,0:T(8,128)S(1)}, u32[]{:S(2)}, u32[]{:S(2)}) collective-permute-start(f32[16,128]{1,0:T(8,128)} %sum.1.p0), channel_id=1, source_target_pairs={{0,2},{1,3},{2,0},{3,1},{4,6},{5,7},{6,4},{7,5},{8,10},{9,11},{10,... | collective-permute-start | bytes 24584 | tf_op jit(solution)/shard_map/owners/ppermute | solution.py:21
  128.5 2.7 %collective-permute-start.12 = (f32[16,128]{1,0:T(8,128)}, f32[16,128]{1,0:T(8,128)S(1)}, u32[]{:S(2)}, u32[]{:S(2)}) collective-permute-start(f32[16,128]{1,0:T(8,128)} %sum.1.p0), channel_id=1, source_target_pairs={{0,3},{1,0},{2,1},{3,2},{4,7},{5,4},{6,5},{7,6},{8,11},{9,8},{10,9... | collective-permute-start | bytes 24584 | tf_op jit(solution)/shard_map/owners/ppermute | solution.py:21
  128.6 2.6 %copy-start.10 = (f32[16,128]{1,0:T(8,128)}, f32[16,128]{1,0:T(8,128)S(1)}, u32[]{:S(2)}) copy-start(f32[16,128]{1,0:T(8,128)S(1)} %collective-permute-done.10.p1) | copy-start | bytes 24580
  129.8 1.4 %copy-start.11 = (f32[16,128]{1,0:T(8,128)}, f32[16,128]{1,0:T(8,128)S(1)}, u32[]{:S(2)}) copy-start(f32[16,128]{1,0:T(8,128)S(1)} %collective-permute-done.11.p2) | copy-start | bytes 24580
  131.2 0.6 copy-start.12
where the time goes:
time: 136 us; the launch traced here: 135 us
  Pallas kernels  43.8 us (32%)
  starting transfers between devices  32.2 us (24%)
  blocking collectives  20.7 us (15%)
  waiting for transfers between devices  17.8 us (13%)
  local copies, waits for them, and re-layouts  16.7 us (12%)
  other arithmetic  3.44 us (3%)
    pallas_call x1, Pallas kernels, tile_pairs(): pl.pallas_call(tile_kernel, grid=(count,), out_shape=jax.ShapeDtypeStruct...  28.7 us
    all_to_all x1, blocking collectives, shards(): spread = lax.all_to_all(place(infos, terms), TENS, 0, 0)  20.7 us
    ppermute x12, starting transfers between devices, shift(): return lax.ppermute(values, 'x', [(i, (i + k) % NX) for i in range(NX)])  17.3 us
    all_to_all x1, waiting for transfers between devices, shards(): lax.all_to_all(jnp.broadcast_to(own[None], (32, 4 * NA, 2 * BS)), ZHL, 0, 0)  13.7 us
    all_to_all x1, starting transfers between devices, shards(): lax.all_to_all(jnp.broadcast_to(own[None], (32, 4 * NA, 2 * BS)), ZHL, 0, 0)  11.2 us
    unnamed x32, local copies, waits for them, and re-layouts  10.6 us
    pallas_call x1, Pallas kernels, swap(): pl.pallas_call(swap_kernel, grid=(count // 2,), out_shape=jax.ShapeDtypeS...  8.06 us
    ppermute x12, waiting for transfers between devices, shift(): return lax.ppermute(values, 'x', [(i, (i + k) % NX) for i in range(NX)])  3.74 us
  transfers between devices with their start and end apart: 14, of which 7 were waited for; matrix products, arithmetic and copies ran while one was open for 4% of the time, Pallas kernels for 6%

commit v1 on v0

v1 whole, which is shorter than its diff:
```python
import jax
import jax.numpy as jnp
from jax import lax
from jax.experimental import pallas as pl
from jax.experimental.pallas import tpu as pltpu
from jax.sharding import Mesh, PartitionSpec as P

BS = 64
NA = 16
AUX = 2
ZHL = ("z", "h", "l")
TENS = ("z", "h", "l", "c")
ALL = ("z", "h", "l", "c", "x")
NX = 4
F32, BF16 = jnp.float32, jnp.bfloat16
VMEM = pl.BlockSpec(memory_space=pltpu.VMEM)
SMEM = pl.BlockSpec(memory_space=pltpu.SMEM)
LARGE, SMALL = 58 * 1024 * 1024, 12 * 1024 * 1024


def shift(values, k):
    return lax.ppermute(values, "x", [(i, (i + k) % NX) for i in range(NX)])


def nt(a, b):
    return lax.dot_general(a, b, (((1,), (1,)), ((), ())), preferred_element_type=F32)


def eye(n):
    rows = lax.broadcasted_iota(jnp.int32, (n, n), 0)
    return jnp.where(rows == lax.broadcasted_iota(jnp.int32, (n, n), 1), 1.0, 0.0).astype(BF16)


def low_lanes(rows):
    return lax.broadcasted_iota(jnp.int32, (rows, 128), 1) < BS


def rows_kernel(occ_ref, virt_ref, o_ref, scr):
    for arr, ref in enumerate((occ_ref, virt_ref)):
        values = ref[...].astype(F32)
        for i in range(4):
            for pair in range(8):
                at = (arr * 4 + i) * 8 + pair
                scr[at:at + 1, :] = values[i:i + 1, pair * 128:pair * 128 + 128]
    block = scr[...].astype(BF16)
    for peer in range(o_ref.shape[0]):
        o_ref[peer] = block


def prep_kernel(i0, i1, i2, i3, t_ref, sw_ref, tr_ref, hot_ref, scr):
    @pl.when(pl.program_id(0) == 0)
    def _():
        at = lax.broadcasted_iota(jnp.int32, (32, 256), 0)
        row = jnp.zeros((32, 256), jnp.int32)
        col = jnp.zeros((32, 256), jnp.int32)
        for k, info in enumerate((i0, i1, i2, i3)):
            for t in range(8):
                here = at == k * 8 + t
                row = jnp.where(here, info[0, t], row)
                col = jnp.where(here, info[1, t], col)
        lane = lax.broadcasted_iota(jnp.int32, (32, 256), 1)
        for arr, first in enumerate((row, col)):
            for q in range(2):
                second = first if q == 0 else (col if arr == 0 else row)
                for odd in range(2):
                    for i in range(2):
                        hit = (first == (lane >> 4)) & ((lane & 15) == i * 8 + (second >> 1)) & ((second & 1) == odd)
                        start = ((q * 2 + odd) * 2 + i) * 32
                        hot_ref[arr, start:start + 32, :] = jnp.where(hit, 1.0, 0.0).astype(BF16)

    wide, narrow = eye(256), eye(128)
    for s in range(16):
        cut = slice(s * 256, s * 256 + 256)
        turned = jnp.concatenate([t_ref[0, :, cut], t_ref[1, :, cut]], axis=0).T
        scr[cut, :] = turned.astype(F32)
        tr_ref[0, cut, :] = turned.astype(BF16)
    for s in range(16):
        cut = slice(s * 256, s * 256 + 256)
        rows = jnp.concatenate([scr[pl.ds(4 * s + k, BS, stride=BS), :] for k in range(4)], axis=0)
        back = rows.astype(BF16).T
        sw_ref[0, :, cut] = back[:BS]
        sw_ref[1, :, cut] = back[BS:]


def prep(infos, tiles):
    count = tiles.shape[0]
    spec = pl.BlockSpec((2, BS, BS * BS), lambda i: (i, 0, 0))
    return pl.pallas_call(
        prep_kernel,
        grid=(count // 2,),
        out_shape=(
            jax.ShapeDtypeStruct(tiles.shape, BF16),
            jax.ShapeDtypeStruct((count // 2, BS * BS, 128), BF16),
            jax.ShapeDtypeStruct((2, 256, 256), BF16),
        ),
        in_specs=[SMEM] * 4 + [spec],
        out_specs=(spec, pl.BlockSpec((1, BS * BS, 128), lambda i: (i, 0, 0)), pl.BlockSpec((2, 256, 256), lambda i: (0, 0, 0))),
        scratch_shapes=[pltpu.VMEM((BS * BS, 128), F32)],
        cost_estimate=pl.CostEstimate(flops=9_000_000_000, bytes_accessed=6 * tiles.size, transcendentals=0),
        compiler_params=pltpu.CompilerParams(vmem_limit_bytes=LARGE),
        name="prep",
    )(*infos, tiles)


def pick_kernel(core_ref, hot_ref, own_ref, other_ref, o0, o1, o2, o3):
    core = core_ref[0]
    low = low_lanes(BS)
    for side, ref in ((core, own_ref), (1 - core, other_ref)):
        for l in range(2):
            for ih in range(2):
                found = []
                for arr in range(2):
                    first = (arr * 2 + ih) * 16
                    table = jnp.concatenate([ref[2 * b + l, first:first + 16, :] for b in range(NA)], axis=0)
                    got = jnp.dot(hot_ref[arr], table, preferred_element_type=F32)
                    left = got[:BS] + pltpu.roll(got[BS:2 * BS], BS, 1)
                    right = pltpu.roll(got[2 * BS:3 * BS], BS, 1) + got[3 * BS:]
                    found.append(jnp.where(low, left, right))
                for il in range(2):
                    for k, o_ref in enumerate((o0, o1, o2, o3)):
                        start = il * 32 + k * 8
                        o_ref[l, side, ih * 2 + il] = jnp.concatenate([f[start:start + 8] for f in found], axis=0).astype(BF16)


def tile_kernel(me_ref, t_ref, sw_ref, tr_ref, g0, g1, g2, g3, o0, o1, o2, o3, gscr, us, ws, ys, zs, pk):
    step = pl.program_id(0)
    me = me_ref[0]

    @pl.when(step == 0)
    def _():
        for k, ref in enumerate((g0, g1, g2, g3)):
            start = pl.multiple_of(((me - k + NX) & 3) * 256, 256)
            gscr[pl.ds(start, 256), :] = ref[...].reshape(256, 128).astype(F32)

    m = lax.broadcasted_iota(jnp.int32, (BS, BS), 0)
    place = (((m >> 2) & 3) << 4) + ((m >> 5) << 3) + (((m >> 4) & 1) << 2) + (m & 3)
    order = jnp.where(place == lax.broadcasted_iota(jnp.int32, (BS, BS), 1), 1.0, 0.0).astype(BF16)
    low = low_lanes(BS)

    def blocks_t(arr, u):
        rows = gscr[pl.ds(arr * 8 + step * 2 + u, BS, stride=16), :].astype(BF16)
        rows = jnp.dot(order, rows, preferred_element_type=F32)
        turned = jnp.concatenate([rows, rows], axis=0).T
        return turned[:BS], turned[BS:]

    def two(b):
        return jnp.concatenate([jnp.where(low, b, 0.0), jnp.where(low, 0.0, b)], axis=0).astype(BF16)

    def four(b):
        pair = two(b)
        none = jnp.zeros((128, 128), BF16)
        return jnp.concatenate([jnp.concatenate([pair, none], axis=1), jnp.concatenate([none, pair], axis=1)], axis=0)

    (cc0, cr0), (cc1, cr1) = blocks_t(1, 0), blocks_t(1, 1)
    virt = jnp.concatenate([
        jnp.concatenate([two(cc0), two(cc1)], axis=1),
        jnp.concatenate([two(cr0), two(cr1)], axis=1),
    ], axis=0)
    low128 = low_lanes(128)
    zero = jnp.zeros((128, 128), BF16)
    for s in range(16):
        a = tr_ref[0, s * 256:s * 256 + 128, :]
        b = tr_ref[0, s * 256 + 128:s * 256 + 256, :]
        rhs = jnp.concatenate([
            jnp.concatenate([jnp.where(low128, a, zero), jnp.where(low128, b, zero)], axis=1),
            jnp.concatenate([jnp.where(low128, zero, a), jnp.where(low128, zero, b)], axis=1),
        ], axis=0)
        out = jnp.dot(virt, rhs, preferred_element_type=F32)
        for ref, first in ((us, 0), (ws, 128)):
            ref[s * 256:s * 256 + 128, :] = out[first:first + 128, :128]
            ref[s * 256 + 128:s * 256 + 256, :] = out[first:first + 128, 128:]
    for u in range(2):
        same, cross = blocks_t(0, u)
        for ref, dest, block in ((sw_ref, ys, same), (t_ref, zs, cross)):
            rows = jnp.concatenate([ref[u, :, s * 256:s * 256 + 256] for s in range(16)], axis=0)
            out = jnp.dot(rows, four(block), preferred_element_type=F32).astype(BF16)
            for s in range(16):
                dest[u * BS:u * BS + BS, s * 256:s * 256 + 256] = out[s * BS:s * BS + BS]
    acc = jnp.zeros((128, 128), F32)
    for left, right in ((ys, us), (zs, ws)):
        for s in range(16):
            rows = jnp.concatenate([right[pl.ds(4 * s + k, BS, stride=BS), :] for k in range(4)], axis=0)
            acc += jnp.dot(left[:, s * 256:s * 256 + 256], rows.astype(BF16), preferred_element_type=F32)
    acc = acc.T * (1.0 / BS)
    low32 = low_lanes(32)
    pk[0] = jnp.where(low32, acc[:32], pltpu.roll(acc[32:64], BS, 1))
    pk[1] = jnp.where(low32, pltpu.roll(acc[64:96], BS, 1), acc[96:])
    for k, o_ref in enumerate((o0, o1, o2, o3)):
        start = pl.multiple_of(((me + k) & 3) * 8, 8)
        for u in range(2):
            o_ref[u] = pk[u, pl.ds(start, 8), :]


def tile_pairs(me, tiles, swapped, turned, got):
    count = tiles.shape[0]
    tile = pl.BlockSpec((2, BS, BS * BS), lambda i: (i, 0, 0))
    return pl.pallas_call(
        tile_kernel,
        grid=(count // 2,),
        out_shape=[jax.ShapeDtypeStruct((count, 8, 128), F32)] * NX,
        in_specs=[SMEM, tile, tile, pl.BlockSpec((1, BS * BS, 128), lambda i: (i, 0, 0))] + [VMEM] * 4,
        out_specs=[pl.BlockSpec((2, 8, 128), lambda i: (i, 0, 0))] * NX,
        scratch_shapes=[
            pltpu.VMEM((1024, 128), F32), pltpu.VMEM((BS * BS, 128), F32), pltpu.VMEM((BS * BS, 128), F32),
            pltpu.VMEM((128, BS * BS), BF16), pltpu.VMEM((128, BS * BS), BF16), pltpu.VMEM((2, 32, 128), F32),
        ],
        compiler_params=pltpu.CompilerParams(vmem_limit_bytes=LARGE),
        name="tile_pairs",
    )(me, tiles, swapped, turned, *got)


def place_kernel(i0, i1, i2, i3, t0, t1, t2, t3, o_ref, total):
    total[...] = jnp.zeros_like(total)
    for info, terms in ((i0, t0), (i1, t1), (i2, t2), (i3, t3)):
        for t in range(terms.shape[0]):
            at = info[2, t]
            total[at] += terms[t]
    o_ref[...] = total[...].reshape(o_ref.shape).astype(BF16)


def place(infos, terms):
    return pl.pallas_call(
        place_kernel,
        out_shape=jax.ShapeDtypeStruct((64, 16, 128), BF16),
        in_specs=[SMEM] * 4 + [VMEM] * 4,
        out_specs=VMEM,
        scratch_shapes=[pltpu.VMEM((128, 8, 128), F32)],
        compiler_params=pltpu.CompilerParams(vmem_limit_bytes=SMALL),
        name="place",
    )(*infos, *terms)


def sum_kernel(s_ref, o_ref):
    o_ref[...] = jnp.sum(s_ref[...].astype(F32), axis=0)


def finish_kernel(me_ref, p0, p1, p2, p3, o_ref, whole):
    me = me_ref[0]
    for k, ref in enumerate((p0, p1, p2, p3)):
        x = (me - k + NX) & 3
        for aux in range(AUX):
            whole[aux, x] = ref[8 * aux:8 * aux + 8]
    for aux in range(AUX):
        rows = whole[aux].reshape(32, 128)
        o_ref[aux * BS:aux * BS + 32, :] = rows[:, :BS]
        o_ref[aux * BS + 32:(aux + 1) * BS, :] = pltpu.roll(rows, BS, 1)[:, :BS]


def shards(tiles, tile_dest, tile_aux, tile_row, tile_col, green_occ, green_virt):
    count = tiles.shape[0]
    x = lax.axis_index("x")
    me = x.reshape(1)
    info = jnp.stack([tile_row, tile_col, tile_dest * AUX + tile_aux])
    infos = [info] + [shift(info, k) for k in range(1, NX)]

    with jax.named_scope("gather_rows"):
        own = pl.pallas_call(
            rows_kernel,
            out_shape=jax.ShapeDtypeStruct((32, BS, 128), BF16),
            in_specs=[VMEM] * 2,
            out_specs=VMEM,
            scratch_shapes=[pltpu.VMEM((BS, 128), F32)],
            compiler_params=pltpu.CompilerParams(vmem_limit_bytes=SMALL),
            name="rows",
        )(green_occ, green_virt)
        rows = lax.all_to_all(own, ZHL, 0, 0)
        other = lax.ppermute(rows, "c", [(0, 1), (1, 0)])
    swapped, turned, hot = prep(infos, tiles)

    with jax.named_scope("pick_blocks"):
        picked = pl.pallas_call(
            pick_kernel,
            out_shape=[jax.ShapeDtypeStruct((2, 2, 4, 2 * count, 128), BF16)] * NX,
            in_specs=[SMEM] + [VMEM] * 3,
            out_specs=[VMEM] * NX,
            compiler_params=pltpu.CompilerParams(vmem_limit_bytes=SMALL),
            name="pick",
        )(lax.axis_index("c").reshape(1), hot, rows, other)
        got = [picked[0]] + [shift(picked[NX - k], k) for k in range(1, NX)]

    quarters = tile_pairs(me, tiles, swapped, turned, got)

    with jax.named_scope("owners"):
        terms = [quarters[0]] + [shift(quarters[k], k) for k in range(1, NX)]
        spread = lax.all_to_all(place(infos, terms), TENS, 0, 0)
        owned = pl.pallas_call(
            sum_kernel, out_shape=jax.ShapeDtypeStruct((16, 128), F32), in_specs=[VMEM], out_specs=VMEM,
            compiler_params=pltpu.CompilerParams(vmem_limit_bytes=SMALL), name="sum",
        )(spread)
        parts = [owned] + [shift(owned, k) for k in range(1, NX)]
        return pl.pallas_call(
            finish_kernel,
            out_shape=jax.ShapeDtypeStruct((AUX * BS, BS), F32),
            in_specs=[SMEM] + [VMEM] * 4,
            out_specs=pl.BlockSpec((AUX * BS, BS), lambda: (0, 0)),
            scratch_shapes=[pltpu.VMEM((AUX, NX, 8, 128), F32)],
            compiler_params=pltpu.CompilerParams(vmem_limit_bytes=SMALL),
            name="finish",
        )(me, *parts)


def solution(mesh):
    fine = Mesh(mesh.devices.reshape(8, 2, 2, 2, 4), ALL)
    return jax.shard_map(
        shards,
        mesh=fine,
        in_specs=(P(ALL, None, None), P(ALL), P(ALL), P(ALL), P(ALL), P(ALL, None), P(ALL, None)),
        out_specs=P(TENS, None),
        check_vma=False,
    )
```

time: 136 us -> 109 us (0.80)
  Pallas kernels: 43.8 us -> 31.3 us
  local copies, waits for them, and re-layouts: 16.7 us -> 6.22 us
  other arithmetic: 3.44 us -> 1.36 us
    pallas_call x3 -> x4, Pallas kernels: 38.9 us -> 30.3 us  [the longest x1 20 us: tile_pairs(): pl.pallas_call(tile_kernel, grid=(count // 2,), out_shape=[jax.ShapeDtype...]
    unnamed x32, local copies, waits for them, and re-layouts: 10.6 us -> 5.52 us
    all_to_all x1, waiting for transfers between devices: 13.7 us -> 10 us  [shards(): rows = lax.all_to_all(own, ZHL, 0, 0)]
    ppermute x12, waiting for transfers between devices: 3.74 us -> 6.6 us  [shift(): return lax.ppermute(values, 'x', [(i, (i + k) % NX) for i in range(NX)])]
    another operation x9 -> x0, local copies, waits for them, and re-layouts: 1.98 us -> none  [the longest x2 1.56 us: shards(): own = jnp.stack([green_occ, green_virt]).reshape(2, 2, 2, NA, BS)]
    squeeze x2 -> x0, local copies, waits for them, and re-layouts: 1.59 us -> none  [the longest x1 0.95 us: shards(): got[NX - k] = shift(picked[k], NX - k)]
    pallas_call x1, Pallas kernels: 1.63 us -> 0.08 us  [shards(): pl.pallas_call(sum_kernel, out_shape=jax.ShapeDtypeStruct((16, 128), F32)...]
    pallas_call x1, Pallas kernels: 1.46 us -> 0.08 us  [shards(): pl.pallas_call(finish_kernel, out_shape=jax.ShapeDtypeStruct((AUX * BS, B...]
  transfers between devices with their start and end apart: 14 -> 14, of which waited for: 7 -> 9; matrix products, arithmetic and copies ran while one was open for 4% -> 1% of each run, Pallas kernels for 6% -> 8%
where the time goes in v1:
time: 109 us
  starting transfers between devices  31.8 us (29%)
  Pallas kernels  31.3 us (29%)
  blocking collectives  21.1 us (19%)
  waiting for transfers between devices  16.6 us (15%)
  local copies, waits for them, and re-layouts  6.22 us (6%)
  other arithmetic  1.36 us (1%)
    all_to_all x1, blocking collectives, shards(): spread = lax.all_to_all(place(infos, terms), TENS, 0, 0)  21.1 us
    pallas_call x1, Pallas kernels, tile_pairs(): pl.pallas_call(tile_kernel, grid=(count // 2,), out_shape=[jax.ShapeDtype...  20 us
    ppermute x12, starting transfers between devices, shift(): return lax.ppermute(values, 'x', [(i, (i + k) % NX) for i in range(NX)])  17.4 us
    all_to_all x1, starting transfers between devices, shards(): rows = lax.all_to_all(own, ZHL, 0, 0)  12 us
    all_to_all x1, waiting for transfers between devices, shards(): rows = lax.all_to_all(own, ZHL, 0, 0)  10 us
    pallas_call x1, Pallas kernels, prep(): pl.pallas_call(prep_kernel, grid=(count // 2,), out_shape=(jax.ShapeDtype...  8.69 us
    ppermute x12, waiting for transfers between devices, shift(): return lax.ppermute(values, 'x', [(i, (i + k) % NX) for i in range(NX)])  6.6 us
    unnamed x32, local copies, waits for them, and re-layouts  5.52 us
  transfers between devices with their start and end apart: 14, of which 9 were waited for; matrix products, arithmetic and copies ran while one was open for 1% of the time, Pallas kernels for 8%

profile of v1, /device:TPU:1, one launch (start us, length us, event | category | flops | bytes accessed | tf_op | source)
XLA Modules:
  0.0 108.5 jit_solution(4338733114588710718)
XLA Ops:
  0.0 0.0 copy-start.3
  0.0 0.7 copy-done.3
  0.7 0.0 copy-start.4
  0.7 0.7 copy-done.4
  1.4 0.9 rows.1
  2.3 12.0 %all-to-all-start = ((bf16[32,64,128]{2,1,0:T(8,128)(2,1)}), bf16[32,64,128]{2,1,0:T(8,128)(2,1)S(1)}, u32[]{:S(2)}, u32[]{:S(2)}) async-start(bf16[32,64,128]{2,1,0:T(8,128)(2,1)} %rows.1), calls=%async_computation | async-start | bytes 1048576 | tf_op jit(solution)/shard_map/gather_rows/all_to_all | solution.py:266
  14.3 0.7 add_bitcast_fusion
  15.0 0.7 pad_add_fusion.i0
  15.7 0.0 copy-start.5
  15.7 1.3 %collective-permute-start = (s32[3,8]{1,0:T(4,128)S(1)}, s32[3,8]{1,0:T(4,128)S(1)}, u32[]{:S(2)}, u32[]{:S(2)}) collective-permute-start(s32[3,8]{1,0:T(4,128)S(1)} %pad_add_fusion.i0), channel_id=1, source_target_pairs={{0,1},{1,2},{2,3},{3,0},{4,5},{5,6},{6,7},{7,4},{8,9},{9,10},{10,1... | collective-permute-start | bytes 296 | tf_op jit(solution)/shard_map/ppermute | solution.py:22
  17.0 2.5 %collective-permute-start.1 = (s32[3,8]{1,0:T(4,128)S(1)}, s32[3,8]{1,0:T(4,128)S(1)}, u32[]{:S(2)}, u32[]{:S(2)}) collective-permute-start(s32[3,8]{1,0:T(4,128)S(1)} %pad_add_fusion.i0), channel_id=1, source_target_pairs={{0,2},{1,3},{2,0},{3,1},{4,6},{5,7},{6,4},{7,5},{8,10},{9,11},{10,... | collective-permute-start | bytes 296 | tf_op jit(solution)/shard_map/ppermute | solution.py:22
  19.4 1.2 %collective-permute-start.2 = (s32[3,8]{1,0:T(4,128)S(1)}, s32[3,8]{1,0:T(4,128)S(1)}, u32[]{:S(2)}, u32[]{:S(2)}) collective-permute-start(s32[3,8]{1,0:T(4,128)S(1)} %pad_add_fusion.i0), channel_id=1, source_target_pairs={{0,3},{1,0},{2,1},{3,2},{4,7},{5,4},{6,5},{7,6},{8,11},{9,8},{10,9... | collective-permute-start | bytes 296 | tf_op jit(solution)/shard_map/ppermute | solution.py:22
  20.6 10.0 %all-to-all-done.own_ref = bf16[32,64,128]{2,1,0:T(8,128)(2,1)S(1)} async-done(((bf16[32,64,128]{2,1,0:T(8,128)(2,1)}), bf16[32,64,128]{2,1,0:T(8,128)(2,1)S(1)}, u32[]{:S(2)}, u32[]{:S(2)}) %all-to-all-start) | async-done | bytes 524320 | tf_op jit(solution)/shard_map/gather_rows/all_to_all | solution.py:266
  30.6 2.4 %collective-permute-start.3 = (bf16[32,64,128]{2,1,0:T(8,128)(2,1)S(1)}, bf16[32,64,128]{2,1,0:T(8,128)(2,1)S(1)}, u32[]{:S(2)}, u32[]{:S(2)}) collective-permute-start(bf16[32,64,128]{2,1,0:T(8,128)(2,1)S(1)} %all-to-all-done.own_ref), channel_id=1, source_target_pairs={{0,4},{4,0},{1,5},{5,1},{2,6},{6,2},{3,7},{7,3},{8,12},{12,8},{9,1... | collective-permute-start | bytes 1572872 | tf_op jit(solution)/shard_map/gather_rows/ppermute | solution.py:267
  33.0 0.0 collective-permute-done.i1
  33.0 0.0 copy-start.7
  33.0 0.0 collective-permute-done.1.i2
  33.0 0.0 copy-start.9
  33.0 0.0 collective-permute-done.2.i3
  33.0 0.0 copy-done.5
  33.0 0.5 copy-done.7
  33.5 0.1 copy-done.9
  33.6 0.0 copy-start.11
  33.6 0.6 copy-done.11
  34.2 8.7 %prep.1 = (bf16[8,64,4096]{2,1,0:T(8,128)(2,1)}, bf16[4,4096,128]{2,1,0:T(8,128)(2,1)}, bf16[2,256,256]{2,1,0:T(8,128)(2,1)}) custom-call(s32[3,8]{1,0:T(4,128)} %copy-done.5, s32[3,8]{1,0:T(4,128)} %copy-done.7, s32[3,8]{1,0:T(4,128)} %copy-done.9, s32[3,8]{1,0:T(4,128)} %copy-done.11, bf16[8,64,4096]{2,1,0:T(8,128)(2,1)} %t_ref.3), custom_call_target="tpu_custom_call" | custom-call | flops 8999999488 | bytes 12582912 | tf_op jit(solution)/shard_map/prep/pallas_call | solution.py:88
  42.9 0.0 collective-permute-done.3.other_ref
  42.9 0.0 copy-start
  42.9 0.9 copy-done
  43.8 0.7 pick.1
  44.6 0.0 copy-start.1
  44.6 0.6 copy-done.1
  45.2 1.2 %collective-permute-start.4 = (bf16[2,2,4,16,128]{4,3,2,1,0:T(8,128)(2,1)S(1)}, bf16[2,2,4,16,128]{4,3,2,1,0:T(8,128)(2,1)S(1)}, u32[]{:S(2)}, u32[]{:S(2)}) collective-permute-start(bf16[2,2,4,16,128]{4,3,2,1,0:T(8,128)(2,1)S(1)} %get-tuple-element.20), channel_id=1, source_target_pairs={{0,1},{1,2},{2,3},{3,0},{4,5},{5,6},{6,7},{7,4},{8,9},{9,10},{10,1... | collective-permute-start | bytes 196616 | tf_op jit(solution)/shard_map/pick_blocks/ppermute | solution.py:22
  46.4 2.4 %collective-permute-start.5 = (bf16[2,2,4,16,128]{4,3,2,1,0:T(8,128)(2,1)S(1)}, bf16[2,2,4,16,128]{4,3,2,1,0:T(8,128)(2,1)S(1)}, u32[]{:S(2)}, u32[]{:S(2)}) collective-permute-start(bf16[2,2,4,16,128]{4,3,2,1,0:T(8,128)(2,1)S(1)} %get-tuple-element.21), channel_id=1, source_target_pairs={{0,2},{1,3},{2,0},{3,1},{4,6},{5,7},{6,4},{7,5},{8,10},{9,11},{10,... | collective-permute-start | bytes 196616 | tf_op jit(solution)/shard_map/pick_blocks/ppermute | solution.py:22
  48.8 1.2 %collective-permute-start.6 = (bf16[2,2,4,16,128]{4,3,2,1,0:T(8,128)(2,1)S(1)}, bf16[2,2,4,16,128]{4,3,2,1,0:T(8,128)(2,1)S(1)}, u32[]{:S(2)}, u32[]{:S(2)}) collective-permute-start(bf16[2,2,4,16,128]{4,3,2,1,0:T(8,128)(2,1)S(1)} %get-tuple-element.22), channel_id=1, source_target_pairs={{0,3},{1,0},{2,1},{3,2},{4,7},{5,4},{6,5},{7,6},{8,11},{9,8},{10,9... | collective-permute-start | bytes 196616 | tf_op jit(solution)/shard_map/pick_blocks/ppermute | solution.py:22
  50.0 0.1 collective-permute-done.4.g1
  50.1 2.4 %collective-permute-done.5.g2 = bf16[2,2,4,16,128]{4,3,2,1,0:T(8,128)(2,1)S(1)} collective-permute-done((bf16[2,2,4,16,128]{4,3,2,1,0:T(8,128)(2,1)S(1)}, bf16[2,2,4,16,128]{4,3,2,1,0:T(8,128)(2,1)S(1)}, u32[]{:S(2)}, u32[]{:S(2)}) %collective-permute-start.5) | collective-permute-done | bytes 65568 | tf_op jit(solution)/shard_map/pick_blocks/ppermute | solution.py:22
  52.5 0.0 collective-permute-done.6.g3
  52.5 0.0 copy-done.13
  52.5 0.6 copy-done.14
  53.1 0.0 copy-done.15
  53.2 20.0 %tile_pairs.1 = (f32[8,8,128]{2,1,0:T(8,128)}, f32[8,8,128]{2,1,0:T(8,128)}, f32[8,8,128]{2,1,0:T(8,128)}, f32[8,8,128]{2,1,0:T(8,128)}) custom-call(s32[1]{0:T(128)} %bitcast.me_ref, bf16[8,64,4096]{2,1,0:T(8,128)(2,1)} %t_ref.3, bf16[8,64,4096]{2,1,0:T(8,128)(2,1)} %get-tuple-element.16.sw_ref, bf16[4,4096,128]{2,1,0:T(8,128)(2,1)} %get-tuple-element.17.tr_ref, ...), custom_call_target="tpu_custom_call" | custom-call | tf_op jit(solution)/shard_map/tile_pairs/pallas_call | solution.py:197
  73.1 0.3 collective-permute-start.7
  73.4 3.0 %collective-permute-start.8 = (f32[8,8,128]{2,1,0:T(8,128)}, f32[8,8,128]{2,1,0:T(8,128)S(1)}, u32[]{:S(2)}, u32[]{:S(2)}) collective-permute-start(f32[8,8,128]{2,1,0:T(8,128)} %get-tuple-element.25), channel_id=1, source_target_pairs={{0,2},{1,3},{2,0},{3,1},{4,6},{5,7},{6,4},{7,5},{8,10},{9,11},{10,... | collective-permute-start | bytes 98312 | tf_op jit(solution)/shard_map/owners/ppermute | solution.py:22
  76.4 1.1 collective-permute-start.9
  77.5 0.1 collective-permute-done.7.t1
  77.6 0.7 collective-permute-done.8.t2
  78.2 1.3 %collective-permute-done.9.t3 = f32[8,8,128]{2,1,0:T(8,128)S(1)} collective-permute-done((f32[8,8,128]{2,1,0:T(8,128)}, f32[8,8,128]{2,1,0:T(8,128)S(1)}, u32[]{:S(2)}, u32[]{:S(2)}) %collective-permute-start.9) | collective-permute-done | bytes 32800 | tf_op jit(solution)/shard_map/owners/ppermute | solution.py:22
  79.5 0.0 copy-done.6
  79.5 0.0 copy-done.8
  79.5 0.0 copy-done.10
  79.5 0.0 copy-done.12
  79.5 0.0 copy-start.2
  79.5 0.7 copy-done.2
  80.3 0.8 place.1
  81.1 21.1 %all_to_all.10.s_ref = bf16[64,16,128]{2,1,0:T(8,128)(2,1)S(1)} all-to-all(bf16[64,16,128]{2,1,0:T(8,128)(2,1)S(1)} %place.1), channel_id=1, replica_groups=mesh['z'=8,'h'=2,'l'=2,'c'=2,'x'=4] {'z','h','l','c'}, dimensions={0} | all-to-all | bytes 524288 | tf_op jit(solution)/shard_map/owners/all_to_all | solution.py:285
  102.2 0.1 sum.1.p0
  102.3 0.1 collective-permute-start.10
  102.4 2.9 %collective-permute-start.11 = (f32[16,128]{1,0:T(8,128)S(1)}, f32[16,128]{1,0:T(8,128)S(1)}, u32[]{:S(2)}, u32[]{:S(2)}) collective-permute-start(f32[16,128]{1,0:T(8,128)S(1)} %sum.1.p0), channel_id=1, source_target_pairs={{0,2},{1,3},{2,0},{3,1},{4,6},{5,7},{6,4},{7,5},{8,10},{9,11},{10,... | collective-permute-start | bytes 24584 | tf_op jit(solution)/shard_map/owners/ppermute | solution.py:22
  105.2 0.4 collective-permute-start.12
  105.7 0.4 collective-permute-done.10.p1
  106.1 0.4 collective-permute-done.11.p2
  106.5 1.3 %collective-permute-done.12.p3 = f32[16,128]{1,0:T(8,128)S(1)} collective-permute-done((f32[16,128]{1,0:T(8,128)S(1)}, f32[16,128]{1,0:T(8,128)S(1)}, u32[]{:S(2)}, u32[]{:S(2)}) %collective-permute-start.12) | collective-permute-done | bytes 8224 | tf_op jit(solution)/shard_map/owners/ppermute | solution.py:22
  107.7 0.1 finish.1
  107.8 0.7 copy.8
  (7 shorter events, 0.0 us)
Async XLA Ops:
  0.0 0.7 copy-start.3
  0.7 0.7 copy-start.4
  2.3 28.3 %all-to-all-start = ((bf16[32,64,128]{2,1,0:T(8,128)(2,1)}), bf16[32,64,128]{2,1,0:T(8,128)(2,1)S(1)}, u32[]{:S(2)}, u32[]{:S(2)}) async-start(bf16[32,64,128]{2,1,0:T(8,128)(2,1)} %rows.1), calls=%async_computation | async-start | bytes 1048576 | tf_op jit(solution)/shard_map/gather_rows/all_to_all | solution.py:266
  15.7 17.3 %copy-start.5 = (s32[3,8]{1,0:T(4,128)}, s32[3,8]{1,0:T(4,128)S(1)}, u32[]{:S(2)}) copy-start(s32[3,8]{1,0:T(4,128)S(1)} %pad_add_fusion.i0) | copy-start | bytes 292
  15.7 17.3 %collective-permute-start = (s32[3,8]{1,0:T(4,128)S(1)}, s32[3,8]{1,0:T(4,128)S(1)}, u32[]{:S(2)}, u32[]{:S(2)}) collective-permute-start(s32[3,8]{1,0:T(4,128)S(1)} %pad_add_fusion.i0), channel_id=1, source_target_pairs={{0,1},{1,2},{2,3},{3,0},{4,5},{5,6},{6,7},{7,4},{8,9},{9,10},{10,1... | collective-permute-start | bytes 296 | tf_op jit(solution)/shard_map/ppermute | solution.py:22
  17.0 16.0 %collective-permute-start.1 = (s32[3,8]{1,0:T(4,128)S(1)}, s32[3,8]{1,0:T(4,128)S(1)}, u32[]{:S(2)}, u32[]{:S(2)}) collective-permute-start(s32[3,8]{1,0:T(4,128)S(1)} %pad_add_fusion.i0), channel_id=1, source_target_pairs={{0,2},{1,3},{2,0},{3,1},{4,6},{5,7},{6,4},{7,5},{8,10},{9,11},{10,... | collective-permute-start | bytes 296 | tf_op jit(solution)/shard_map/ppermute | solution.py:22
  19.4 13.6 %collective-permute-start.2 = (s32[3,8]{1,0:T(4,128)S(1)}, s32[3,8]{1,0:T(4,128)S(1)}, u32[]{:S(2)}, u32[]{:S(2)}) collective-permute-start(s32[3,8]{1,0:T(4,128)S(1)} %pad_add_fusion.i0), channel_id=1, source_target_pairs={{0,3},{1,0},{2,1},{3,2},{4,7},{5,4},{6,5},{7,6},{8,11},{9,8},{10,9... | collective-permute-start | bytes 296 | tf_op jit(solution)/shard_map/ppermute | solution.py:22
  30.6 12.3 %collective-permute-start.3 = (bf16[32,64,128]{2,1,0:T(8,128)(2,1)S(1)}, bf16[32,64,128]{2,1,0:T(8,128)(2,1)S(1)}, u32[]{:S(2)}, u32[]{:S(2)}) collective-permute-start(bf16[32,64,128]{2,1,0:T(8,128)(2,1)S(1)} %all-to-all-done.own_ref), channel_id=1, source_target_pairs={{0,4},{4,0},{1,5},{5,1},{2,6},{6,2},{3,7},{7,3},{8,12},{12,8},{9,1... | collective-permute-start | bytes 1572872 | tf_op jit(solution)/shard_map/gather_rows/ppermute | solution.py:267
  33.0 0.5 copy-start.7
  33.0 0.6 copy-start.9
  33.6 0.6 copy-start.11
  42.9 1.0 copy-start
  44.6 0.6 copy-start.1
  45.2 4.9 %collective-permute-start.4 = (bf16[2,2,4,16,128]{4,3,2,1,0:T(8,128)(2,1)S(1)}, bf16[2,2,4,16,128]{4,3,2,1,0:T(8,128)(2,1)S(1)}, u32[]{:S(2)}, u32[]{:S(2)}) collective-permute-start(bf16[2,2,4,16,128]{4,3,2,1,0:T(8,128)(2,1)S(1)} %get-tuple-element.20), channel_id=1, source_target_pairs={{0,1},{1,2},{2,3},{3,0},{4,5},{5,6},{6,7},{7,4},{8,9},{9,10},{10,1... | collective-permute-start | bytes 196616 | tf_op jit(solution)/shard_map/pick_blocks/ppermute | solution.py:22
  46.4 6.1 %collective-permute-start.5 = (bf16[2,2,4,16,128]{4,3,2,1,0:T(8,128)(2,1)S(1)}, bf16[2,2,4,16,128]{4,3,2,1,0:T(8,128)(2,1)S(1)}, u32[]{:S(2)}, u32[]{:S(2)}) collective-permute-start(bf16[2,2,4,16,128]{4,3,2,1,0:T(8,128)(2,1)S(1)} %get-tuple-element.21), channel_id=1, source_target_pairs={{0,2},{1,3},{2,0},{3,1},{4,6},{5,7},{6,4},{7,5},{8,10},{9,11},{10,... | collective-permute-start | bytes 196616 | tf_op jit(solution)/shard_map/pick_blocks/ppermute | solution.py:22
  48.8 3.7 %collective-permute-start.6 = (bf16[2,2,4,16,128]{4,3,2,1,0:T(8,128)(2,1)S(1)}, bf16[2,2,4,16,128]{4,3,2,1,0:T(8,128)(2,1)S(1)}, u32[]{:S(2)}, u32[]{:S(2)}) collective-permute-start(bf16[2,2,4,16,128]{4,3,2,1,0:T(8,128)(2,1)S(1)} %get-tuple-element.22), channel_id=1, source_target_pairs={{0,3},{1,0},{2,1},{3,2},{4,7},{5,4},{6,5},{7,6},{8,11},{9,8},{10,9... | collective-permute-start | bytes 196616 | tf_op jit(solution)/shard_map/pick_blocks/ppermute | solution.py:22
  50.1 2.4 %copy-start.13 = (bf16[2,2,4,16,128]{4,3,2,1,0:T(8,128)(2,1)}, bf16[2,2,4,16,128]{4,3,2,1,0:T(8,128)(2,1)S(1)}, u32[]{:S(2)}) copy-start(bf16[2,2,4,16,128]{4,3,2,1,0:T(8,128)(2,1)S(1)} %collective-permute-done.4.g1) | copy-start | bytes 196612
  52.5 0.6 copy-start.14
  52.5 0.6 copy-start.15
  53.1 26.4 %copy-start.6 = (s32[3,8]{1,0:T(4,128)S(1)}, s32[3,8]{1,0:T(4,128)}, u32[]{:S(2)}) copy-start(s32[3,8]{1,0:T(4,128)} %copy-done.5) | copy-start | bytes 292
  53.1 26.4 %copy-start.8 = (s32[3,8]{1,0:T(4,128)S(1)}, s32[3,8]{1,0:T(4,128)}, u32[]{:S(2)}) copy-start(s32[3,8]{1,0:T(4,128)} %copy-done.7) | copy-start | bytes 292
  53.2 26.4 %copy-start.10 = (s32[3,8]{1,0:T(4,128)S(1)}, s32[3,8]{1,0:T(4,128)}, u32[]{:S(2)}) copy-start(s32[3,8]{1,0:T(4,128)} %copy-done.9) | copy-start | bytes 292
  53.2 26.4 %copy-start.12 = (s32[3,8]{1,0:T(4,128)S(1)}, s32[3,8]{1,0:T(4,128)}, u32[]{:S(2)}) copy-start(s32[3,8]{1,0:T(4,128)} %copy-done.11) | copy-start | bytes 292
  73.1 4.4 %collective-permute-start.7 = (f32[8,8,128]{2,1,0:T(8,128)}, f32[8,8,128]{2,1,0:T(8,128)S(1)}, u32[]{:S(2)}, u32[]{:S(2)}) collective-permute-start(f32[8,8,128]{2,1,0:T(8,128)} %get-tuple-element.24), channel_id=1, source_target_pairs={{0,1},{1,2},{2,3},{3,0},{4,5},{5,6},{6,7},{7,4},{8,9},{9,10},{10,1... | collective-permute-start | bytes 98312 | tf_op jit(solution)/shard_map/owners/ppermute | solution.py:22
  73.4 4.8 %collective-permute-start.8 = (f32[8,8,128]{2,1,0:T(8,128)}, f32[8,8,128]{2,1,0:T(8,128)S(1)}, u32[]{:S(2)}, u32[]{:S(2)}) collective-permute-start(f32[8,8,128]{2,1,0:T(8,128)} %get-tuple-element.25), channel_id=1, source_target_pairs={{0,2},{1,3},{2,0},{3,1},{4,6},{5,7},{6,4},{7,5},{8,10},{9,11},{10,... | collective-permute-start | bytes 98312 | tf_op jit(solution)/shard_map/owners/ppermute | solution.py:22
  76.4 3.1 %collective-permute-start.9 = (f32[8,8,128]{2,1,0:T(8,128)}, f32[8,8,128]{2,1,0:T(8,128)S(1)}, u32[]{:S(2)}, u32[]{:S(2)}) collective-permute-start(f32[8,8,128]{2,1,0:T(8,128)} %get-tuple-element.26), channel_id=1, source_target_pairs={{0,3},{1,0},{2,1},{3,2},{4,7},{5,4},{6,5},{7,6},{8,11},{9,8},{10,9... | collective-permute-start | bytes 98312 | tf_op jit(solution)/shard_map/owners/ppermute | solution.py:22
  79.5 0.8 copy-start.2
  102.3 3.8 %collective-permute-start.10 = (f32[16,128]{1,0:T(8,128)S(1)}, f32[16,128]{1,0:T(8,128)S(1)}, u32[]{:S(2)}, u32[]{:S(2)}) collective-permute-start(f32[16,128]{1,0:T(8,128)S(1)} %sum.1.p0), channel_id=1, source_target_pairs={{0,1},{1,2},{2,3},{3,0},{4,5},{5,6},{6,7},{7,4},{8,9},{9,10},{10,1... | collective-permute-start | bytes 24584 | tf_op jit(solution)/shard_map/owners/ppermute | solution.py:22
  102.4 4.1 %collective-permute-start.11 = (f32[16,128]{1,0:T(8,128)S(1)}, f32[16,128]{1,0:T(8,128)S(1)}, u32[]{:S(2)}, u32[]{:S(2)}) collective-permute-start(f32[16,128]{1,0:T(8,128)S(1)} %sum.1.p0), channel_id=1, source_target_pairs={{0,2},{1,3},{2,0},{3,1},{4,6},{5,7},{6,4},{7,5},{8,10},{9,11},{10,... | collective-permute-start | bytes 24584 | tf_op jit(solution)/shard_map/owners/ppermute | solution.py:22
  105.2 2.5 %collective-permute-start.12 = (f32[16,128]{1,0:T(8,128)S(1)}, f32[16,128]{1,0:T(8,128)S(1)}, u32[]{:S(2)}, u32[]{:S(2)}) collective-permute-start(f32[16,128]{1,0:T(8,128)S(1)} %sum.1.p0), channel_id=1, source_target_pairs={{0,3},{1,0},{2,1},{3,2},{4,7},{5,4},{6,5},{7,6},{8,11},{9,8},{10,9... | collective-permute-start | bytes 24584 | tf_op jit(solution)/shard_map/owners/ppermute | solution.py:22

commit v2 on v1

--- a/solution.py
+++ b/solution.py
@@ -16,6 +16,7 @@
 VMEM = pl.BlockSpec(memory_space=pltpu.VMEM)
 SMEM = pl.BlockSpec(memory_space=pltpu.SMEM)
 LARGE, SMALL = 58 * 1024 * 1024, 12 * 1024 * 1024
+PITCH = 65
 
 
 def shift(values, k):
@@ -24,11 +25,6 @@
 
 def nt(a, b):
     return lax.dot_general(a, b, (((1,), (1,)), ((), ())), preferred_element_type=F32)
-
-
-def eye(n):
-    rows = lax.broadcasted_iota(jnp.int32, (n, n), 0)
-    return jnp.where(rows == lax.broadcasted_iota(jnp.int32, (n, n), 1), 1.0, 0.0).astype(BF16)
 
 
 def low_lanes(rows):
@@ -68,15 +64,16 @@
                         start = ((q * 2 + odd) * 2 + i) * 32
                         hot_ref[arr, start:start + 32, :] = jnp.where(hit, 1.0, 0.0).astype(BF16)
 
-    wide, narrow = eye(256), eye(128)
     for s in range(16):
         cut = slice(s * 256, s * 256 + 256)
         turned = jnp.concatenate([t_ref[0, :, cut], t_ref[1, :, cut]], axis=0).T
-        scr[cut, :] = turned.astype(F32)
+        for k in range(4):
+            at = (4 * s + k) * PITCH
+            scr[at:at + BS, :] = turned[k * BS:k * BS + BS].astype(F32)
         tr_ref[0, cut, :] = turned.astype(BF16)
     for s in range(16):
         cut = slice(s * 256, s * 256 + 256)
-        rows = jnp.concatenate([scr[pl.ds(4 * s + k, BS, stride=BS), :] for k in range(4)], axis=0)
+        rows = jnp.concatenate([scr[pl.ds(4 * s + k, BS, stride=PITCH), :] for k in range(4)], axis=0)
         back = rows.astype(BF16).T
         sw_ref[0, :, cut] = back[:BS]
         sw_ref[1, :, cut] = back[BS:]
@@ -95,7 +92,7 @@
         ),
         in_specs=[SMEM] * 4 + [spec],
         out_specs=(spec, pl.BlockSpec((1, BS * BS, 128), lambda i: (i, 0, 0)), pl.BlockSpec((2, 256, 256), lambda i: (0, 0, 0))),
-        scratch_shapes=[pltpu.VMEM((BS * BS, 128), F32)],
+        scratch_shapes=[pltpu.VMEM((BS * PITCH, 128), F32)],
         cost_estimate=pl.CostEstimate(flops=9_000_000_000, bytes_accessed=6 * tiles.size, transcendentals=0),
         compiler_params=pltpu.CompilerParams(vmem_limit_bytes=LARGE),
         name="prep",
@@ -129,17 +126,17 @@
     @pl.when(step == 0)
     def _():
         for k, ref in enumerate((g0, g1, g2, g3)):
-            start = pl.multiple_of(((me - k + NX) & 3) * 256, 256)
-            gscr[pl.ds(start, 256), :] = ref[...].reshape(256, 128).astype(F32)
-
-    m = lax.broadcasted_iota(jnp.int32, (BS, BS), 0)
-    place = (((m >> 2) & 3) << 4) + ((m >> 5) << 3) + (((m >> 4) & 1) << 2) + (m & 3)
-    order = jnp.where(place == lax.broadcasted_iota(jnp.int32, (BS, BS), 1), 1.0, 0.0).astype(BF16)
+            first = ((me - k + NX) & 3) * 4
+            for l in range(2):
+                for c in range(2):
+                    for i in range(4):
+                        at = pl.multiple_of((first + (l * 32 + c * 16 + i)) * 24, 8)
+                        gscr[pl.ds(at, 16), :] = ref[l, c, i].astype(F32)
+
     low = low_lanes(BS)
 
     def blocks_t(arr, u):
-        rows = gscr[pl.ds(arr * 8 + step * 2 + u, BS, stride=16), :].astype(BF16)
-        rows = jnp.dot(order, rows, preferred_element_type=F32)
+        rows = gscr[pl.ds(arr * 8 + step * 2 + u, BS, stride=24), :]
         turned = jnp.concatenate([rows, rows], axis=0).T
         return turned[:BS], turned[BS:]
 
@@ -167,8 +164,9 @@
         ], axis=0)
         out = jnp.dot(virt, rhs, preferred_element_type=F32)
         for ref, first in ((us, 0), (ws, 128)):
-            ref[s * 256:s * 256 + 128, :] = out[first:first + 128, :128]
-            ref[s * 256 + 128:s * 256 + 256, :] = out[first:first + 128, 128:]
+            for k in range(4):
+                at, row, lane = (4 * s + k) * PITCH, first + (k % 2) * BS, (k // 2) * 128
+                ref[at:at + BS, :] = out[row:row + BS, lane:lane + 128]
     for u in range(2):
         same, cross = blocks_t(0, u)
         for ref, dest, block in ((sw_ref, ys, same), (t_ref, zs, cross)):
@@ -179,9 +177,9 @@
     acc = jnp.zeros((128, 128), F32)
     for left, right in ((ys, us), (zs, ws)):
         for s in range(16):
-            rows = jnp.concatenate([right[pl.ds(4 * s + k, BS, stride=BS), :] for k in range(4)], axis=0)
+            rows = jnp.concatenate([right[pl.ds(4 * s + k, BS, stride=PITCH), :] for k in range(4)], axis=0)
             acc += jnp.dot(left[:, s * 256:s * 256 + 256], rows.astype(BF16), preferred_element_type=F32)
-    acc = acc.T * (1.0 / BS)
+    acc = acc * (1.0 / BS)
     low32 = low_lanes(32)
     pk[0] = jnp.where(low32, acc[:32], pltpu.roll(acc[32:64], BS, 1))
     pk[1] = jnp.where(low32, pltpu.roll(acc[64:96], BS, 1), acc[96:])
@@ -201,7 +199,7 @@
         in_specs=[SMEM, tile, tile, pl.BlockSpec((1, BS * BS, 128), lambda i: (i, 0, 0))] + [VMEM] * 4,
         out_specs=[pl.BlockSpec((2, 8, 128), lambda i: (i, 0, 0))] * NX,
         scratch_shapes=[
-            pltpu.VMEM((1024, 128), F32), pltpu.VMEM((BS * BS, 128), F32), pltpu.VMEM((BS * BS, 128), F32),
+            pltpu.VMEM((BS * 24, 128), F32), pltpu.VMEM((BS * PITCH, 128), F32), pltpu.VMEM((BS * PITCH, 128), F32),
             pltpu.VMEM((128, BS * BS), BF16), pltpu.VMEM((128, BS * BS), BF16), pltpu.VMEM((2, 32, 128), F32),
         ],
         compiler_params=pltpu.CompilerParams(vmem_limit_bytes=LARGE),
@@ -240,10 +238,10 @@
         x = (me - k + NX) & 3
         for aux in range(AUX):
             whole[aux, x] = ref[8 * aux:8 * aux + 8]
-    for aux in range(AUX):
-        rows = whole[aux].reshape(32, 128)
-        o_ref[aux * BS:aux * BS + 32, :] = rows[:, :BS]
-        o_ref[aux * BS + 32:(aux + 1) * BS, :] = pltpu.roll(rows, BS, 1)[:, :BS]
+    one, two = whole[0].reshape(32, 128), whole[1].reshape(32, 128)
+    low = low_lanes(32)
+    o_ref[:32, :] = jnp.where(low, one, pltpu.roll(two, BS, 1))
+    o_ref[32:, :] = jnp.where(low, pltpu.roll(one, BS, 1), two)
 
 
 def shards(tiles, tile_dest, tile_aux, tile_row, tile_col, green_occ, green_virt):
@@ -264,8 +262,9 @@
             name="rows",
         )(green_occ, green_virt)
         rows = lax.all_to_all(own, ZHL, 0, 0)
-        other = lax.ppermute(rows, "c", [(0, 1), (1, 0)])
     swapped, turned, hot = prep(infos, tiles)
+    rows, hot = lax.optimization_barrier((rows, hot))
+    other = lax.ppermute(rows, "c", [(0, 1), (1, 0)])
 
     with jax.named_scope("pick_blocks"):
         picked = pl.pallas_call(
@@ -288,15 +287,16 @@
             compiler_params=pltpu.CompilerParams(vmem_limit_bytes=SMALL), name="sum",
         )(spread)
         parts = [owned] + [shift(owned, k) for k in range(1, NX)]
-        return pl.pallas_call(
+        out = pl.pallas_call(
             finish_kernel,
-            out_shape=jax.ShapeDtypeStruct((AUX * BS, BS), F32),
+            out_shape=jax.ShapeDtypeStruct((BS, AUX * BS), F32),
             in_specs=[SMEM] + [VMEM] * 4,
-            out_specs=pl.BlockSpec((AUX * BS, BS), lambda: (0, 0)),
+            out_specs=pl.BlockSpec((BS, AUX * BS), lambda: (0, 0)),
             scratch_shapes=[pltpu.VMEM((AUX, NX, 8, 128), F32)],
             compiler_params=pltpu.CompilerParams(vmem_limit_bytes=SMALL),
             name="finish",
         )(me, *parts)
+        return out.T
 
 
 def solution(mesh):

time: 109 us -> 94.7 us (0.87)
  Pallas kernels: 31.3 us -> 20.6 us
  blocking collectives: 21.1 us -> 24.6 us
  waiting for transfers between devices: 16.6 us -> 13.5 us
  starting transfers between devices: 31.8 us -> 28.8 us
    all_to_all x1, waiting for transfers between devices: 10 us -> 0.41 us  [shards(): rows = lax.all_to_all(own, ZHL, 0, 0)]
    pallas_call x1, Pallas kernels: 20 us -> 10.7 us  [tile_pairs(): pl.pallas_call(tile_kernel, grid=(count // 2,), out_shape=[jax.ShapeDtype...]
    ppermute x12, waiting for transfers between devices: 6.6 us -> 11.6 us  [shift(): return lax.ppermute(values, 'x', [(i, (i + k) % NX) for i in range(NX)])]
    all_to_all x1, blocking collectives: 21.1 us -> 24.6 us  [shards(): spread = lax.all_to_all(place(infos, terms), TENS, 0, 0)]
    ppermute x12, starting transfers between devices: 17.4 us -> 14.4 us  [shift(): return lax.ppermute(values, 'x', [(i, (i + k) % NX) for i in range(NX)])]
    pallas_call x1, Pallas kernels: 8.69 us -> 6.55 us  [prep(): pl.pallas_call(prep_kernel, grid=(count // 2,), out_shape=(jax.ShapeDtype...]
    ppermute x1, waiting for transfers between devices: 0.01 us -> 1.54 us  [shards(): other = lax.ppermute(rows, 'c', [(0, 1), (1, 0)])]
  transfers between devices with their start and end apart: 14 -> 14, of which waited for: 9 -> 12; matrix products, arithmetic and copies ran while one was open for 1% -> 1% of each run, Pallas kernels for 8% -> 7%
where the time goes in v2:
time: 94.7 us; the launch traced here: 94.2 us
  starting transfers between devices  28.8 us (30%)
  blocking collectives  24.6 us (26%)
  Pallas kernels  20.6 us (22%)
  waiting for transfers between devices  13.5 us (14%)
  local copies, waits for them, and re-layouts  5.27 us (6%)
  other arithmetic  1.36 us (1%)
    all_to_all x1, blocking collectives, shards(): spread = lax.all_to_all(place(infos, terms), TENS, 0, 0)  24.6 us
    ppermute x12, starting transfers between devices, shift(): return lax.ppermute(values, 'x', [(i, (i + k) % NX) for i in range(NX)])  14.4 us
    all_to_all x1, starting transfers between devices, shards(): rows = lax.all_to_all(own, ZHL, 0, 0)  12 us
    ppermute x12, waiting for transfers between devices, shift(): return lax.ppermute(values, 'x', [(i, (i + k) % NX) for i in range(NX)])  11.6 us
    pallas_call x1, Pallas kernels, tile_pairs(): pl.pallas_call(tile_kernel, grid=(count // 2,), out_shape=[jax.ShapeDtype...  10.7 us
    pallas_call x1, Pallas kernels, prep(): pl.pallas_call(prep_kernel, grid=(count // 2,), out_shape=(jax.ShapeDtype...  6.55 us
    unnamed x32, local copies, waits for them, and re-layouts  5.27 us
    ppermute x1, starting transfers between devices, shards(): other = lax.ppermute(rows, 'c', [(0, 1), (1, 0)])  2.39 us
  transfers between devices with their start and end apart: 14, of which 12 were waited for; matrix products, arithmetic and copies ran while one was open for 1% of the time, Pallas kernels for 7%

profile of v2, /device:TPU:1, one launch (start us, length us, event | category | flops | bytes accessed | tf_op | source)
XLA Modules:
  0.0 94.2 jit_solution(15309053907599710313)
XLA Ops:
  0.0 0.0 copy-start.3
  0.0 0.7 copy-done.3
  0.7 0.7 copy-done.4
  1.4 0.9 rows.1
  2.3 12.0 %all-to-all-start = ((bf16[32,64,128]{2,1,0:T(8,128)(2,1)}), bf16[32,64,128]{2,1,0:T(8,128)(2,1)S(1)}, u32[]{:S(2)}, u32[]{:S(2)}) async-start(bf16[32,64,128]{2,1,0:T(8,128)(2,1)} %rows.1), calls=%async_computation | async-start | bytes 1048576 | tf_op jit(solution)/shard_map/gather_rows/all_to_all | solution.py:264
  14.4 0.7 add_bitcast_fusion
  15.0 0.7 pad_add_fusion.i0
  15.7 0.0 copy-start.5
  15.7 2.6 %collective-permute-start.2 = (s32[3,8]{1,0:T(4,128)S(1)}, s32[3,8]{1,0:T(4,128)S(1)}, u32[]{:S(2)}, u32[]{:S(2)}) collective-permute-start(s32[3,8]{1,0:T(4,128)S(1)} %pad_add_fusion.i0), channel_id=1, source_target_pairs={{0,3},{1,0},{2,1},{3,2},{4,7},{5,4},{6,5},{7,6},{8,11},{9,8},{10,9... | collective-permute-start | bytes 296 | tf_op jit(solution)/shard_map/ppermute | solution.py:23
  18.3 0.5 collective-permute-start.1
  18.8 0.6 collective-permute-start
  19.4 0.0 collective-permute-done.2.i3
  19.4 0.0 copy-start.7
  19.4 3.1 %collective-permute-done.1.i2 = s32[3,8]{1,0:T(4,128)S(1)} collective-permute-done((s32[3,8]{1,0:T(4,128)S(1)}, s32[3,8]{1,0:T(4,128)S(1)}, u32[]{:S(2)}, u32[]{:S(2)}) %collective-permute-start.1) | collective-permute-done | bytes 128 | tf_op jit(solution)/shard_map/ppermute | solution.py:23
  22.5 0.0 copy-start.9
  22.5 0.2 collective-permute-done.i1
  22.7 0.0 copy-done.5
  22.7 0.0 copy-done.7
  22.7 0.4 copy-done.9
  23.1 0.0 copy-start.11
  23.1 0.6 copy-done.11
  23.7 6.6 %prep.1 = (bf16[8,64,4096]{2,1,0:T(8,128)(2,1)}, bf16[4,4096,128]{2,1,0:T(8,128)(2,1)}, bf16[2,256,256]{2,1,0:T(8,128)(2,1)}) custom-call(s32[3,8]{1,0:T(4,128)} %copy-done.5, s32[3,8]{1,0:T(4,128)} %copy-done.11, s32[3,8]{1,0:T(4,128)} %copy-done.9, s32[3,8]{1,0:T(4,128)} %copy-done.7, bf16[8,64,4096]{2,1,0:T(8,128)(2,1)} %t_ref.3), custom_call_target="tpu_custom_call" | custom-call | flops 8999999488 | bytes 12582912 | tf_op jit(solution)/shard_map/prep/pallas_call | solution.py:85
  30.2 0.4 all-to-all-done.own_ref
  30.6 2.4 %collective-permute-start.3 = (bf16[32,64,128]{2,1,0:T(8,128)(2,1)S(1)}, bf16[32,64,128]{2,1,0:T(8,128)(2,1)S(1)}, u32[]{:S(2)}, u32[]{:S(2)}) collective-permute-start(bf16[32,64,128]{2,1,0:T(8,128)(2,1)S(1)} %all-to-all-done.own_ref), channel_id=1, source_target_pairs={{0,4},{4,0},{1,5},{5,1},{2,6},{6,2},{3,7},{7,3},{8,12},{12,8},{9,1... | collective-permute-start | bytes 1572872 | tf_op jit(solution)/shard_map/ppermute | solution.py:267
  33.0 1.5 %collective-permute-done.3.other_ref = bf16[32,64,128]{2,1,0:T(8,128)(2,1)S(1)} collective-permute-done((bf16[32,64,128]{2,1,0:T(8,128)(2,1)S(1)}, bf16[32,64,128]{2,1,0:T(8,128)(2,1)S(1)}, u32[]{:S(2)}, u32[]{:S(2)}) %collective-permute-start.3) | collective-permute-done | bytes 524320 | tf_op jit(solution)/shard_map/ppermute | solution.py:267
  34.6 0.0 copy-start
  34.6 0.9 %copy-done = bf16[2,256,256]{2,1,0:T(8,128)(2,1)S(1)} copy-done((bf16[2,256,256]{2,1,0:T(8,128)(2,1)S(1)}, bf16[2,256,256]{2,1,0:T(8,128)(2,1)}, u32[]{:S(2)}) %copy-start) | copy-done | bytes 262168
  35.5 0.7 pick.1
  36.3 0.0 copy-start.1
  36.3 0.6 copy-done.1
  36.9 1.2 %collective-permute-start.4 = (bf16[2,2,4,16,128]{4,3,2,1,0:T(8,128)(2,1)S(1)}, bf16[2,2,4,16,128]{4,3,2,1,0:T(8,128)(2,1)S(1)}, u32[]{:S(2)}, u32[]{:S(2)}) collective-permute-start(bf16[2,2,4,16,128]{4,3,2,1,0:T(8,128)(2,1)S(1)} %get-tuple-element.24), channel_id=1, source_target_pairs={{0,1},{1,2},{2,3},{3,0},{4,5},{5,6},{6,7},{7,4},{8,9},{9,10},{10,1... | collective-permute-start | bytes 196616 | tf_op jit(solution)/shard_map/pick_blocks/ppermute | solution.py:23
  38.1 2.4 %collective-permute-start.5 = (bf16[2,2,4,16,128]{4,3,2,1,0:T(8,128)(2,1)S(1)}, bf16[2,2,4,16,128]{4,3,2,1,0:T(8,128)(2,1)S(1)}, u32[]{:S(2)}, u32[]{:S(2)}) collective-permute-start(bf16[2,2,4,16,128]{4,3,2,1,0:T(8,128)(2,1)S(1)} %get-tuple-element.25), channel_id=1, source_target_pairs={{0,2},{1,3},{2,0},{3,1},{4,6},{5,7},{6,4},{7,5},{8,10},{9,11},{10,... | collective-permute-start | bytes 196616 | tf_op jit(solution)/shard_map/pick_blocks/ppermute | solution.py:23
  40.5 1.2 %collective-permute-start.6 = (bf16[2,2,4,16,128]{4,3,2,1,0:T(8,128)(2,1)S(1)}, bf16[2,2,4,16,128]{4,3,2,1,0:T(8,128)(2,1)S(1)}, u32[]{:S(2)}, u32[]{:S(2)}) collective-permute-start(bf16[2,2,4,16,128]{4,3,2,1,0:T(8,128)(2,1)S(1)} %get-tuple-element.26), channel_id=1, source_target_pairs={{0,3},{1,0},{2,1},{3,2},{4,7},{5,4},{6,5},{7,6},{8,11},{9,8},{10,9... | collective-permute-start | bytes 196616 | tf_op jit(solution)/shard_map/pick_blocks/ppermute | solution.py:23
  41.7 0.0 collective-permute-done.4.g1
  41.7 0.0 copy-start.13
  41.7 1.8 %collective-permute-done.5.g2 = bf16[2,2,4,16,128]{4,3,2,1,0:T(8,128)(2,1)S(1)} collective-permute-done((bf16[2,2,4,16,128]{4,3,2,1,0:T(8,128)(2,1)S(1)}, bf16[2,2,4,16,128]{4,3,2,1,0:T(8,128)(2,1)S(1)}, u32[]{:S(2)}, u32[]{:S(2)}) %collective-permute-start.5) | collective-permute-done | bytes 65568 | tf_op jit(solution)/shard_map/pick_blocks/ppermute | solution.py:23
  43.5 0.0 copy-start.14
  43.5 0.5 collective-permute-done.6.g3
  44.0 0.0 copy-done.13
  44.0 0.1 copy-done.14
  44.1 0.5 copy-done.15
  44.6 10.7 %tile_pairs.1 = (f32[8,8,128]{2,1,0:T(8,128)}, f32[8,8,128]{2,1,0:T(8,128)}, f32[8,8,128]{2,1,0:T(8,128)}, f32[8,8,128]{2,1,0:T(8,128)}) custom-call(s32[1]{0:T(128)} %bitcast.me_ref, bf16[8,64,4096]{2,1,0:T(8,128)(2,1)} %t_ref.3, bf16[8,64,4096]{2,1,0:T(8,128)(2,1)} %get-tuple-element.18.sw_ref, bf16[4,4096,128]{2,1,0:T(8,128)(2,1)} %get-tuple-element.19.tr_ref, ...), custom_call_target="tpu_custom_call" | custom-call | tf_op jit(solution)/shard_map/tile_pairs/pallas_call | solution.py:195
  55.3 0.1 collective-permute-start.7
  55.5 3.2 %collective-permute-start.8 = (f32[8,8,128]{2,1,0:T(8,128)}, f32[8,8,128]{2,1,0:T(8,128)S(1)}, u32[]{:S(2)}, u32[]{:S(2)}) collective-permute-start(f32[8,8,128]{2,1,0:T(8,128)} %get-tuple-element.29), channel_id=1, source_target_pairs={{0,2},{1,3},{2,0},{3,1},{4,6},{5,7},{6,4},{7,5},{8,10},{9,11},{10,... | collective-permute-start | bytes 98312 | tf_op jit(solution)/shard_map/owners/ppermute | solution.py:23
  58.7 0.4 collective-permute-start.9
  59.0 0.6 collective-permute-done.7.t1
  59.6 0.9 collective-permute-done.8.t2
  60.5 1.4 %collective-permute-done.9.t3 = f32[8,8,128]{2,1,0:T(8,128)S(1)} collective-permute-done((f32[8,8,128]{2,1,0:T(8,128)}, f32[8,8,128]{2,1,0:T(8,128)S(1)}, u32[]{:S(2)}, u32[]{:S(2)}) %collective-permute-start.9) | collective-permute-done | bytes 32800 | tf_op jit(solution)/shard_map/owners/ppermute | solution.py:23
  61.9 0.0 copy-done.6
  61.9 0.0 copy-done.8
  61.9 0.0 copy-done.10
  62.0 0.0 copy-done.12
  62.0 0.0 copy-start.2
  62.0 0.7 copy-done.2
  62.7 0.8 place.1
  63.6 24.6 %all_to_all.10.s_ref = bf16[64,16,128]{2,1,0:T(8,128)(2,1)S(1)} all-to-all(bf16[64,16,128]{2,1,0:T(8,128)(2,1)S(1)} %place.1), channel_id=1, replica_groups=mesh['z'=8,'h'=2,'l'=2,'c'=2,'x'=4] {'z','h','l','c'}, dimensions={0} | all-to-all | bytes 524288 | tf_op jit(solution)/shard_map/owners/all_to_all | solution.py:284
  88.2 0.1 sum.1.p0
  88.3 1.0 %collective-permute-start.12 = (f32[16,128]{1,0:T(8,128)S(1)}, f32[16,128]{1,0:T(8,128)S(1)}, u32[]{:S(2)}, u32[]{:S(2)}) collective-permute-start(f32[16,128]{1,0:T(8,128)S(1)} %sum.1.p0), channel_id=1, source_target_pairs={{0,3},{1,0},{2,1},{3,2},{4,7},{5,4},{6,5},{7,6},{8,11},{9,8},{10,9... | collective-permute-start | bytes 24584 | tf_op jit(solution)/shard_map/owners/ppermute | solution.py:23
  89.3 0.5 collective-permute-start.11
  89.8 0.6 collective-permute-start.10
  90.5 0.4 collective-permute-done.12.p3
  90.9 2.4 %collective-permute-done.11.p2 = f32[16,128]{1,0:T(8,128)S(1)} collective-permute-done((f32[16,128]{1,0:T(8,128)S(1)}, f32[16,128]{1,0:T(8,128)S(1)}, u32[]{:S(2)}, u32[]{:S(2)}) %collective-permute-start.11) | collective-permute-done | bytes 8224 | tf_op jit(solution)/shard_map/owners/ppermute | solution.py:23
  93.3 0.2 collective-permute-done.10.p1
  93.5 0.7 finish.1
  (6 shorter events, 0.0 us)
Async XLA Ops:
  0.0 0.7 copy-start.3
  0.7 0.7 copy-start.4
  2.3 28.3 %all-to-all-start = ((bf16[32,64,128]{2,1,0:T(8,128)(2,1)}), bf16[32,64,128]{2,1,0:T(8,128)(2,1)S(1)}, u32[]{:S(2)}, u32[]{:S(2)}) async-start(bf16[32,64,128]{2,1,0:T(8,128)(2,1)} %rows.1), calls=%async_computation | async-start | bytes 1048576 | tf_op jit(solution)/shard_map/gather_rows/all_to_all | solution.py:264
  15.7 7.0 %copy-start.5 = (s32[3,8]{1,0:T(4,128)}, s32[3,8]{1,0:T(4,128)S(1)}, u32[]{:S(2)}) copy-start(s32[3,8]{1,0:T(4,128)S(1)} %pad_add_fusion.i0) | copy-start | bytes 292
  15.7 3.7 %collective-permute-start.2 = (s32[3,8]{1,0:T(4,128)S(1)}, s32[3,8]{1,0:T(4,128)S(1)}, u32[]{:S(2)}, u32[]{:S(2)}) collective-permute-start(s32[3,8]{1,0:T(4,128)S(1)} %pad_add_fusion.i0), channel_id=1, source_target_pairs={{0,3},{1,0},{2,1},{3,2},{4,7},{5,4},{6,5},{7,6},{8,11},{9,8},{10,9... | collective-permute-start | bytes 296 | tf_op jit(solution)/shard_map/ppermute | solution.py:23
  18.3 4.2 %collective-permute-start.1 = (s32[3,8]{1,0:T(4,128)S(1)}, s32[3,8]{1,0:T(4,128)S(1)}, u32[]{:S(2)}, u32[]{:S(2)}) collective-permute-start(s32[3,8]{1,0:T(4,128)S(1)} %pad_add_fusion.i0), channel_id=1, source_target_pairs={{0,2},{1,3},{2,0},{3,1},{4,6},{5,7},{6,4},{7,5},{8,10},{9,11},{10,... | collective-permute-start | bytes 296 | tf_op jit(solution)/shard_map/ppermute | solution.py:23
  18.8 3.9 %collective-permute-start = (s32[3,8]{1,0:T(4,128)S(1)}, s32[3,8]{1,0:T(4,128)S(1)}, u32[]{:S(2)}, u32[]{:S(2)}) collective-permute-start(s32[3,8]{1,0:T(4,128)S(1)} %pad_add_fusion.i0), channel_id=1, source_target_pairs={{0,1},{1,2},{2,3},{3,0},{4,5},{5,6},{6,7},{7,4},{8,9},{9,10},{10,1... | collective-permute-start | bytes 296 | tf_op jit(solution)/shard_map/ppermute | solution.py:23
  19.4 3.3 %copy-start.7 = (s32[3,8]{1,0:T(4,128)}, s32[3,8]{1,0:T(4,128)S(1)}, u32[]{:S(2)}) copy-start(s32[3,8]{1,0:T(4,128)S(1)} %collective-permute-done.2.i3) | copy-start | bytes 292
  22.5 0.6 copy-start.9
  23.1 0.6 copy-start.11
  30.6 3.9 %collective-permute-start.3 = (bf16[32,64,128]{2,1,0:T(8,128)(2,1)S(1)}, bf16[32,64,128]{2,1,0:T(8,128)(2,1)S(1)}, u32[]{:S(2)}, u32[]{:S(2)}) collective-permute-start(bf16[32,64,128]{2,1,0:T(8,128)(2,1)S(1)} %all-to-all-done.own_ref), channel_id=1, source_target_pairs={{0,4},{4,0},{1,5},{5,1},{2,6},{6,2},{3,7},{7,3},{8,12},{12,8},{9,1... | collective-permute-start | bytes 1572872 | tf_op jit(solution)/shard_map/ppermute | solution.py:267
  34.6 0.9 %copy-start = (bf16[2,256,256]{2,1,0:T(8,128)(2,1)S(1)}, bf16[2,256,256]{2,1,0:T(8,128)(2,1)}, u32[]{:S(2)}) copy-start(bf16[2,256,256]{2,1,0:T(8,128)(2,1)} %get-tuple-element.21.hot_ref) | copy-start | bytes 786436
  36.3 0.6 copy-start.1
  36.9 4.8 %collective-permute-start.4 = (bf16[2,2,4,16,128]{4,3,2,1,0:T(8,128)(2,1)S(1)}, bf16[2,2,4,16,128]{4,3,2,1,0:T(8,128)(2,1)S(1)}, u32[]{:S(2)}, u32[]{:S(2)}) collective-permute-start(bf16[2,2,4,16,128]{4,3,2,1,0:T(8,128)(2,1)S(1)} %get-tuple-element.24), channel_id=1, source_target_pairs={{0,1},{1,2},{2,3},{3,0},{4,5},{5,6},{6,7},{7,4},{8,9},{9,10},{10,1... | collective-permute-start | bytes 196616 | tf_op jit(solution)/shard_map/pick_blocks/ppermute | solution.py:23
  38.1 5.4 %collective-permute-start.5 = (bf16[2,2,4,16,128]{4,3,2,1,0:T(8,128)(2,1)S(1)}, bf16[2,2,4,16,128]{4,3,2,1,0:T(8,128)(2,1)S(1)}, u32[]{:S(2)}, u32[]{:S(2)}) collective-permute-start(bf16[2,2,4,16,128]{4,3,2,1,0:T(8,128)(2,1)S(1)} %get-tuple-element.25), channel_id=1, source_target_pairs={{0,2},{1,3},{2,0},{3,1},{4,6},{5,7},{6,4},{7,5},{8,10},{9,11},{10,... | collective-permute-start | bytes 196616 | tf_op jit(solution)/shard_map/pick_blocks/ppermute | solution.py:23
  40.5 3.4 %collective-permute-start.6 = (bf16[2,2,4,16,128]{4,3,2,1,0:T(8,128)(2,1)S(1)}, bf16[2,2,4,16,128]{4,3,2,1,0:T(8,128)(2,1)S(1)}, u32[]{:S(2)}, u32[]{:S(2)}) collective-permute-start(bf16[2,2,4,16,128]{4,3,2,1,0:T(8,128)(2,1)S(1)} %get-tuple-element.26), channel_id=1, source_target_pairs={{0,3},{1,0},{2,1},{3,2},{4,7},{5,4},{6,5},{7,6},{8,11},{9,8},{10,9... | collective-permute-start | bytes 196616 | tf_op jit(solution)/shard_map/pick_blocks/ppermute | solution.py:23
  41.7 2.3 %copy-start.13 = (bf16[2,2,4,16,128]{4,3,2,1,0:T(8,128)(2,1)}, bf16[2,2,4,16,128]{4,3,2,1,0:T(8,128)(2,1)S(1)}, u32[]{:S(2)}) copy-start(bf16[2,2,4,16,128]{4,3,2,1,0:T(8,128)(2,1)S(1)} %collective-permute-done.4.g1) | copy-start | bytes 196612
  43.5 0.6 copy-start.14
  44.0 0.6 copy-start.15
  44.6 17.4 %copy-start.6 = (s32[3,8]{1,0:T(4,128)S(1)}, s32[3,8]{1,0:T(4,128)}, u32[]{:S(2)}) copy-start(s32[3,8]{1,0:T(4,128)} %copy-done.5) | copy-start | bytes 292
  44.6 17.4 %copy-start.8 = (s32[3,8]{1,0:T(4,128)S(1)}, s32[3,8]{1,0:T(4,128)}, u32[]{:S(2)}) copy-start(s32[3,8]{1,0:T(4,128)} %copy-done.7) | copy-start | bytes 292
  44.6 17.4 %copy-start.10 = (s32[3,8]{1,0:T(4,128)S(1)}, s32[3,8]{1,0:T(4,128)}, u32[]{:S(2)}) copy-start(s32[3,8]{1,0:T(4,128)} %copy-done.9) | copy-start | bytes 292
  44.6 17.4 %copy-start.12 = (s32[3,8]{1,0:T(4,128)S(1)}, s32[3,8]{1,0:T(4,128)}, u32[]{:S(2)}) copy-start(s32[3,8]{1,0:T(4,128)} %copy-done.11) | copy-start | bytes 292
  55.3 4.3 %collective-permute-start.7 = (f32[8,8,128]{2,1,0:T(8,128)}, f32[8,8,128]{2,1,0:T(8,128)S(1)}, u32[]{:S(2)}, u32[]{:S(2)}) collective-permute-start(f32[8,8,128]{2,1,0:T(8,128)} %get-tuple-element.28), channel_id=1, source_target_pairs={{0,1},{1,2},{2,3},{3,0},{4,5},{5,6},{6,7},{7,4},{8,9},{9,10},{10,1... | collective-permute-start | bytes 98312 | tf_op jit(solution)/shard_map/owners/ppermute | solution.py:23
  55.5 5.1 %collective-permute-start.8 = (f32[8,8,128]{2,1,0:T(8,128)}, f32[8,8,128]{2,1,0:T(8,128)S(1)}, u32[]{:S(2)}, u32[]{:S(2)}) collective-permute-start(f32[8,8,128]{2,1,0:T(8,128)} %get-tuple-element.29), channel_id=1, source_target_pairs={{0,2},{1,3},{2,0},{3,1},{4,6},{5,7},{6,4},{7,5},{8,10},{9,11},{10,... | collective-permute-start | bytes 98312 | tf_op jit(solution)/shard_map/owners/ppermute | solution.py:23
  58.7 3.3 %collective-permute-start.9 = (f32[8,8,128]{2,1,0:T(8,128)}, f32[8,8,128]{2,1,0:T(8,128)S(1)}, u32[]{:S(2)}, u32[]{:S(2)}) collective-permute-start(f32[8,8,128]{2,1,0:T(8,128)} %get-tuple-element.30), channel_id=1, source_target_pairs={{0,3},{1,0},{2,1},{3,2},{4,7},{5,4},{6,5},{7,6},{8,11},{9,8},{10,9... | collective-permute-start | bytes 98312 | tf_op jit(solution)/shard_map/owners/ppermute | solution.py:23
  62.0 0.8 copy-start.2
  88.3 2.6 %collective-permute-start.12 = (f32[16,128]{1,0:T(8,128)S(1)}, f32[16,128]{1,0:T(8,128)S(1)}, u32[]{:S(2)}, u32[]{:S(2)}) collective-permute-start(f32[16,128]{1,0:T(8,128)S(1)} %sum.1.p0), channel_id=1, source_target_pairs={{0,3},{1,0},{2,1},{3,2},{4,7},{5,4},{6,5},{7,6},{8,11},{9,8},{10,9... | collective-permute-start | bytes 24584 | tf_op jit(solution)/shard_map/owners/ppermute | solution.py:23
  89.3 4.0 %collective-permute-start.11 = (f32[16,128]{1,0:T(8,128)S(1)}, f32[16,128]{1,0:T(8,128)S(1)}, u32[]{:S(2)}, u32[]{:S(2)}) collective-permute-start(f32[16,128]{1,0:T(8,128)S(1)} %sum.1.p0), channel_id=1, source_target_pairs={{0,2},{1,3},{2,0},{3,1},{4,6},{5,7},{6,4},{7,5},{8,10},{9,11},{10,... | collective-permute-start | bytes 24584 | tf_op jit(solution)/shard_map/owners/ppermute | solution.py:23
  89.8 3.7 %collective-permute-start.10 = (f32[16,128]{1,0:T(8,128)S(1)}, f32[16,128]{1,0:T(8,128)S(1)}, u32[]{:S(2)}, u32[]{:S(2)}) collective-permute-start(f32[16,128]{1,0:T(8,128)S(1)} %sum.1.p0), channel_id=1, source_target_pairs={{0,1},{1,2},{2,3},{3,0},{4,5},{5,6},{6,7},{7,4},{8,9},{9,10},{10,1... | collective-permute-start | bytes 24584 | tf_op jit(solution)/shard_map/owners/ppermute | solution.py:23

commit v3 on v2

v3 whole, which is shorter than its diff:
```python
import jax
import jax.numpy as jnp
from jax import lax
from jax.experimental import pallas as pl
from jax.experimental.pallas import tpu as pltpu
from jax.sharding import Mesh, PartitionSpec as P

BS = 64
NA = 16
AUX = 2
ZH = ("z", "h")
ZHL = ("z", "h", "l")
LCX = ("l", "c", "x")
TENS = ("z", "h", "l", "c")
ALL = ("z", "h", "l", "c", "x")
NX = 4
NG = 16
F32, BF16 = jnp.float32, jnp.bfloat16
VMEM = pl.BlockSpec(memory_space=pltpu.VMEM)
SMEM = pl.BlockSpec(memory_space=pltpu.SMEM)
LARGE, MIDDLE, SMALL = 58 * 1024 * 1024, 52 * 1024 * 1024, 12 * 1024 * 1024
PITCH = 65


def shift(values, k):
    return lax.ppermute(values, "x", [(i, (i + k) % NX) for i in range(NX)])


def low_lanes(rows):
    return lax.broadcasted_iota(jnp.int32, (rows, 128), 1) < BS


def rows_kernel(occ_ref, virt_ref, o_ref, scr):
    for arr, ref in enumerate((occ_ref, virt_ref)):
        values = ref[...].astype(F32)
        for i in range(4):
            for pair in range(8):
                at = (arr * 4 + i) * 8 + pair
                scr[at:at + 1, :] = values[i:i + 1, pair * 128:pair * 128 + 128]
    block = scr[...].astype(BF16)
    for peer in range(o_ref.shape[0]):
        o_ref[peer] = block


def wants_kernel(row_ref, col_ref, dest_ref, aux_ref, o_ref):
    at = lax.broadcasted_iota(jnp.int32, (8, 128), 0)
    for j in range(3):
        found = jnp.zeros((8, 128), jnp.int32)
        for t in range(8):
            value = row_ref[t] if j == 0 else col_ref[t] if j == 1 else dest_ref[t] * AUX + aux_ref[t]
            found = jnp.where(at == t, value, found)
        o_ref[j] = found


def prep_kernel(t_ref, sw_ref, tr_ref, scr):
    for s in range(16):
        cut = slice(s * 256, s * 256 + 256)
        turned = jnp.concatenate([t_ref[0, :, cut], t_ref[1, :, cut]], axis=0).T
        for k in range(4):
            at = (4 * s + k) * PITCH
            scr[at:at + BS, :] = turned[k * BS:k * BS + BS].astype(F32)
        tr_ref[0, cut, :] = turned.astype(BF16)
    for s in range(16):
        cut = slice(s * 256, s * 256 + 256)
        rows = jnp.concatenate([scr[pl.ds(4 * s + k, BS, stride=PITCH), :] for k in range(4)], axis=0)
        back = rows.astype(BF16).T
        sw_ref[0, :, cut] = back[:BS]
        sw_ref[1, :, cut] = back[BS:]


def prep(tiles):
    count = tiles.shape[0]
    spec = pl.BlockSpec((2, BS, BS * BS), lambda i: (i, 0, 0))
    return pl.pallas_call(
        prep_kernel,
        grid=(count // 2,),
        out_shape=(
            jax.ShapeDtypeStruct(tiles.shape, BF16),
            jax.ShapeDtypeStruct((count // 2, BS * BS, 128), BF16),
        ),
        in_specs=[spec],
        out_specs=(spec, pl.BlockSpec((1, BS * BS, 128), lambda i: (i, 0, 0))),
        scratch_shapes=[pltpu.VMEM((BS * PITCH, 128), F32)],
        cost_estimate=pl.CostEstimate(flops=9_000_000_000, bytes_accessed=6 * tiles.size, transcendentals=0),
        compiler_params=pltpu.CompilerParams(vmem_limit_bytes=LARGE),
        name="prep",
    )(tiles)


def pick_kernel(core_ref, w0, w1, w2, w3, own_ref, other_ref, o0, o1, o2, o3):
    core = core_ref[0]
    row, col = (jnp.concatenate([w[j] for w in (w0, w1, w2, w3)], axis=0) for j in range(2))
    lane = lax.broadcasted_iota(jnp.int32, (32, 128), 1)
    low = low_lanes(32)
    hots = []
    for arr, first in enumerate((row, col)):
        hot = []
        for q in range(2):
            second = first if q == 0 else (col if arr == 0 else row)
            for odd in range(2):
                for i in range(2):
                    key = jnp.where((second & 1) == odd, first * 16 + i * 8 + (second >> 1), -1)
                    hot.append(jnp.concatenate([
                        jnp.where(lane == key, 1.0, 0.0).astype(BF16),
                        jnp.where(lane + 128 == key, 1.0, 0.0).astype(BF16),
                    ], axis=1))
        hots.append(jnp.concatenate(hot, axis=0))
    for side, ref in ((core, own_ref), (1 - core, other_ref)):
        for l in range(2):
            for ih in range(2):
                got = []
                for arr in range(2):
                    start = (arr * 2 + ih) * 16
                    table = jnp.concatenate([ref[2 * b + l, start:start + 16, :] for b in range(NA)], axis=0)
                    got.append(jnp.dot(hots[arr], table, preferred_element_type=F32))
                for il in range(2):
                    found = []
                    for arr in range(2):
                        g = [got[arr][(k * 2 + il) * 32:(k * 2 + il) * 32 + 32] for k in range(4)]
                        left = g[0] + pltpu.roll(g[1], BS, 1)
                        right = pltpu.roll(g[2], BS, 1) + g[3]
                        found.append(jnp.where(low, left, right))
                    for k, o_ref in enumerate((o0, o1, o2, o3)):
                        cut = slice(k * 8, k * 8 + 8)
                        o_ref[l, side, ih * 2 + il] = jnp.concatenate([f[cut] for f in found], axis=0).astype(BF16)


def tile_kernel(me_ref, t_ref, sw_ref, tr_ref, wants_ref, g0, g1, g2, g3, o_ref, gscr, us, ws, ys, zs, pk):
    step = pl.program_id(0)

    @pl.when(step == 0)
    def _():
        for k, ref in enumerate((g0, g1, g2, g3)):
            first = ((me_ref[0] - k + NX) & 3) * 4
            for l in range(2):
                for c in range(2):
                    for i in range(4):
                        at = pl.multiple_of((first + (l * 32 + c * 16 + i)) * 24, 8)
                        gscr[pl.ds(at, 16), :] = ref[l, c, i].astype(F32)

    low = low_lanes(BS)

    def blocks_t(arr, u):
        rows = gscr[pl.ds(arr * 8 + step * 2 + u, BS, stride=24), :]
        turned = jnp.concatenate([rows, rows], axis=0).T
        return turned[:BS], turned[BS:]

    def two(b):
        return jnp.concatenate([jnp.where(low, b, 0.0), jnp.where(low, 0.0, b)], axis=0).astype(BF16)

    def four(b):
        pair = two(b)
        none = jnp.zeros((128, 128), BF16)
        return jnp.concatenate([jnp.concatenate([pair, none], axis=1), jnp.concatenate([none, pair], axis=1)], axis=0)

    (cc0, cr0), (cc1, cr1) = blocks_t(1, 0), blocks_t(1, 1)
    virt = jnp.concatenate([
        jnp.concatenate([two(cc0), two(cc1)], axis=1),
        jnp.concatenate([two(cr0), two(cr1)], axis=1),
    ], axis=0)
    low128 = low_lanes(128)
    zero = jnp.zeros((128, 128), BF16)
    for s in range(16):
        a = tr_ref[0, s * 256:s * 256 + 128, :]
        b = tr_ref[0, s * 256 + 128:s * 256 + 256, :]
        rhs = jnp.concatenate([
            jnp.concatenate([jnp.where(low128, a, zero), jnp.where(low128, b, zero)], axis=1),
            jnp.concatenate([jnp.where(low128, zero, a), jnp.where(low128, zero, b)], axis=1),
        ], axis=0)
        out = jnp.dot(virt, rhs, preferred_element_type=F32)
        for ref, first in ((us, 0), (ws, 128)):
            for k in range(4):
                at, row, lane = (4 * s + k) * PITCH, first + (k % 2) * BS, (k // 2) * 128
                ref[at:at + BS, :] = out[row:row + BS, lane:lane + 128]
    for u in range(2):
        same, cross = blocks_t(0, u)
        for ref, dest, block in ((sw_ref, ys, same), (t_ref, zs, cross)):
            rows = jnp.concatenate([ref[u, :, s * 256:s * 256 + 256] for s in range(16)], axis=0)
            out = jnp.dot(rows, four(block), preferred_element_type=F32).astype(BF16)
            for s in range(16):
                dest[u * BS:u * BS + BS, s * 256:s * 256 + 256] = out[s * BS:s * BS + BS]
    acc = jnp.zeros((128, 128), F32)
    for left, right in ((ys, us), (zs, ws)):
        for s in range(16):
            rows = jnp.concatenate([right[pl.ds(4 * s + k, BS, stride=PITCH), :] for k in range(4)], axis=0)
            acc += jnp.dot(left[:, s * 256:s * 256 + 256], rows.astype(BF16), preferred_element_type=F32)
    acc = acc * (1.0 / BS)
    low32 = low_lanes(32)
    packed = (
        jnp.where(low32, acc[:32], pltpu.roll(acc[32:64], BS, 1)),
        jnp.where(low32, pltpu.roll(acc[64:96], BS, 1), acc[96:]),
    )
    for u in range(2):
        pk[pl.ds(pl.multiple_of((step * 2 + u) * 40, 8), 32), :] = packed[u]

    @pl.when(step == pl.num_programs(0) - 1)
    def _():
        target = wants_ref[2].astype(F32)
        for peer in range(NG):
            for half in range(2):
                o_ref[peer, half * 8:half * 8 + 8] = pk[pl.ds(2 * peer + half, 8, stride=40), :]
            o_ref[peer, 16:24] = target


def tile_pairs(me, tiles, swapped, turned, wants, got):
    count = tiles.shape[0]
    tile = pl.BlockSpec((2, BS, BS * BS), lambda i: (i, 0, 0))
    return pl.pallas_call(
        tile_kernel,
        grid=(count // 2,),
        out_shape=jax.ShapeDtypeStruct((NG, 3 * count, 128), F32),
        in_specs=[SMEM, tile, tile, pl.BlockSpec((1, BS * BS, 128), lambda i: (i, 0, 0))] + [VMEM] * 5,
        out_specs=pl.BlockSpec((NG, 3 * count, 128), lambda i: (0, 0, 0)),
        scratch_shapes=[
            pltpu.VMEM((BS * 24, 128), F32), pltpu.VMEM((BS * PITCH, 128), F32), pltpu.VMEM((BS * PITCH, 128), F32),
            pltpu.VMEM((128, BS * BS), BF16), pltpu.VMEM((128, BS * BS), BF16), pltpu.VMEM((count * 40, 128), F32),
        ],
        compiler_params=pltpu.CompilerParams(vmem_limit_bytes=MIDDLE),
        name="tile_pairs",
    )(me, tiles, swapped, turned, wants, *got)


def place_kernel(t_ref, o_ref):
    target = t_ref[:, 16:24, :].reshape(128, 128).astype(jnp.int32)
    lane = lax.broadcasted_iota(jnp.int32, (128, 128), 1)
    hot = jnp.where(lane == target, 1.0, 0.0).T.astype(BF16)
    dense = []
    for half in range(2):
        terms = t_ref[:, half * 8:half * 8 + 8, :].reshape(128, 128)
        high = terms.astype(BF16)
        rest = (terms - high.astype(F32)).astype(BF16)
        dense.append(jnp.dot(hot, high, preferred_element_type=F32) + jnp.dot(hot, rest, preferred_element_type=F32))
    for peer in range(NG):
        o_ref[peer] = jnp.concatenate([d[peer * 8:peer * 8 + 8] for d in dense], axis=0).astype(BF16)


def sum_kernel(s_ref, o_ref):
    total = jnp.sum(s_ref[...].astype(F32), axis=0)
    none = jnp.zeros((4, 128), F32)
    for peer in range(NG):
        at = (peer // 4) * 2
        rows = [total[half * 8 + at + aux:half * 8 + at + aux + 1] for aux in range(AUX) for half in range(2)]
        o_ref[peer] = jnp.concatenate(rows + [none], axis=0)


def finish_kernel(p_ref, o_ref, whole):
    for aux in range(AUX):
        for peer in range(NG):
            whole[aux, 2 * peer:2 * peer + 2, :] = p_ref[peer, 2 * aux:2 * aux + 2, :]
    one, two = whole[0], whole[1]
    low = low_lanes(32)
    o_ref[:32, :] = jnp.where(low, one, pltpu.roll(two, BS, 1))
    o_ref[32:, :] = jnp.where(low, pltpu.roll(one, BS, 1), two)


def call(kernel, name, out, *args, spaces=None, limit=SMALL, **more):
    return pl.pallas_call(
        kernel,
        out_shape=[jax.ShapeDtypeStruct(*s) for s in out] if isinstance(out, list) else jax.ShapeDtypeStruct(*out),
        in_specs=spaces or [VMEM] * len(args),
        compiler_params=pltpu.CompilerParams(vmem_limit_bytes=limit),
        name=name,
        **more,
    )(*args)


def shards(tiles, tile_dest, tile_aux, tile_row, tile_col, green_occ, green_virt):
    me = lax.axis_index("x").reshape(1)
    own = call(rows_kernel, "rows", ((32, BS, 128), BF16), green_occ, green_virt, limit=LARGE,
               out_specs=VMEM, scratch_shapes=[pltpu.VMEM((BS, 128), F32)])
    rows = lax.all_to_all(own, ZHL, 0, 0)
    tile_row, own = lax.optimization_barrier((tile_row, own))
    wants = call(wants_kernel, "wants", ((3, 8, 128), jnp.int32), tile_row, tile_col, tile_dest, tile_aux,
                 spaces=[SMEM] * 4, limit=LARGE, out_specs=VMEM)
    asked = [wants] + [shift(wants, k) for k in range(1, NX)]
    swapped, turned = prep(tiles)
    rows, turned, asked = lax.optimization_barrier((rows, turned, asked))
    other = lax.ppermute(rows, "c", [(0, 1), (1, 0)])
    picked = call(pick_kernel, "pick", [((2, 2, 4, 16, 128), BF16)] * NX, lax.axis_index("c").reshape(1), *asked, rows, other,
                  spaces=[SMEM] + [VMEM] * 6, out_specs=[VMEM] * NX)
    got = [picked[0]] + [shift(picked[NX - k], k) for k in range(1, NX)]
    pieces = tile_pairs(me, tiles, swapped, turned, wants, got)
    terms = lax.all_to_all(pieces, LCX, 0, 0)
    dense = call(place_kernel, "place", ((NG, 16, 128), BF16), terms, out_specs=VMEM)
    spread = lax.all_to_all(dense, ZH, 0, 0)
    owned = call(sum_kernel, "sum", ((NG, 8, 128), F32), spread, out_specs=VMEM)
    parts = lax.all_to_all(owned, LCX, 0, 0)
    out = call(finish_kernel, "finish", ((BS, AUX * BS), F32), parts,
               out_specs=pl.BlockSpec((BS, AUX * BS), lambda: (0, 0)),
               scratch_shapes=[pltpu.VMEM((AUX, 32, 128), F32)])
    return out.T


def solution(mesh):
    fine = Mesh(mesh.devices.reshape(8, 2, 2, 2, 4), ALL)
    return jax.shard_map(
        shards,
        mesh=fine,
        in_specs=(P(ALL, None, None), P(ALL), P(ALL), P(ALL), P(ALL), P(ALL, None), P(ALL, None)),
        out_specs=P(TENS, None),
        check_vma=False,
    )
```

time: 94.7 us -> 89 us (0.940)
  blocking collectives: 24.6 us -> 36 us
  starting transfers between devices: 28.8 us -> 22.9 us
  local copies, waits for them, and re-layouts: 5.27 us -> 0.01 us
  waiting for transfers between devices: 13.5 us -> 8.79 us
  other arithmetic: 1.36 us -> 0 us
    all_to_all x1 -> x3, blocking collectives: 24.6 us -> 36 us  [the longest x1 13.2 us: shards(): spread = lax.all_to_all(dense, ZH, 0, 0)]
    ppermute x12 -> x6, waiting for transfers between devices: 11.6 us -> 2.27 us  [shift(): return lax.ppermute(values, 'x', [(i, (i + k) % NX) for i in range(NX)])]
    ppermute x12 -> x6, starting transfers between devices: 14.4 us -> 8.49 us  [shift(): return lax.ppermute(values, 'x', [(i, (i + k) % NX) for i in range(NX)])]
    unnamed x32 -> x2, local copies, waits for them, and re-layouts: 5.27 us -> 0.01 us
    all_to_all x1, waiting for transfers between devices: 0.41 us -> 4.99 us  [shards(): rows = lax.all_to_all(own, ZHL, 0, 0)]
    another operation x2 -> x0, other arithmetic: 1.36 us -> none  [shards(): info = jnp.stack([tile_row, tile_col, tile_dest * AUX + tile_aux])]
    pallas_call x6 -> x7, Pallas kernels: 14 us -> 14.4 us  [the longest x1 9.76 us: tile_pairs(): pl.pallas_call(tile_kernel, grid=(count // 2,), out_shape=jax.ShapeDtypeS...]
  transfers between devices with their start and end apart: 14 -> 8, of which waited for: 12 -> 4; matrix products, arithmetic and copies ran while one was open for 1% -> 0% of each run, Pallas kernels for 7% -> 9%
where the time goes in v3:
time: 89 us; the launch traced here: 88.5 us
  blocking collectives  36 us (40%)
  starting transfers between devices  22.9 us (26%)
  Pallas kernels  20.8 us (23%)
  waiting for transfers between devices  8.79 us (10%)
    all_to_all x1, blocking collectives, shards(): spread = lax.all_to_all(dense, ZH, 0, 0)  13.2 us
    all_to_all x1, blocking collectives, shards(): terms = lax.all_to_all(pieces, LCX, 0, 0)  12.6 us
    all_to_all x1, starting transfers between devices, shards(): rows = lax.all_to_all(own, ZHL, 0, 0)  12 us
    all_to_all x1, blocking collectives, shards(): parts = lax.all_to_all(owned, LCX, 0, 0)  10.2 us
    pallas_call x1, Pallas kernels, tile_pairs(): pl.pallas_call(tile_kernel, grid=(count // 2,), out_shape=jax.ShapeDtypeS...  9.76 us
    ppermute x6, starting transfers between devices, shift(): return lax.ppermute(values, 'x', [(i, (i + k) % NX) for i in range(NX)])  8.49 us
    pallas_call x1, Pallas kernels, prep(): pl.pallas_call(prep_kernel, grid=(count // 2,), out_shape=(jax.ShapeDtype...  6.35 us
    all_to_all x1, waiting for transfers between devices, shards(): rows = lax.all_to_all(own, ZHL, 0, 0)  4.99 us
  transfers between devices with their start and end apart: 8, of which 4 were waited for; matrix products, arithmetic and copies ran while one was open for 0% of the time, Pallas kernels for 9%

profile of v3, /device:TPU:1, one launch (start us, length us, event | category | flops | bytes accessed | tf_op | source)
XLA Modules:
  0.0 88.5 jit_solution(14430345205986244432)
XLA Ops:
  0.0 1.6 %rows.1 = bf16[32,64,128]{2,1,0:T(8,128)(2,1)} custom-call(bf16[4,1024]{1,0:T(4,128)(2,1)} %occ_ref.1, bf16[4,1024]{1,0:T(4,128)(2,1)} %virt_ref.1), custom_call_target="tpu_custom_call" | custom-call | tf_op jit(solution)/shard_map/rows/pallas_call | solution.py:257
  1.6 12.0 %all-to-all-start = ((bf16[32,64,128]{2,1,0:T(8,128)(2,1)}), bf16[32,64,128]{2,1,0:T(8,128)(2,1)S(1)}, u32[]{:S(2)}, u32[]{:S(2)}) async-start(bf16[32,64,128]{2,1,0:T(8,128)(2,1)} %rows.1), calls=%async_computation | async-start | bytes 1048576 | tf_op jit(solution)/shard_map/all_to_all | solution.py:271
  13.7 1.3 %wants.1.w0.wants_ref = s32[3,8,128]{2,1,0:T(8,128)} custom-call(s32[8]{0:T(128)} %row_ref, s32[8]{0:T(128)} %col_ref.1, s32[8]{0:T(128)} %dest_ref.1, s32[8]{0:T(128)} %aux_ref.1), custom_call_target="tpu_custom_call" | custom-call | tf_op jit(solution)/shard_map/wants/pallas_call | solution.py:257
  15.0 0.0 copy-start
  15.0 2.5 %collective-permute-start.2 = (s32[3,8,128]{2,1,0:T(8,128)}, s32[3,8,128]{2,1,0:T(8,128)S(1)}, u32[]{:S(2)}, u32[]{:S(2)}) collective-permute-start(s32[3,8,128]{2,1,0:T(8,128)} %wants.1.w0.wants_ref), channel_id=1, source_target_pairs={{0,3},{1,0},{2,1},{3,2},{4,7},{5,4},{6,5},{7,6},{8,11},{9,8},{10,9... | collective-permute-start | bytes 36872 | tf_op jit(solution)/shard_map/ppermute | solution.py:26
  17.4 0.5 collective-permute-start.1
  18.0 0.6 collective-permute-start
  18.6 6.3 %prep.1 = (bf16[8,64,4096]{2,1,0:T(8,128)(2,1)}, bf16[4,4096,128]{2,1,0:T(8,128)(2,1)}) custom-call(bf16[8,64,4096]{2,1,0:T(8,128)(2,1)} %t_ref.3), custom_call_target="tpu_custom_call" | custom-call | flops 8999999488 | bytes 12582912 | tf_op jit(solution)/shard_map/prep/pallas_call | solution.py:74
  24.9 0.0 collective-permute-done.2.w3
  24.9 0.0 collective-permute-done.1.w2
  24.9 0.0 collective-permute-done.w1
  24.9 5.0 %all-to-all-done.own_ref = bf16[32,64,128]{2,1,0:T(8,128)(2,1)S(1)} async-done(((bf16[32,64,128]{2,1,0:T(8,128)(2,1)}), bf16[32,64,128]{2,1,0:T(8,128)(2,1)S(1)}, u32[]{:S(2)}, u32[]{:S(2)}) %all-to-all-start) | async-done | bytes 524320 | tf_op jit(solution)/shard_map/all_to_all | solution.py:271
  29.9 2.4 %collective-permute-start.3 = (bf16[32,64,128]{2,1,0:T(8,128)(2,1)S(1)}, bf16[32,64,128]{2,1,0:T(8,128)(2,1)S(1)}, u32[]{:S(2)}, u32[]{:S(2)}) collective-permute-start(bf16[32,64,128]{2,1,0:T(8,128)(2,1)S(1)} %all-to-all-done.own_ref), channel_id=1, source_target_pairs={{0,4},{4,0},{1,5},{5,1},{2,6},{6,2},{3,7},{7,3},{8,12},{12,8},{9,1... | collective-permute-start | bytes 1572872 | tf_op jit(solution)/shard_map/ppermute | solution.py:278
  32.3 1.5 %collective-permute-done.3.other_ref = bf16[32,64,128]{2,1,0:T(8,128)(2,1)S(1)} collective-permute-done((bf16[32,64,128]{2,1,0:T(8,128)(2,1)S(1)}, bf16[32,64,128]{2,1,0:T(8,128)(2,1)S(1)}, u32[]{:S(2)}, u32[]{:S(2)}) %collective-permute-start.3) | collective-permute-done | bytes 524320 | tf_op jit(solution)/shard_map/ppermute | solution.py:278
  33.9 0.0 copy-done
  33.9 0.8 pick.1
  34.7 1.3 %collective-permute-start.4 = (bf16[2,2,4,16,128]{4,3,2,1,0:T(8,128)(2,1)S(1)}, bf16[2,2,4,16,128]{4,3,2,1,0:T(8,128)(2,1)S(1)}, u32[]{:S(2)}, u32[]{:S(2)}) collective-permute-start(bf16[2,2,4,16,128]{4,3,2,1,0:T(8,128)(2,1)S(1)} %get-tuple-element.28), channel_id=1, source_target_pairs={{0,1},{1,2},{2,3},{3,0},{4,5},{5,6},{6,7},{7,4},{8,9},{9,10},{10,1... | collective-permute-start | bytes 196616 | tf_op jit(solution)/shard_map/ppermute | solution.py:26
  35.9 2.5 %collective-permute-start.5 = (bf16[2,2,4,16,128]{4,3,2,1,0:T(8,128)(2,1)S(1)}, bf16[2,2,4,16,128]{4,3,2,1,0:T(8,128)(2,1)S(1)}, u32[]{:S(2)}, u32[]{:S(2)}) collective-permute-start(bf16[2,2,4,16,128]{4,3,2,1,0:T(8,128)(2,1)S(1)} %get-tuple-element.29), channel_id=1, source_target_pairs={{0,2},{1,3},{2,0},{3,1},{4,6},{5,7},{6,4},{7,5},{8,10},{9,11},{10,... | collective-permute-start | bytes 196616 | tf_op jit(solution)/shard_map/ppermute | solution.py:26
  38.4 1.1 %collective-permute-start.6 = (bf16[2,2,4,16,128]{4,3,2,1,0:T(8,128)(2,1)S(1)}, bf16[2,2,4,16,128]{4,3,2,1,0:T(8,128)(2,1)S(1)}, u32[]{:S(2)}, u32[]{:S(2)}) collective-permute-start(bf16[2,2,4,16,128]{4,3,2,1,0:T(8,128)(2,1)S(1)} %get-tuple-element.30), channel_id=1, source_target_pairs={{0,3},{1,0},{2,1},{3,2},{4,7},{5,4},{6,5},{7,6},{8,11},{9,8},{10,9... | collective-permute-start | bytes 196616 | tf_op jit(solution)/shard_map/ppermute | solution.py:26
  39.5 0.0 collective-permute-done.4.g1
  39.6 1.8 %collective-permute-done.5.g2 = bf16[2,2,4,16,128]{4,3,2,1,0:T(8,128)(2,1)S(1)} collective-permute-done((bf16[2,2,4,16,128]{4,3,2,1,0:T(8,128)(2,1)S(1)}, bf16[2,2,4,16,128]{4,3,2,1,0:T(8,128)(2,1)S(1)}, u32[]{:S(2)}, u32[]{:S(2)}) %collective-permute-start.5) | collective-permute-done | bytes 65568 | tf_op jit(solution)/shard_map/ppermute | solution.py:26
  41.4 0.5 collective-permute-done.6.g3
  41.8 9.8 %tile_pairs.1 = f32[16,24,128]{2,1,0:T(8,128)S(1)} custom-call(s32[1]{0:T(128)} %bitcast.me_ref, bf16[8,64,4096]{2,1,0:T(8,128)(2,1)} %t_ref.3, bf16[8,64,4096]{2,1,0:T(8,128)(2,1)} %get-tuple-element.18.sw_ref, bf16[4,4096,128]{2,1,0:T(8,128)(2,1)} %get-tuple-element.21.tr_ref, s32[3,8,128]{2,1,0:T(8,128)S(1)} %copy-done, ...), custom_call_target="tpu_custom_call" | custom-call | tf_op jit(solution)/shard_map/tile_pairs/pallas_call | solution.py:208
  51.6 12.6 %all_to_all.20.t_ref = f32[16,24,128]{2,1,0:T(8,128)S(1)} all-to-all(f32[16,24,128]{2,1,0:T(8,128)S(1)} %tile_pairs.1), channel_id=1, replica_groups=mesh['z'=8,'h'=2,'l'=2,'c'=2,'x'=4] {'l','c','x'}, dimensions={0} | all-to-all | bytes 393216 | tf_op jit(solution)/shard_map/all_to_all | solution.py:283
  64.2 0.2 place.1
  64.4 13.2 %all_to_all.21.s_ref = bf16[16,16,128]{2,1,0:T(8,128)(2,1)S(1)} all-to-all(bf16[16,16,128]{2,1,0:T(8,128)(2,1)S(1)} %place.1), channel_id=1, replica_groups=mesh['z'=8,'h'=2,'l'=2,'c'=2,'x'=4] {'z','h'}, dimensions={0} | all-to-all | bytes 131072 | tf_op jit(solution)/shard_map/all_to_all | solution.py:285
  77.7 10.2 %all_to_all.22.p_ref = f32[16,8,128]{2,1,0:T(8,128)S(1)} all-to-all(f32[16,8,128]{2,1,0:T(8,128)S(1)} %sum.1), channel_id=1, replica_groups=mesh['z'=8,'h'=2,'l'=2,'c'=2,'x'=4] {'l','c','x'}, dimensions={0} | all-to-all | bytes 131072 | tf_op jit(solution)/shard_map/all_to_all | solution.py:287
  87.8 0.7 finish.1
  (1 shorter events, 0.0 us)
Async XLA Ops:
  1.6 28.3 %all-to-all-start = ((bf16[32,64,128]{2,1,0:T(8,128)(2,1)}), bf16[32,64,128]{2,1,0:T(8,128)(2,1)S(1)}, u32[]{:S(2)}, u32[]{:S(2)}) async-start(bf16[32,64,128]{2,1,0:T(8,128)(2,1)} %rows.1), calls=%async_computation | async-start | bytes 1048576 | tf_op jit(solution)/shard_map/all_to_all | solution.py:271
  15.0 18.9 %copy-start = (s32[3,8,128]{2,1,0:T(8,128)S(1)}, s32[3,8,128]{2,1,0:T(8,128)}, u32[]{:S(2)}) copy-start(s32[3,8,128]{2,1,0:T(8,128)} %wants.1.w0.wants_ref) | copy-start | bytes 36868
  15.0 10.0 %collective-permute-start.2 = (s32[3,8,128]{2,1,0:T(8,128)}, s32[3,8,128]{2,1,0:T(8,128)S(1)}, u32[]{:S(2)}, u32[]{:S(2)}) collective-permute-start(s32[3,8,128]{2,1,0:T(8,128)} %wants.1.w0.wants_ref), channel_id=1, source_target_pairs={{0,3},{1,0},{2,1},{3,2},{4,7},{5,4},{6,5},{7,6},{8,11},{9,8},{10,9... | collective-permute-start | bytes 36872 | tf_op jit(solution)/shard_map/ppermute | solution.py:26
  17.4 7.5 %collective-permute-start.1 = (s32[3,8,128]{2,1,0:T(8,128)}, s32[3,8,128]{2,1,0:T(8,128)S(1)}, u32[]{:S(2)}, u32[]{:S(2)}) collective-permute-start(s32[3,8,128]{2,1,0:T(8,128)} %wants.1.w0.wants_ref), channel_id=1, source_target_pairs={{0,2},{1,3},{2,0},{3,1},{4,6},{5,7},{6,4},{7,5},{8,10},{9,11},{10,... | collective-permute-start | bytes 36872 | tf_op jit(solution)/shard_map/ppermute | solution.py:26
  18.0 7.0 %collective-permute-start = (s32[3,8,128]{2,1,0:T(8,128)}, s32[3,8,128]{2,1,0:T(8,128)S(1)}, u32[]{:S(2)}, u32[]{:S(2)}) collective-permute-start(s32[3,8,128]{2,1,0:T(8,128)} %wants.1.w0.wants_ref), channel_id=1, source_target_pairs={{0,1},{1,2},{2,3},{3,0},{4,5},{5,6},{6,7},{7,4},{8,9},{9,10},{10,1... | collective-permute-start | bytes 36872 | tf_op jit(solution)/shard_map/ppermute | solution.py:26
  29.9 3.9 %collective-permute-start.3 = (bf16[32,64,128]{2,1,0:T(8,128)(2,1)S(1)}, bf16[32,64,128]{2,1,0:T(8,128)(2,1)S(1)}, u32[]{:S(2)}, u32[]{:S(2)}) collective-permute-start(bf16[32,64,128]{2,1,0:T(8,128)(2,1)S(1)} %all-to-all-done.own_ref), channel_id=1, source_target_pairs={{0,4},{4,0},{1,5},{5,1},{2,6},{6,2},{3,7},{7,3},{8,12},{12,8},{9,1... | collective-permute-start | bytes 1572872 | tf_op jit(solution)/shard_map/ppermute | solution.py:278
  34.7 4.9 %collective-permute-start.4 = (bf16[2,2,4,16,128]{4,3,2,1,0:T(8,128)(2,1)S(1)}, bf16[2,2,4,16,128]{4,3,2,1,0:T(8,128)(2,1)S(1)}, u32[]{:S(2)}, u32[]{:S(2)}) collective-permute-start(bf16[2,2,4,16,128]{4,3,2,1,0:T(8,128)(2,1)S(1)} %get-tuple-element.28), channel_id=1, source_target_pairs={{0,1},{1,2},{2,3},{3,0},{4,5},{5,6},{6,7},{7,4},{8,9},{9,10},{10,1... | collective-permute-start | bytes 196616 | tf_op jit(solution)/shard_map/ppermute | solution.py:26
  35.9 5.4 %collective-permute-start.5 = (bf16[2,2,4,16,128]{4,3,2,1,0:T(8,128)(2,1)S(1)}, bf16[2,2,4,16,128]{4,3,2,1,0:T(8,128)(2,1)S(1)}, u32[]{:S(2)}, u32[]{:S(2)}) collective-permute-start(bf16[2,2,4,16,128]{4,3,2,1,0:T(8,128)(2,1)S(1)} %get-tuple-element.29), channel_id=1, source_target_pairs={{0,2},{1,3},{2,0},{3,1},{4,6},{5,7},{6,4},{7,5},{8,10},{9,11},{10,... | collective-permute-start | bytes 196616 | tf_op jit(solution)/shard_map/ppermute | solution.py:26
  38.4 3.4 %collective-permute-start.6 = (bf16[2,2,4,16,128]{4,3,2,1,0:T(8,128)(2,1)S(1)}, bf16[2,2,4,16,128]{4,3,2,1,0:T(8,128)(2,1)S(1)}, u32[]{:S(2)}, u32[]{:S(2)}) collective-permute-start(bf16[2,2,4,16,128]{4,3,2,1,0:T(8,128)(2,1)S(1)} %get-tuple-element.30), channel_id=1, source_target_pairs={{0,3},{1,0},{2,1},{3,2},{4,7},{5,4},{6,5},{7,6},{8,11},{9,8},{10,9... | collective-permute-start | bytes 196616 | tf_op jit(solution)/shard_map/ppermute | solution.py:26

commit v4 on v3

--- a/solution.py
+++ b/solution.py
@@ -8,13 +8,12 @@
 BS = 64
 NA = 16
 AUX = 2
-ZH = ("z", "h")
 ZHL = ("z", "h", "l")
-LCX = ("l", "c", "x")
+CX = ("c", "x")
 TENS = ("z", "h", "l", "c")
 ALL = ("z", "h", "l", "c", "x")
 NX = 4
-NG = 16
+NG = 8
 F32, BF16 = jnp.float32, jnp.bfloat16
 VMEM = pl.BlockSpec(memory_space=pltpu.VMEM)
 SMEM = pl.BlockSpec(memory_space=pltpu.SMEM)
@@ -30,7 +29,14 @@
     return lax.broadcasted_iota(jnp.int32, (rows, 128), 1) < BS
 
 
-def rows_kernel(occ_ref, virt_ref, o_ref, scr):
+def rows_kernel(row_ref, col_ref, dest_ref, aux_ref, occ_ref, virt_ref, o_ref, wants_ref, scr):
+    at = lax.broadcasted_iota(jnp.int32, (8, 128), 0)
+    for j in range(3):
+        found = jnp.zeros((8, 128), jnp.int32)
+        for t in range(8):
+            value = row_ref[t] if j == 0 else col_ref[t] if j == 1 else dest_ref[t] * AUX + aux_ref[t]
+            found = jnp.where(at == t, value, found)
+        wants_ref[j] = found
     for arr, ref in enumerate((occ_ref, virt_ref)):
         values = ref[...].astype(F32)
         for i in range(4):
@@ -42,24 +48,13 @@
         o_ref[peer] = block
 
 
-def wants_kernel(row_ref, col_ref, dest_ref, aux_ref, o_ref):
-    at = lax.broadcasted_iota(jnp.int32, (8, 128), 0)
-    for j in range(3):
-        found = jnp.zeros((8, 128), jnp.int32)
-        for t in range(8):
-            value = row_ref[t] if j == 0 else col_ref[t] if j == 1 else dest_ref[t] * AUX + aux_ref[t]
-            found = jnp.where(at == t, value, found)
-        o_ref[j] = found
-
-
-def prep_kernel(t_ref, sw_ref, tr_ref, scr):
+def prep_kernel(t_ref, sw_ref, scr):
     for s in range(16):
         cut = slice(s * 256, s * 256 + 256)
         turned = jnp.concatenate([t_ref[0, :, cut], t_ref[1, :, cut]], axis=0).T
         for k in range(4):
             at = (4 * s + k) * PITCH
             scr[at:at + BS, :] = turned[k * BS:k * BS + BS].astype(F32)
-        tr_ref[0, cut, :] = turned.astype(BF16)
     for s in range(16):
         cut = slice(s * 256, s * 256 + 256)
         rows = jnp.concatenate([scr[pl.ds(4 * s + k, BS, stride=PITCH), :] for k in range(4)], axis=0)
@@ -74,14 +69,11 @@
     return pl.pallas_call(
         prep_kernel,
         grid=(count // 2,),
-        out_shape=(
-            jax.ShapeDtypeStruct(tiles.shape, BF16),
-            jax.ShapeDtypeStruct((count // 2, BS * BS, 128), BF16),
-        ),
+        out_shape=jax.ShapeDtypeStruct(tiles.shape, BF16),
         in_specs=[spec],
-        out_specs=(spec, pl.BlockSpec((1, BS * BS, 128), lambda i: (i, 0, 0))),
+        out_specs=spec,
         scratch_shapes=[pltpu.VMEM((BS * PITCH, 128), F32)],
-        cost_estimate=pl.CostEstimate(flops=9_000_000_000, bytes_accessed=6 * tiles.size, transcendentals=0),
+        cost_estimate=pl.CostEstimate(flops=9_000_000_000, bytes_accessed=4 * tiles.size, transcendentals=0),
         compiler_params=pltpu.CompilerParams(vmem_limit_bytes=LARGE),
         name="prep",
     )(tiles)
@@ -125,7 +117,7 @@
                         o_ref[l, side, ih * 2 + il] = jnp.concatenate([f[cut] for f in found], axis=0).astype(BF16)
 
 
-def tile_kernel(me_ref, t_ref, sw_ref, tr_ref, wants_ref, g0, g1, g2, g3, o_ref, gscr, us, ws, ys, zs, pk):
+def tile_kernel(me_ref, t_ref, sw_ref, wants_ref, g0, g1, g2, g3, o_ref, gscr, us, ws, ys, zs, pk):
     step = pl.program_id(0)
 
     @pl.when(step == 0)
@@ -161,8 +153,9 @@
     low128 = low_lanes(128)
     zero = jnp.zeros((128, 128), BF16)
     for s in range(16):
-        a = tr_ref[0, s * 256:s * 256 + 128, :]
-        b = tr_ref[0, s * 256 + 128:s * 256 + 256, :]
+        cut = slice(s * 256, s * 256 + 256)
+        turned = jnp.concatenate([t_ref[0, :, cut], t_ref[1, :, cut]], axis=0).T
+        a, b = turned[:128], turned[128:]
         rhs = jnp.concatenate([
             jnp.concatenate([jnp.where(low128, a, zero), jnp.where(low128, b, zero)], axis=1),
             jnp.concatenate([jnp.where(low128, zero, a), jnp.where(low128, zero, b)], axis=1),
@@ -197,56 +190,59 @@
     def _():
         target = wants_ref[2].astype(F32)
         for peer in range(NG):
-            for half in range(2):
-                o_ref[peer, half * 8:half * 8 + 8] = pk[pl.ds(2 * peer + half, 8, stride=40), :]
-            o_ref[peer, 16:24] = target
-
-
-def tile_pairs(me, tiles, swapped, turned, wants, got):
+            for r in range(4):
+                o_ref[peer, r * 8:r * 8 + 8] = pk[pl.ds(4 * peer + r, 8, stride=40), :]
+            o_ref[peer, 32:40] = target
+
+
+def tile_pairs(me, tiles, swapped, wants, got):
     count = tiles.shape[0]
     tile = pl.BlockSpec((2, BS, BS * BS), lambda i: (i, 0, 0))
     return pl.pallas_call(
         tile_kernel,
         grid=(count // 2,),
-        out_shape=jax.ShapeDtypeStruct((NG, 3 * count, 128), F32),
-        in_specs=[SMEM, tile, tile, pl.BlockSpec((1, BS * BS, 128), lambda i: (i, 0, 0))] + [VMEM] * 5,
-        out_specs=pl.BlockSpec((NG, 3 * count, 128), lambda i: (0, 0, 0)),
+        out_shape=jax.ShapeDtypeStruct((NG, 5 * count, 128), F32),
+        in_specs=[SMEM, tile, tile] + [VMEM] * 5,
+        out_specs=pl.BlockSpec((NG, 5 * count, 128), lambda i: (0, 0, 0)),
         scratch_shapes=[
             pltpu.VMEM((BS * 24, 128), F32), pltpu.VMEM((BS * PITCH, 128), F32), pltpu.VMEM((BS * PITCH, 128), F32),
             pltpu.VMEM((128, BS * BS), BF16), pltpu.VMEM((128, BS * BS), BF16), pltpu.VMEM((count * 40, 128), F32),
         ],
         compiler_params=pltpu.CompilerParams(vmem_limit_bytes=MIDDLE),
         name="tile_pairs",
-    )(me, tiles, swapped, turned, wants, *got)
+    )(me, tiles, swapped, wants, *got)
 
 
 def place_kernel(t_ref, o_ref):
-    target = t_ref[:, 16:24, :].reshape(128, 128).astype(jnp.int32)
+    target = t_ref[:, 32:40, :].reshape(64, 128)
+    target = jnp.concatenate([target, target], axis=0).T.astype(jnp.int32)
     lane = lax.broadcasted_iota(jnp.int32, (128, 128), 1)
-    hot = jnp.where(lane == target, 1.0, 0.0).T.astype(BF16)
-    dense = []
-    for half in range(2):
-        terms = t_ref[:, half * 8:half * 8 + 8, :].reshape(128, 128)
-        high = terms.astype(BF16)
-        rest = (terms - high.astype(F32)).astype(BF16)
-        dense.append(jnp.dot(hot, high, preferred_element_type=F32) + jnp.dot(hot, rest, preferred_element_type=F32))
-    for peer in range(NG):
-        o_ref[peer] = jnp.concatenate([d[peer * 8:peer * 8 + 8] for d in dense], axis=0).astype(BF16)
+    terms = jnp.concatenate([t_ref[:, r * 8:r * 8 + 8, :].reshape(64, 128) for r in range(4)], axis=0)
+    high = terms.astype(BF16)
+    rest = (terms - high.astype(F32)).astype(BF16)
+    for part in range(4):
+        row = lax.broadcasted_iota(jnp.int32, (128, 128), 0) + part * 128
+        here = ((row >> 4) == (target >> 2)) & ((row & 3) == (target & 3))
+        hot = jnp.concatenate([
+            jnp.where(here & (((row >> 2) & 3) == (lane >> 6) + 2 * half), 1.0, 0.0).astype(BF16) for half in range(2)
+        ], axis=1)
+        dense = jnp.dot(hot, high, preferred_element_type=F32) + jnp.dot(hot, rest, preferred_element_type=F32)
+        o_ref[part * 8:part * 8 + 8] = dense.astype(BF16).reshape(8, 16, 128)
 
 
 def sum_kernel(s_ref, o_ref):
     total = jnp.sum(s_ref[...].astype(F32), axis=0)
-    none = jnp.zeros((4, 128), F32)
-    for peer in range(NG):
-        at = (peer // 4) * 2
-        rows = [total[half * 8 + at + aux:half * 8 + at + aux + 1] for aux in range(AUX) for half in range(2)]
-        o_ref[peer] = jnp.concatenate(rows + [none], axis=0)
+    for core in range(2):
+        at = [r * 4 + core * 2 + aux for aux in range(AUX) for r in range(4)]
+        rows = jnp.concatenate([total[i:i + 1] for i in at], axis=0)
+        for x in range(NX):
+            o_ref[core * NX + x] = rows
 
 
 def finish_kernel(p_ref, o_ref, whole):
     for aux in range(AUX):
         for peer in range(NG):
-            whole[aux, 2 * peer:2 * peer + 2, :] = p_ref[peer, 2 * aux:2 * aux + 2, :]
+            whole[aux, 4 * peer:4 * peer + 4, :] = p_ref[peer, 4 * aux:4 * aux + 4, :]
     one, two = whole[0], whole[1]
     low = low_lanes(32)
     o_ref[:32, :] = jnp.where(low, one, pltpu.roll(two, BS, 1))
@@ -266,25 +262,23 @@
 
 def shards(tiles, tile_dest, tile_aux, tile_row, tile_col, green_occ, green_virt):
     me = lax.axis_index("x").reshape(1)
-    own = call(rows_kernel, "rows", ((32, BS, 128), BF16), green_occ, green_virt, limit=LARGE,
-               out_specs=VMEM, scratch_shapes=[pltpu.VMEM((BS, 128), F32)])
+    own, wants = call(rows_kernel, "rows", [((32, BS, 128), BF16), ((3, 8, 128), jnp.int32)],
+                      tile_row, tile_col, tile_dest, tile_aux, green_occ, green_virt,
+                      spaces=[SMEM] * 4 + [VMEM] * 2, limit=LARGE, out_specs=[VMEM] * 2, scratch_shapes=[pltpu.VMEM((BS, 128), F32)])
     rows = lax.all_to_all(own, ZHL, 0, 0)
-    tile_row, own = lax.optimization_barrier((tile_row, own))
-    wants = call(wants_kernel, "wants", ((3, 8, 128), jnp.int32), tile_row, tile_col, tile_dest, tile_aux,
-                 spaces=[SMEM] * 4, limit=LARGE, out_specs=VMEM)
     asked = [wants] + [shift(wants, k) for k in range(1, NX)]
-    swapped, turned = prep(tiles)
-    rows, turned, asked = lax.optimization_barrier((rows, turned, asked))
+    swapped = prep(tiles)
+    rows, swapped, asked = lax.optimization_barrier((rows, swapped, asked))
     other = lax.ppermute(rows, "c", [(0, 1), (1, 0)])
     picked = call(pick_kernel, "pick", [((2, 2, 4, 16, 128), BF16)] * NX, lax.axis_index("c").reshape(1), *asked, rows, other,
                   spaces=[SMEM] + [VMEM] * 6, out_specs=[VMEM] * NX)
     got = [picked[0]] + [shift(picked[NX - k], k) for k in range(1, NX)]
-    pieces = tile_pairs(me, tiles, swapped, turned, wants, got)
-    terms = lax.all_to_all(pieces, LCX, 0, 0)
-    dense = call(place_kernel, "place", ((NG, 16, 128), BF16), terms, out_specs=VMEM)
-    spread = lax.all_to_all(dense, ZH, 0, 0)
+    pieces = tile_pairs(me, tiles, swapped, wants, got)
+    terms = lax.all_to_all(pieces, CX, 0, 0)
+    dense = call(place_kernel, "place", ((32, 16, 128), BF16), terms, out_specs=VMEM)
+    spread = lax.all_to_all(dense, ZHL, 0, 0)
     owned = call(sum_kernel, "sum", ((NG, 8, 128), F32), spread, out_specs=VMEM)
-    parts = lax.all_to_all(owned, LCX, 0, 0)
+    parts = lax.all_to_all(owned, CX, 0, 0)
     out = call(finish_kernel, "finish", ((BS, AUX * BS), F32), parts,
                out_specs=pl.BlockSpec((BS, AUX * BS), lambda: (0, 0)),
                scratch_shapes=[pltpu.VMEM((AUX, 32, 128), F32)])

time: 89 us -> 87.1 us (0.979)
  Pallas kernels: 20.8 us -> 19 us
  blocking collectives: 36 us -> 34.2 us
  waiting for transfers between devices: 8.79 us -> 10.5 us
    all_to_all x3, blocking collectives: 36 us -> 34.2 us  [the longest x1 13.6 us: shards(): spread = lax.all_to_all(dense, ZHL, 0, 0)]
    all_to_all x1, waiting for transfers between devices: 4.99 us -> 6.69 us  [shards(): rows = lax.all_to_all(own, ZHL, 0, 0)]
    pallas_call x6 -> x5, Pallas kernels: 4.68 us -> 3.54 us  [call(): pl.pallas_call(kernel, out_shape=[jax.ShapeDtypeStruct(*s) for s in out]...]
  transfers between devices with their start and end apart: 8 -> 8, of which waited for: 4 -> 4; matrix products, arithmetic and copies ran while one was open for 0% -> 0% of each run, Pallas kernels for 9% -> 7%
where the time goes in v4:
time: 87.1 us; the launch traced here: 86.7 us
  blocking collectives  34.2 us (39%)
  starting transfers between devices  23 us (26%)
  Pallas kernels  19 us (22%)
  waiting for transfers between devices  10.5 us (12%)
    all_to_all x1, blocking collectives, shards(): spread = lax.all_to_all(dense, ZHL, 0, 0)  13.6 us
    all_to_all x1, starting transfers between devices, shards(): rows = lax.all_to_all(own, ZHL, 0, 0)  12 us
    all_to_all x1, blocking collectives, shards(): terms = lax.all_to_all(pieces, CX, 0, 0)  11 us
    all_to_all x1, blocking collectives, shards(): parts = lax.all_to_all(owned, CX, 0, 0)  9.61 us
    pallas_call x1, Pallas kernels, tile_pairs(): pl.pallas_call(tile_kernel, grid=(count // 2,), out_shape=jax.ShapeDtypeS...  9.56 us
    ppermute x6, starting transfers between devices, shift(): return lax.ppermute(values, 'x', [(i, (i + k) % NX) for i in range(NX)])  8.57 us
    all_to_all x1, waiting for transfers between devices, shards(): rows = lax.all_to_all(own, ZHL, 0, 0)  6.69 us
    pallas_call x1, Pallas kernels, prep(): pl.pallas_call(prep_kernel, grid=(count // 2,), out_shape=jax.ShapeDtypeS...  5.88 us
  transfers between devices with their start and end apart: 8, of which 4 were waited for; matrix products, arithmetic and copies ran while one was open for 0% of the time, Pallas kernels for 7%

profile of v4, /device:TPU:1, one launch (start us, length us, event | category | flops | bytes accessed | tf_op | source)
XLA Modules:
  0.0 86.7 jit_solution(12946192060193663977)
XLA Ops:
  0.0 1.6 %rows.1 = (bf16[32,64,128]{2,1,0:T(8,128)(2,1)}, s32[3,8,128]{2,1,0:T(8,128)}) custom-call(s32[8]{0:T(128)} %row_ref.1, s32[8]{0:T(128)} %col_ref.1, s32[8]{0:T(128)} %dest_ref.1, s32[8]{0:T(128)} %aux_ref.1, bf16[4,1024]{1,0:T(4,128)(2,1)} %occ_ref.1, bf16[4,1024]{1,0:T(4,128)(2,1)} %virt_ref.1), custom_call_target="tpu_custom_call" | custom-call | tf_op jit(solution)/shard_map/rows/pallas_call | solution.py:253
  1.6 12.0 %all-to-all-start = ((bf16[32,64,128]{2,1,0:T(8,128)(2,1)}), bf16[32,64,128]{2,1,0:T(8,128)(2,1)S(1)}, u32[]{:S(2)}, u32[]{:S(2)}) async-start(bf16[32,64,128]{2,1,0:T(8,128)(2,1)} %get-tuple-element.17), calls=%async_computation | async-start | bytes 1048576 | tf_op jit(solution)/shard_map/all_to_all | solution.py:268
  13.7 0.0 copy-start
  13.7 2.6 %collective-permute-start.2 = (s32[3,8,128]{2,1,0:T(8,128)}, s32[3,8,128]{2,1,0:T(8,128)S(1)}, u32[]{:S(2)}, u32[]{:S(2)}) collective-permute-start(s32[3,8,128]{2,1,0:T(8,128)} %get-tuple-element.20.w0.wants_ref), channel_id=1, source_target_pairs={{0,3},{1,0},{2,1},{3,2},{4,7},{5,4},{6,5},{7,6},{8,11},{9,8},{10,9... | collective-permute-start | bytes 36872 | tf_op jit(solution)/shard_map/ppermute | solution.py:25
  16.2 0.5 collective-permute-start.1
  16.7 0.6 collective-permute-start
  17.4 5.9 %prep.1.sw_ref = bf16[8,64,4096]{2,1,0:T(8,128)(2,1)} custom-call(bf16[8,64,4096]{2,1,0:T(8,128)(2,1)} %t_ref.3), custom_call_target="tpu_custom_call" | custom-call | flops 8999999488 | bytes 8388608 | tf_op jit(solution)/shard_map/prep/pallas_call | solution.py:69
  23.2 0.0 collective-permute-done.2.w3
  23.2 0.0 collective-permute-done.1.w2
  23.2 0.0 collective-permute-done.w1
  23.2 6.7 %all-to-all-done.own_ref = bf16[32,64,128]{2,1,0:T(8,128)(2,1)S(1)} async-done(((bf16[32,64,128]{2,1,0:T(8,128)(2,1)}), bf16[32,64,128]{2,1,0:T(8,128)(2,1)S(1)}, u32[]{:S(2)}, u32[]{:S(2)}) %all-to-all-start) | async-done | bytes 524320 | tf_op jit(solution)/shard_map/all_to_all | solution.py:268
  29.9 2.4 %collective-permute-start.3 = (bf16[32,64,128]{2,1,0:T(8,128)(2,1)S(1)}, bf16[32,64,128]{2,1,0:T(8,128)(2,1)S(1)}, u32[]{:S(2)}, u32[]{:S(2)}) collective-permute-start(bf16[32,64,128]{2,1,0:T(8,128)(2,1)S(1)} %all-to-all-done.own_ref), channel_id=1, source_target_pairs={{0,4},{4,0},{1,5},{5,1},{2,6},{6,2},{3,7},{7,3},{8,12},{12,8},{9,1... | collective-permute-start | bytes 1572872 | tf_op jit(solution)/shard_map/ppermute | solution.py:272
  32.3 1.5 %collective-permute-done.3.other_ref = bf16[32,64,128]{2,1,0:T(8,128)(2,1)S(1)} collective-permute-done((bf16[32,64,128]{2,1,0:T(8,128)(2,1)S(1)}, bf16[32,64,128]{2,1,0:T(8,128)(2,1)S(1)}, u32[]{:S(2)}, u32[]{:S(2)}) %collective-permute-start.3) | collective-permute-done | bytes 524320 | tf_op jit(solution)/shard_map/ppermute | solution.py:272
  33.9 0.0 copy-done
  33.9 0.8 pick.1
  34.7 1.3 %collective-permute-start.4 = (bf16[2,2,4,16,128]{4,3,2,1,0:T(8,128)(2,1)S(1)}, bf16[2,2,4,16,128]{4,3,2,1,0:T(8,128)(2,1)S(1)}, u32[]{:S(2)}, u32[]{:S(2)}) collective-permute-start(bf16[2,2,4,16,128]{4,3,2,1,0:T(8,128)(2,1)S(1)} %get-tuple-element.26), channel_id=1, source_target_pairs={{0,1},{1,2},{2,3},{3,0},{4,5},{5,6},{6,7},{7,4},{8,9},{9,10},{10,1... | collective-permute-start | bytes 196616 | tf_op jit(solution)/shard_map/ppermute | solution.py:25
  35.9 2.4 %collective-permute-start.5 = (bf16[2,2,4,16,128]{4,3,2,1,0:T(8,128)(2,1)S(1)}, bf16[2,2,4,16,128]{4,3,2,1,0:T(8,128)(2,1)S(1)}, u32[]{:S(2)}, u32[]{:S(2)}) collective-permute-start(bf16[2,2,4,16,128]{4,3,2,1,0:T(8,128)(2,1)S(1)} %get-tuple-element.27), channel_id=1, source_target_pairs={{0,2},{1,3},{2,0},{3,1},{4,6},{5,7},{6,4},{7,5},{8,10},{9,11},{10,... | collective-permute-start | bytes 196616 | tf_op jit(solution)/shard_map/ppermute | solution.py:25
  38.4 1.1 %collective-permute-start.6 = (bf16[2,2,4,16,128]{4,3,2,1,0:T(8,128)(2,1)S(1)}, bf16[2,2,4,16,128]{4,3,2,1,0:T(8,128)(2,1)S(1)}, u32[]{:S(2)}, u32[]{:S(2)}) collective-permute-start(bf16[2,2,4,16,128]{4,3,2,1,0:T(8,128)(2,1)S(1)} %get-tuple-element.28), channel_id=1, source_target_pairs={{0,3},{1,0},{2,1},{3,2},{4,7},{5,4},{6,5},{7,6},{8,11},{9,8},{10,9... | collective-permute-start | bytes 196616 | tf_op jit(solution)/shard_map/ppermute | solution.py:25
  39.5 0.0 collective-permute-done.4.g1
  39.6 1.8 %collective-permute-done.5.g2 = bf16[2,2,4,16,128]{4,3,2,1,0:T(8,128)(2,1)S(1)} collective-permute-done((bf16[2,2,4,16,128]{4,3,2,1,0:T(8,128)(2,1)S(1)}, bf16[2,2,4,16,128]{4,3,2,1,0:T(8,128)(2,1)S(1)}, u32[]{:S(2)}, u32[]{:S(2)}) %collective-permute-start.5) | collective-permute-done | bytes 65568 | tf_op jit(solution)/shard_map/ppermute | solution.py:25
  41.3 0.5 collective-permute-done.6.g3
  41.8 9.6 %tile_pairs.1 = f32[8,40,128]{2,1,0:T(8,128)S(1)} custom-call(s32[1]{0:T(128)} %bitcast.me_ref, bf16[8,64,4096]{2,1,0:T(8,128)(2,1)} %t_ref.3, bf16[8,64,4096]{2,1,0:T(8,128)(2,1)} %prep.1.sw_ref, s32[3,8,128]{2,1,0:T(8,128)S(1)} %copy-done, bf16[2,2,4,16,128]{4,3,2,1,0:T(8,128)(2,1)S(1)} %get-tuple-element.25.g0, ...), custom_call_target="tpu_custom_call" | custom-call | tf_op jit(solution)/shard_map/tile_pairs/pallas_call | solution.py:201
  51.4 11.0 %all_to_all.20.t_ref = f32[8,40,128]{2,1,0:T(8,128)S(1)} all-to-all(f32[8,40,128]{2,1,0:T(8,128)S(1)} %tile_pairs.1), channel_id=1, replica_groups=mesh['z'=8,'h'=2,'l'=2,'c'=2,'x'=4] {'c','x'}, dimensions={0} | all-to-all | bytes 327680 | tf_op jit(solution)/shard_map/all_to_all | solution.py:277
  62.4 0.4 place.1
  62.8 13.6 %all_to_all.21.s_ref = bf16[32,16,128]{2,1,0:T(8,128)(2,1)S(1)} all-to-all(bf16[32,16,128]{2,1,0:T(8,128)(2,1)S(1)} %place.1), channel_id=1, replica_groups=mesh['z'=8,'h'=2,'l'=2,'c'=2,'x'=4] {'z','h','l'}, dimensions={0} | all-to-all | bytes 262144 | tf_op jit(solution)/shard_map/all_to_all | solution.py:279
  76.4 9.6 %all_to_all.22.p_ref = f32[8,8,128]{2,1,0:T(8,128)S(1)} all-to-all(f32[8,8,128]{2,1,0:T(8,128)S(1)} %sum.1), channel_id=1, replica_groups=mesh['z'=8,'h'=2,'l'=2,'c'=2,'x'=4] {'c','x'}, dimensions={0} | all-to-all | bytes 65536 | tf_op jit(solution)/shard_map/all_to_all | solution.py:281
  86.0 0.7 finish.1
  (1 shorter events, 0.0 us)
Async XLA Ops:
  1.6 28.3 %all-to-all-start = ((bf16[32,64,128]{2,1,0:T(8,128)(2,1)}), bf16[32,64,128]{2,1,0:T(8,128)(2,1)S(1)}, u32[]{:S(2)}, u32[]{:S(2)}) async-start(bf16[32,64,128]{2,1,0:T(8,128)(2,1)} %get-tuple-element.17), calls=%async_computation | async-start | bytes 1048576 | tf_op jit(solution)/shard_map/all_to_all | solution.py:268
  13.7 20.2 %copy-start = (s32[3,8,128]{2,1,0:T(8,128)S(1)}, s32[3,8,128]{2,1,0:T(8,128)}, u32[]{:S(2)}) copy-start(s32[3,8,128]{2,1,0:T(8,128)} %get-tuple-element.20.w0.wants_ref) | copy-start | bytes 36868
  13.7 9.6 %collective-permute-start.2 = (s32[3,8,128]{2,1,0:T(8,128)}, s32[3,8,128]{2,1,0:T(8,128)S(1)}, u32[]{:S(2)}, u32[]{:S(2)}) collective-permute-start(s32[3,8,128]{2,1,0:T(8,128)} %get-tuple-element.20.w0.wants_ref), channel_id=1, source_target_pairs={{0,3},{1,0},{2,1},{3,2},{4,7},{5,4},{6,5},{7,6},{8,11},{9,8},{10,9... | collective-permute-start | bytes 36872 | tf_op jit(solution)/shard_map/ppermute | solution.py:25
  16.2 7.0 %collective-permute-start.1 = (s32[3,8,128]{2,1,0:T(8,128)}, s32[3,8,128]{2,1,0:T(8,128)S(1)}, u32[]{:S(2)}, u32[]{:S(2)}) collective-permute-start(s32[3,8,128]{2,1,0:T(8,128)} %get-tuple-element.20.w0.wants_ref), channel_id=1, source_target_pairs={{0,2},{1,3},{2,0},{3,1},{4,6},{5,7},{6,4},{7,5},{8,10},{9,11},{10,... | collective-permute-start | bytes 36872 | tf_op jit(solution)/shard_map/ppermute | solution.py:25
  16.7 6.5 %collective-permute-start = (s32[3,8,128]{2,1,0:T(8,128)}, s32[3,8,128]{2,1,0:T(8,128)S(1)}, u32[]{:S(2)}, u32[]{:S(2)}) collective-permute-start(s32[3,8,128]{2,1,0:T(8,128)} %get-tuple-element.20.w0.wants_ref), channel_id=1, source_target_pairs={{0,1},{1,2},{2,3},{3,0},{4,5},{5,6},{6,7},{7,4},{8,9},{9,10},{10,1... | collective-permute-start | bytes 36872 | tf_op jit(solution)/shard_map/ppermute | solution.py:25
  29.9 3.9 %collective-permute-start.3 = (bf16[32,64,128]{2,1,0:T(8,128)(2,1)S(1)}, bf16[32,64,128]{2,1,0:T(8,128)(2,1)S(1)}, u32[]{:S(2)}, u32[]{:S(2)}) collective-permute-start(bf16[32,64,128]{2,1,0:T(8,128)(2,1)S(1)} %all-to-all-done.own_ref), channel_id=1, source_target_pairs={{0,4},{4,0},{1,5},{5,1},{2,6},{6,2},{3,7},{7,3},{8,12},{12,8},{9,1... | collective-permute-start | bytes 1572872 | tf_op jit(solution)/shard_map/ppermute | solution.py:272
  34.7 4.9 %collective-permute-start.4 = (bf16[2,2,4,16,128]{4,3,2,1,0:T(8,128)(2,1)S(1)}, bf16[2,2,4,16,128]{4,3,2,1,0:T(8,128)(2,1)S(1)}, u32[]{:S(2)}, u32[]{:S(2)}) collective-permute-start(bf16[2,2,4,16,128]{4,3,2,1,0:T(8,128)(2,1)S(1)} %get-tuple-element.26), channel_id=1, source_target_pairs={{0,1},{1,2},{2,3},{3,0},{4,5},{5,6},{6,7},{7,4},{8,9},{9,10},{10,1... | collective-permute-start | bytes 196616 | tf_op jit(solution)/shard_map/ppermute | solution.py:25
  35.9 5.4 %collective-permute-start.5 = (bf16[2,2,4,16,128]{4,3,2,1,0:T(8,128)(2,1)S(1)}, bf16[2,2,4,16,128]{4,3,2,1,0:T(8,128)(2,1)S(1)}, u32[]{:S(2)}, u32[]{:S(2)}) collective-permute-start(bf16[2,2,4,16,128]{4,3,2,1,0:T(8,128)(2,1)S(1)} %get-tuple-element.27), channel_id=1, source_target_pairs={{0,2},{1,3},{2,0},{3,1},{4,6},{5,7},{6,4},{7,5},{8,10},{9,11},{10,... | collective-permute-start | bytes 196616 | tf_op jit(solution)/shard_map/ppermute | solution.py:25
  38.4 3.4 %collective-permute-start.6 = (bf16[2,2,4,16,128]{4,3,2,1,0:T(8,128)(2,1)S(1)}, bf16[2,2,4,16,128]{4,3,2,1,0:T(8,128)(2,1)S(1)}, u32[]{:S(2)}, u32[]{:S(2)}) collective-permute-start(bf16[2,2,4,16,128]{4,3,2,1,0:T(8,128)(2,1)S(1)} %get-tuple-element.28), channel_id=1, source_target_pairs={{0,3},{1,0},{2,1},{3,2},{4,7},{5,4},{6,5},{7,6},{8,11},{9,8},{10,9... | collective-permute-start | bytes 196616 | tf_op jit(solution)/shard_map/ppermute | solution.py:25

commit v5 on v4

--- a/solution.py
+++ b/solution.py
@@ -9,10 +9,11 @@
 NA = 16
 AUX = 2
 ZHL = ("z", "h", "l")
+HL = ("h", "l")
 CX = ("c", "x")
 TENS = ("z", "h", "l", "c")
 ALL = ("z", "h", "l", "c", "x")
-NX = 4
+NX = NY = 4
 NG = 8
 F32, BF16 = jnp.float32, jnp.bfloat16
 VMEM = pl.BlockSpec(memory_space=pltpu.VMEM)
@@ -79,8 +80,12 @@
     )(tiles)
 
 
-def pick_kernel(core_ref, w0, w1, w2, w3, own_ref, other_ref, o0, o1, o2, o3):
-    core = core_ref[0]
+def pick_kernel(core_ref, y_ref, w0, w1, w2, w3, *refs):
+    pieces, (o0, o1, o2, o3, rows) = refs[:2 * NY], refs[2 * NY:]
+    for k in range(NY):
+        y = (y_ref[0] - k + NY) & 3
+        rows[core_ref[0], y] = pieces[k][...]
+        rows[1 - core_ref[0], y] = pieces[NY + k][...]
     row, col = (jnp.concatenate([w[j] for w in (w0, w1, w2, w3)], axis=0) for j in range(2))
     lane = lax.broadcasted_iota(jnp.int32, (32, 128), 1)
     low = low_lanes(32)
@@ -97,13 +102,13 @@
                         jnp.where(lane + 128 == key, 1.0, 0.0).astype(BF16),
                     ], axis=1))
         hots.append(jnp.concatenate(hot, axis=0))
-    for side, ref in ((core, own_ref), (1 - core, other_ref)):
+    for side in range(2):
         for l in range(2):
             for ih in range(2):
                 got = []
                 for arr in range(2):
                     start = (arr * 2 + ih) * 16
-                    table = jnp.concatenate([ref[2 * b + l, start:start + 16, :] for b in range(NA)], axis=0)
+                    table = jnp.concatenate([rows[side, 2 * (b % 2) + l, b // 2, start:start + 16, :] for b in range(NA)], axis=0)
                     got.append(jnp.dot(hots[arr], table, preferred_element_type=F32))
                 for il in range(2):
                     found = []
@@ -262,16 +267,20 @@
 
 def shards(tiles, tile_dest, tile_aux, tile_row, tile_col, green_occ, green_virt):
     me = lax.axis_index("x").reshape(1)
-    own, wants = call(rows_kernel, "rows", [((32, BS, 128), BF16), ((3, 8, 128), jnp.int32)],
+    own, wants = call(rows_kernel, "rows", [((8, BS, 128), BF16), ((3, 8, 128), jnp.int32)],
                       tile_row, tile_col, tile_dest, tile_aux, green_occ, green_virt,
                       spaces=[SMEM] * 4 + [VMEM] * 2, limit=LARGE, out_specs=[VMEM] * 2, scratch_shapes=[pltpu.VMEM((BS, 128), F32)])
-    rows = lax.all_to_all(own, ZHL, 0, 0)
+    rows = lax.all_to_all(own, "z", 0, 0)
+    pieces = [rows] + [lax.ppermute(rows, HL, [(i, (i + k) % NY) for i in range(NY)]) for k in range(1, NY)]
     asked = [wants] + [shift(wants, k) for k in range(1, NX)]
     swapped = prep(tiles)
-    rows, swapped, asked = lax.optimization_barrier((rows, swapped, asked))
-    other = lax.ppermute(rows, "c", [(0, 1), (1, 0)])
-    picked = call(pick_kernel, "pick", [((2, 2, 4, 16, 128), BF16)] * NX, lax.axis_index("c").reshape(1), *asked, rows, other,
-                  spaces=[SMEM] + [VMEM] * 6, out_specs=[VMEM] * NX)
+    *others, swapped, asked = lax.optimization_barrier((*pieces[1:], swapped, asked))
+    pieces = pieces[:1] + others
+    pieces += [lax.ppermute(p, "c", [(0, 1), (1, 0)]) for p in pieces]
+    y = lax.axis_index(HL).reshape(1)
+    picked = call(pick_kernel, "pick", [((2, 2, 4, 16, 128), BF16)] * NX, lax.axis_index("c").reshape(1), y, *asked, *pieces,
+                  spaces=[SMEM] * 2 + [VMEM] * (NX + 2 * NY), out_specs=[VMEM] * NX,
+                  scratch_shapes=[pltpu.VMEM((2, NY, 8, BS, 128), BF16)])
     got = [picked[0]] + [shift(picked[NX - k], k) for k in range(1, NX)]
     pieces = tile_pairs(me, tiles, swapped, wants, got)
     terms = lax.all_to_all(pieces, CX, 0, 0)

time: 87.1 us -> 85.3 us (0.979)
  waiting for transfers between devices: 10.5 us -> 7.43 us
  starting transfers between devices: 23 us -> 25.4 us
  blocking collectives: 34.2 us -> 33.2 us
    ppermute x1 -> x7, starting transfers between devices: 2.39 us -> 7.77 us  [the longest x4 3.99 us: shards(): pieces += [lax.ppermute(p, 'c', [(0, 1), (1, 0)]) for p in pieces]]
    all_to_all x1, starting transfers between devices: 12 us -> 9.02 us  [shards(): rows = lax.all_to_all(own, 'z', 0, 0)]
    all_to_all x1, waiting for transfers between devices: 6.69 us -> 4.08 us  [shards(): rows = lax.all_to_all(own, 'z', 0, 0)]
  transfers between devices with their start and end apart: 8 -> 14, of which waited for: 4 -> 7; matrix products, arithmetic and copies ran while one was open for 0% -> 0% of each run, Pallas kernels for 7% -> 7%
where the time goes in v5:
time: 85.3 us; the launch traced here: 84.9 us
  blocking collectives  33.2 us (39%)
  starting transfers between devices  25.4 us (30%)
  Pallas kernels  18.8 us (22%)
  waiting for transfers between devices  7.43 us (9%)
    all_to_all x1, blocking collectives, shards(): spread = lax.all_to_all(dense, ZHL, 0, 0)  12.7 us
    all_to_all x1, blocking collectives, shards(): terms = lax.all_to_all(pieces, CX, 0, 0)  10.9 us
    all_to_all x1, blocking collectives, shards(): parts = lax.all_to_all(owned, CX, 0, 0)  9.61 us
    pallas_call x1, Pallas kernels, tile_pairs(): pl.pallas_call(tile_kernel, grid=(count // 2,), out_shape=jax.ShapeDtypeS...  9.56 us
    all_to_all x1, starting transfers between devices, shards(): rows = lax.all_to_all(own, 'z', 0, 0)  9.02 us
    ppermute x6, starting transfers between devices, shift(): return lax.ppermute(values, 'x', [(i, (i + k) % NX) for i in range(NX)])  8.57 us
    pallas_call x1, Pallas kernels, prep(): pl.pallas_call(prep_kernel, grid=(count // 2,), out_shape=jax.ShapeDtypeS...  5.89 us
    all_to_all x1, waiting for transfers between devices, shards(): rows = lax.all_to_all(own, 'z', 0, 0)  4.08 us
  transfers between devices with their start and end apart: 14, of which 7 were waited for; matrix products, arithmetic and copies ran while one was open for 0% of the time, Pallas kernels for 7%

profile of v5, /device:TPU:1, one launch (start us, length us, event | category | flops | bytes accessed | tf_op | source)
XLA Modules:
  0.0 84.9 jit_solution(5360065843328448549)
XLA Ops:
  0.0 1.4 %rows.1 = (bf16[8,64,128]{2,1,0:T(8,128)(2,1)}, s32[3,8,128]{2,1,0:T(8,128)}) custom-call(s32[8]{0:T(128)} %row_ref.1, s32[8]{0:T(128)} %col_ref.1, s32[8]{0:T(128)} %dest_ref.1, s32[8]{0:T(128)} %aux_ref.1, bf16[4,1024]{1,0:T(4,128)(2,1)} %occ_ref.1, bf16[4,1024]{1,0:T(4,128)(2,1)} %virt_ref.1), custom_call_target="tpu_custom_call" | custom-call | tf_op jit(solution)/shard_map/rows/pallas_call | solution.py:258
  1.4 9.0 %all-to-all-start = ((bf16[8,64,128]{2,1,0:T(8,128)(2,1)}), bf16[8,64,128]{2,1,0:T(8,128)(2,1)S(1)}, u32[]{:S(2)}, u32[]{:S(2)}) async-start(bf16[8,64,128]{2,1,0:T(8,128)(2,1)} %get-tuple-element.19), calls=%async_computation | async-start | bytes 262144 | tf_op jit(solution)/shard_map/all_to_all | solution.py:273
  10.4 0.0 copy-start
  10.4 2.6 %collective-permute-start.5 = (s32[3,8,128]{2,1,0:T(8,128)}, s32[3,8,128]{2,1,0:T(8,128)S(1)}, u32[]{:S(2)}, u32[]{:S(2)}) collective-permute-start(s32[3,8,128]{2,1,0:T(8,128)} %get-tuple-element.22.w0.wants_ref), channel_id=1, source_target_pairs={{0,3},{1,0},{2,1},{3,2},{4,7},{5,4},{6,5},{7,6},{8,11},{9,8},{10,9... | collective-permute-start | bytes 36872 | tf_op jit(solution)/shard_map/ppermute | solution.py:26
  13.0 0.5 collective-permute-start.4
  13.5 0.6 collective-permute-start.3
  14.1 4.1 %all-to-all-done.refs_0_ = bf16[8,64,128]{2,1,0:T(8,128)(2,1)S(1)} async-done(((bf16[8,64,128]{2,1,0:T(8,128)(2,1)}), bf16[8,64,128]{2,1,0:T(8,128)(2,1)S(1)}, u32[]{:S(2)}, u32[]{:S(2)}) %all-to-all-start) | async-done | bytes 131104 | tf_op jit(solution)/shard_map/all_to_all | solution.py:273
  18.2 2.7 %collective-permute-start.2 = (bf16[8,64,128]{2,1,0:T(8,128)(2,1)S(1)}, bf16[8,64,128]{2,1,0:T(8,128)(2,1)S(1)}, u32[]{:S(2)}, u32[]{:S(2)}) collective-permute-start(bf16[8,64,128]{2,1,0:T(8,128)(2,1)S(1)} %all-to-all-done.refs_0_), channel_id=1, source_target_pairs={{0,24},{8,0},{16,8},{24,16},{1,25},{9,1},{17,9},{25,17},{2,26},{10... | collective-permute-start | bytes 393224 | tf_op jit(solution)/shard_map/ppermute | solution.py:274
  20.9 0.3 collective-permute-start.1
  21.3 0.0 collective-permute-done.5.w3
  21.3 0.7 collective-permute-start
  22.0 5.9 %prep.1.sw_ref = bf16[8,64,4096]{2,1,0:T(8,128)(2,1)} custom-call(bf16[8,64,4096]{2,1,0:T(8,128)(2,1)} %t_ref.3), custom_call_target="tpu_custom_call" | custom-call | flops 8999999488 | bytes 8388608 | tf_op jit(solution)/shard_map/prep/pallas_call | solution.py:70
  27.9 0.0 collective-permute-done.4.w2
  27.9 3.1 %collective-permute-start.6 = (bf16[8,64,128]{2,1,0:T(8,128)(2,1)S(1)}, bf16[8,64,128]{2,1,0:T(8,128)(2,1)S(1)}, u32[]{:S(2)}, u32[]{:S(2)}) collective-permute-start(bf16[8,64,128]{2,1,0:T(8,128)(2,1)S(1)} %all-to-all-done.refs_0_), channel_id=1, source_target_pairs={{0,4},{4,0},{1,5},{5,1},{2,6},{6,2},{3,7},{7,3},{8,12},{12,8},{9,1... | collective-permute-start | bytes 393224 | tf_op jit(solution)/shard_map/ppermute | solution.py:279
  31.0 0.0 collective-permute-done.3.w1
  31.0 0.0 collective-permute-done.2.refs_3_
  31.0 0.0 collective-permute-done.1.refs_2_
  31.0 0.0 collective-permute-done.refs_1_
  31.0 0.4 collective-permute-start.7
  31.4 0.2 collective-permute-start.8
  31.6 0.3 collective-permute-start.9
  31.9 0.1 collective-permute-done.6.refs_4_
  32.0 0.5 collective-permute-done.7.refs_5_
  32.5 0.3 collective-permute-done.8.refs_6_
  32.7 0.2 collective-permute-done.9.refs_7_
  33.0 0.0 copy-done
  33.0 0.8 pick.1
  33.8 1.3 %collective-permute-start.10 = (bf16[2,2,4,16,128]{4,3,2,1,0:T(8,128)(2,1)S(1)}, bf16[2,2,4,16,128]{4,3,2,1,0:T(8,128)(2,1)S(1)}, u32[]{:S(2)}, u32[]{:S(2)}) collective-permute-start(bf16[2,2,4,16,128]{4,3,2,1,0:T(8,128)(2,1)S(1)} %get-tuple-element.30), channel_id=1, source_target_pairs={{0,1},{1,2},{2,3},{3,0},{4,5},{5,6},{6,7},{7,4},{8,9},{9,10},{10,1... | collective-permute-start | bytes 196616 | tf_op jit(solution)/shard_map/ppermute | solution.py:26
  35.1 2.5 %collective-permute-start.11 = (bf16[2,2,4,16,128]{4,3,2,1,0:T(8,128)(2,1)S(1)}, bf16[2,2,4,16,128]{4,3,2,1,0:T(8,128)(2,1)S(1)}, u32[]{:S(2)}, u32[]{:S(2)}) collective-permute-start(bf16[2,2,4,16,128]{4,3,2,1,0:T(8,128)(2,1)S(1)} %get-tuple-element.31), channel_id=1, source_target_pairs={{0,2},{1,3},{2,0},{3,1},{4,6},{5,7},{6,4},{7,5},{8,10},{9,11},{10,... | collective-permute-start | bytes 196616 | tf_op jit(solution)/shard_map/ppermute | solution.py:26
  37.6 1.2 %collective-permute-start.12 = (bf16[2,2,4,16,128]{4,3,2,1,0:T(8,128)(2,1)S(1)}, bf16[2,2,4,16,128]{4,3,2,1,0:T(8,128)(2,1)S(1)}, u32[]{:S(2)}, u32[]{:S(2)}) collective-permute-start(bf16[2,2,4,16,128]{4,3,2,1,0:T(8,128)(2,1)S(1)} %get-tuple-element.32), channel_id=1, source_target_pairs={{0,3},{1,0},{2,1},{3,2},{4,7},{5,4},{6,5},{7,6},{8,11},{9,8},{10,9... | collective-permute-start | bytes 196616 | tf_op jit(solution)/shard_map/ppermute | solution.py:26
  38.7 0.0 collective-permute-done.10.g1
  38.7 2.2 %collective-permute-done.11.g2 = bf16[2,2,4,16,128]{4,3,2,1,0:T(8,128)(2,1)S(1)} collective-permute-done((bf16[2,2,4,16,128]{4,3,2,1,0:T(8,128)(2,1)S(1)}, bf16[2,2,4,16,128]{4,3,2,1,0:T(8,128)(2,1)S(1)}, u32[]{:S(2)}, u32[]{:S(2)}) %collective-permute-start.11) | collective-permute-done | bytes 65568 | tf_op jit(solution)/shard_map/ppermute | solution.py:26
  40.9 0.1 collective-permute-done.12.g3
  41.0 9.6 %tile_pairs.1 = f32[8,40,128]{2,1,0:T(8,128)S(1)} custom-call(s32[1]{0:T(128)} %bitcast.me_ref, bf16[8,64,4096]{2,1,0:T(8,128)(2,1)} %t_ref.3, bf16[8,64,4096]{2,1,0:T(8,128)(2,1)} %prep.1.sw_ref, s32[3,8,128]{2,1,0:T(8,128)S(1)} %copy-done, bf16[2,2,4,16,128]{4,3,2,1,0:T(8,128)(2,1)S(1)} %get-tuple-element.29.g0, ...), custom_call_target="tpu_custom_call" | custom-call | tf_op jit(solution)/shard_map/tile_pairs/pallas_call | solution.py:206
  50.5 10.9 %all_to_all.20.t_ref = f32[8,40,128]{2,1,0:T(8,128)S(1)} all-to-all(f32[8,40,128]{2,1,0:T(8,128)S(1)} %tile_pairs.1), channel_id=1, replica_groups=mesh['z'=8,'h'=2,'l'=2,'c'=2,'x'=4] {'c','x'}, dimensions={0} | all-to-all | bytes 327680 | tf_op jit(solution)/shard_map/all_to_all | solution.py:286
  61.5 0.4 place.1
  61.9 12.7 %all_to_all.21.s_ref = bf16[32,16,128]{2,1,0:T(8,128)(2,1)S(1)} all-to-all(bf16[32,16,128]{2,1,0:T(8,128)(2,1)S(1)} %place.1), channel_id=1, replica_groups=mesh['z'=8,'h'=2,'l'=2,'c'=2,'x'=4] {'z','h','l'}, dimensions={0} | all-to-all | bytes 262144 | tf_op jit(solution)/shard_map/all_to_all | solution.py:288
  74.6 9.6 %all_to_all.22.p_ref = f32[8,8,128]{2,1,0:T(8,128)S(1)} all-to-all(f32[8,8,128]{2,1,0:T(8,128)S(1)} %sum.1), channel_id=1, replica_groups=mesh['z'=8,'h'=2,'l'=2,'c'=2,'x'=4] {'c','x'}, dimensions={0} | all-to-all | bytes 65536 | tf_op jit(solution)/shard_map/all_to_all | solution.py:290
  84.2 0.7 finish.1
  (1 shorter events, 0.0 us)
Async XLA Ops:
  1.4 16.8 %all-to-all-start = ((bf16[8,64,128]{2,1,0:T(8,128)(2,1)}), bf16[8,64,128]{2,1,0:T(8,128)(2,1)S(1)}, u32[]{:S(2)}, u32[]{:S(2)}) async-start(bf16[8,64,128]{2,1,0:T(8,128)(2,1)} %get-tuple-element.19), calls=%async_computation | async-start | bytes 262144 | tf_op jit(solution)/shard_map/all_to_all | solution.py:273
  10.4 22.5 %copy-start = (s32[3,8,128]{2,1,0:T(8,128)S(1)}, s32[3,8,128]{2,1,0:T(8,128)}, u32[]{:S(2)}) copy-start(s32[3,8,128]{2,1,0:T(8,128)} %get-tuple-element.22.w0.wants_ref) | copy-start | bytes 36868
  10.4 10.9 %collective-permute-start.5 = (s32[3,8,128]{2,1,0:T(8,128)}, s32[3,8,128]{2,1,0:T(8,128)S(1)}, u32[]{:S(2)}, u32[]{:S(2)}) collective-permute-start(s32[3,8,128]{2,1,0:T(8,128)} %get-tuple-element.22.w0.wants_ref), channel_id=1, source_target_pairs={{0,3},{1,0},{2,1},{3,2},{4,7},{5,4},{6,5},{7,6},{8,11},{9,8},{10,9... | collective-permute-start | bytes 36872 | tf_op jit(solution)/shard_map/ppermute | solution.py:26
  13.0 14.9 %collective-permute-start.4 = (s32[3,8,128]{2,1,0:T(8,128)}, s32[3,8,128]{2,1,0:T(8,128)S(1)}, u32[]{:S(2)}, u32[]{:S(2)}) collective-permute-start(s32[3,8,128]{2,1,0:T(8,128)} %get-tuple-element.22.w0.wants_ref), channel_id=1, source_target_pairs={{0,2},{1,3},{2,0},{3,1},{4,6},{5,7},{6,4},{7,5},{8,10},{9,11},{10,... | collective-permute-start | bytes 36872 | tf_op jit(solution)/shard_map/ppermute | solution.py:26
  13.5 17.5 %collective-permute-start.3 = (s32[3,8,128]{2,1,0:T(8,128)}, s32[3,8,128]{2,1,0:T(8,128)S(1)}, u32[]{:S(2)}, u32[]{:S(2)}) collective-permute-start(s32[3,8,128]{2,1,0:T(8,128)} %get-tuple-element.22.w0.wants_ref), channel_id=1, source_target_pairs={{0,1},{1,2},{2,3},{3,0},{4,5},{5,6},{6,7},{7,4},{8,9},{9,10},{10,1... | collective-permute-start | bytes 36872 | tf_op jit(solution)/shard_map/ppermute | solution.py:26
  18.2 12.8 %collective-permute-start.2 = (bf16[8,64,128]{2,1,0:T(8,128)(2,1)S(1)}, bf16[8,64,128]{2,1,0:T(8,128)(2,1)S(1)}, u32[]{:S(2)}, u32[]{:S(2)}) collective-permute-start(bf16[8,64,128]{2,1,0:T(8,128)(2,1)S(1)} %all-to-all-done.refs_0_), channel_id=1, source_target_pairs={{0,24},{8,0},{16,8},{24,16},{1,25},{9,1},{17,9},{25,17},{2,26},{10... | collective-permute-start | bytes 393224 | tf_op jit(solution)/shard_map/ppermute | solution.py:274
  20.9 10.1 %collective-permute-start.1 = (bf16[8,64,128]{2,1,0:T(8,128)(2,1)S(1)}, bf16[8,64,128]{2,1,0:T(8,128)(2,1)S(1)}, u32[]{:S(2)}, u32[]{:S(2)}) collective-permute-start(bf16[8,64,128]{2,1,0:T(8,128)(2,1)S(1)} %all-to-all-done.refs_0_), channel_id=1, source_target_pairs={{0,16},{8,24},{16,0},{24,8},{1,17},{9,25},{17,1},{25,9},{2,18},{10... | collective-permute-start | bytes 393224 | tf_op jit(solution)/shard_map/ppermute | solution.py:274
  21.3 9.7 %collective-permute-start = (bf16[8,64,128]{2,1,0:T(8,128)(2,1)S(1)}, bf16[8,64,128]{2,1,0:T(8,128)(2,1)S(1)}, u32[]{:S(2)}, u32[]{:S(2)}) collective-permute-start(bf16[8,64,128]{2,1,0:T(8,128)(2,1)S(1)} %all-to-all-done.refs_0_), channel_id=1, source_target_pairs={{0,8},{8,16},{16,24},{24,0},{1,9},{9,17},{17,25},{25,1},{2,10},{10... | collective-permute-start | bytes 393224 | tf_op jit(solution)/shard_map/ppermute | solution.py:274
  27.9 4.1 %collective-permute-start.6 = (bf16[8,64,128]{2,1,0:T(8,128)(2,1)S(1)}, bf16[8,64,128]{2,1,0:T(8,128)(2,1)S(1)}, u32[]{:S(2)}, u32[]{:S(2)}) collective-permute-start(bf16[8,64,128]{2,1,0:T(8,128)(2,1)S(1)} %all-to-all-done.refs_0_), channel_id=1, source_target_pairs={{0,4},{4,0},{1,5},{5,1},{2,6},{6,2},{3,7},{7,3},{8,12},{12,8},{9,1... | collective-permute-start | bytes 393224 | tf_op jit(solution)/shard_map/ppermute | solution.py:279
  31.0 1.4 %collective-permute-start.7 = (bf16[8,64,128]{2,1,0:T(8,128)(2,1)S(1)}, bf16[8,64,128]{2,1,0:T(8,128)(2,1)S(1)}, u32[]{:S(2)}, u32[]{:S(2)}) collective-permute-start(bf16[8,64,128]{2,1,0:T(8,128)(2,1)S(1)} %collective-permute-done.refs_1_), channel_id=1, source_target_pairs={{0,4},{4,0},{1,5},{5,1},{2,6},{6,2},{3,7},{7,3},{8,12},{12,8},{9,1... | collective-permute-start | bytes 393224 | tf_op jit(solution)/shard_map/ppermute | solution.py:279
  31.4 1.3 %collective-permute-start.8 = (bf16[8,64,128]{2,1,0:T(8,128)(2,1)S(1)}, bf16[8,64,128]{2,1,0:T(8,128)(2,1)S(1)}, u32[]{:S(2)}, u32[]{:S(2)}) collective-permute-start(bf16[8,64,128]{2,1,0:T(8,128)(2,1)S(1)} %collective-permute-done.1.refs_2_), channel_id=1, source_target_pairs={{0,4},{4,0},{1,5},{5,1},{2,6},{6,2},{3,7},{7,3},{8,12},{12,8},{9,1... | collective-permute-start | bytes 393224 | tf_op jit(solution)/shard_map/ppermute | solution.py:279
  31.6 1.3 %collective-permute-start.9 = (bf16[8,64,128]{2,1,0:T(8,128)(2,1)S(1)}, bf16[8,64,128]{2,1,0:T(8,128)(2,1)S(1)}, u32[]{:S(2)}, u32[]{:S(2)}) collective-permute-start(bf16[8,64,128]{2,1,0:T(8,128)(2,1)S(1)} %collective-permute-done.2.refs_3_), channel_id=1, source_target_pairs={{0,4},{4,0},{1,5},{5,1},{2,6},{6,2},{3,7},{7,3},{8,12},{12,8},{9,1... | collective-permute-start | bytes 393224 | tf_op jit(solution)/shard_map/ppermute | solution.py:279
  33.8 4.9 %collective-permute-start.10 = (bf16[2,2,4,16,128]{4,3,2,1,0:T(8,128)(2,1)S(1)}, bf16[2,2,4,16,128]{4,3,2,1,0:T(8,128)(2,1)S(1)}, u32[]{:S(2)}, u32[]{:S(2)}) collective-permute-start(bf16[2,2,4,16,128]{4,3,2,1,0:T(8,128)(2,1)S(1)} %get-tuple-element.30), channel_id=1, source_target_pairs={{0,1},{1,2},{2,3},{3,0},{4,5},{5,6},{6,7},{7,4},{8,9},{9,10},{10,1... | collective-permute-start | bytes 196616 | tf_op jit(solution)/shard_map/ppermute | solution.py:26
  35.1 5.8 %collective-permute-start.11 = (bf16[2,2,4,16,128]{4,3,2,1,0:T(8,128)(2,1)S(1)}, bf16[2,2,4,16,128]{4,3,2,1,0:T(8,128)(2,1)S(1)}, u32[]{:S(2)}, u32[]{:S(2)}) collective-permute-start(bf16[2,2,4,16,128]{4,3,2,1,0:T(8,128)(2,1)S(1)} %get-tuple-element.31), channel_id=1, source_target_pairs={{0,2},{1,3},{2,0},{3,1},{4,6},{5,7},{6,4},{7,5},{8,10},{9,11},{10,... | collective-permute-start | bytes 196616 | tf_op jit(solution)/shard_map/ppermute | solution.py:26
  37.6 3.4 %collective-permute-start.12 = (bf16[2,2,4,16,128]{4,3,2,1,0:T(8,128)(2,1)S(1)}, bf16[2,2,4,16,128]{4,3,2,1,0:T(8,128)(2,1)S(1)}, u32[]{:S(2)}, u32[]{:S(2)}) collective-permute-start(bf16[2,2,4,16,128]{4,3,2,1,0:T(8,128)(2,1)S(1)} %get-tuple-element.32), channel_id=1, source_target_pairs={{0,3},{1,0},{2,1},{3,2},{4,7},{5,4},{6,5},{7,6},{8,11},{9,8},{10,9... | collective-permute-start | bytes 196616 | tf_op jit(solution)/shard_map/ppermute | solution.py:26

commit v6 on v5

--- a/solution.py
+++ b/solution.py
@@ -194,10 +194,12 @@
     @pl.when(step == pl.num_programs(0) - 1)
     def _():
         target = wants_ref[2].astype(F32)
+        target = jnp.concatenate([target, target], axis=0).astype(BF16)
         for peer in range(NG):
-            for r in range(4):
-                o_ref[peer, r * 8:r * 8 + 8] = pk[pl.ds(4 * peer + r, 8, stride=40), :]
-            o_ref[peer, 32:40] = target
+            for r in (0, 2):
+                rows = [pk[pl.ds(4 * peer + r + i, 8, stride=40), :] for i in range(2)]
+                o_ref[peer, r * 8:r * 8 + 16] = jnp.concatenate(rows, axis=0).astype(BF16)
+            o_ref[peer, 32:48] = target
 
 
 def tile_pairs(me, tiles, swapped, wants, got):
@@ -206,9 +208,9 @@
     return pl.pallas_call(
         tile_kernel,
         grid=(count // 2,),
-        out_shape=jax.ShapeDtypeStruct((NG, 5 * count, 128), F32),
+        out_shape=jax.ShapeDtypeStruct((NG, 6 * count, 128), BF16),
         in_specs=[SMEM, tile, tile] + [VMEM] * 5,
-        out_specs=pl.BlockSpec((NG, 5 * count, 128), lambda i: (0, 0, 0)),
+        out_specs=pl.BlockSpec((NG, 6 * count, 128), lambda i: (0, 0, 0)),
         scratch_shapes=[
             pltpu.VMEM((BS * 24, 128), F32), pltpu.VMEM((BS * PITCH, 128), F32), pltpu.VMEM((BS * PITCH, 128), F32),
             pltpu.VMEM((128, BS * BS), BF16), pltpu.VMEM((128, BS * BS), BF16), pltpu.VMEM((count * 40, 128), F32),
@@ -219,19 +221,18 @@
 
 
 def place_kernel(t_ref, o_ref):
-    target = t_ref[:, 32:40, :].reshape(64, 128)
+    given = t_ref[...].astype(F32)
+    target = given[:, 32:40, :].reshape(64, 128)
     target = jnp.concatenate([target, target], axis=0).T.astype(jnp.int32)
     lane = lax.broadcasted_iota(jnp.int32, (128, 128), 1)
-    terms = jnp.concatenate([t_ref[:, r * 8:r * 8 + 8, :].reshape(64, 128) for r in range(4)], axis=0)
-    high = terms.astype(BF16)
-    rest = (terms - high.astype(F32)).astype(BF16)
+    terms = jnp.concatenate([given[:, r * 8:r * 8 + 8, :].reshape(64, 128) for r in range(4)], axis=0).astype(BF16)
     for part in range(4):
         row = lax.broadcasted_iota(jnp.int32, (128, 128), 0) + part * 128
         here = ((row >> 4) == (target >> 2)) & ((row & 3) == (target & 3))
         hot = jnp.concatenate([
             jnp.where(here & (((row >> 2) & 3) == (lane >> 6) + 2 * half), 1.0, 0.0).astype(BF16) for half in range(2)
         ], axis=1)
-        dense = jnp.dot(hot, high, preferred_element_type=F32) + jnp.dot(hot, rest, preferred_element_type=F32)
+        dense = jnp.dot(hot, terms, preferred_element_type=F32)
         o_ref[part * 8:part * 8 + 8] = dense.astype(BF16).reshape(8, 16, 128)
 
 

time: 85.3 us -> 84.5 us (level)
  no operation moved by 1% of the time
where the time goes in v6:
time: 84.5 us; the launch traced here: 84.1 us
  blocking collectives  32.6 us (39%)
  starting transfers between devices  25.4 us (30%)
  Pallas kernels  18.7 us (22%)
  waiting for transfers between devices  7.43 us (9%)
    all_to_all x1, blocking collectives, shards(): spread = lax.all_to_all(dense, ZHL, 0, 0)  12.7 us
    all_to_all x1, blocking collectives, shards(): terms = lax.all_to_all(pieces, CX, 0, 0)  10.4 us
    pallas_call x1, Pallas kernels, tile_pairs(): pl.pallas_call(tile_kernel, grid=(count // 2,), out_shape=jax.ShapeDtypeS...  9.56 us
    all_to_all x1, blocking collectives, shards(): parts = lax.all_to_all(owned, CX, 0, 0)  9.42 us
    all_to_all x1, starting transfers between devices, shards(): rows = lax.all_to_all(own, 'z', 0, 0)  9.02 us
    ppermute x6, starting transfers between devices, shift(): return lax.ppermute(values, 'x', [(i, (i + k) % NX) for i in range(NX)])  8.57 us
    pallas_call x1, Pallas kernels, prep(): pl.pallas_call(prep_kernel, grid=(count // 2,), out_shape=jax.ShapeDtypeS...  5.89 us
    all_to_all x1, waiting for transfers between devices, shards(): rows = lax.all_to_all(own, 'z', 0, 0)  4.08 us
  transfers between devices with their start and end apart: 14, of which 7 were waited for; matrix products, arithmetic and copies ran while one was open for 0% of the time, Pallas kernels for 7%

profile of v6, /device:TPU:1, one launch (start us, length us, event | category | flops | bytes accessed | tf_op | source)
XLA Modules:
  0.0 84.1 jit_solution(16761916518150622765)
XLA Ops:
  0.0 1.4 %rows.1 = (bf16[8,64,128]{2,1,0:T(8,128)(2,1)}, s32[3,8,128]{2,1,0:T(8,128)}) custom-call(s32[8]{0:T(128)} %row_ref.1, s32[8]{0:T(128)} %col_ref.1, s32[8]{0:T(128)} %dest_ref.1, s32[8]{0:T(128)} %aux_ref.1, bf16[4,1024]{1,0:T(4,128)(2,1)} %occ_ref.1, bf16[4,1024]{1,0:T(4,128)(2,1)} %virt_ref.1), custom_call_target="tpu_custom_call" | custom-call | tf_op jit(solution)/shard_map/rows/pallas_call | solution.py:259
  1.4 9.0 %all-to-all-start = ((bf16[8,64,128]{2,1,0:T(8,128)(2,1)}), bf16[8,64,128]{2,1,0:T(8,128)(2,1)S(1)}, u32[]{:S(2)}, u32[]{:S(2)}) async-start(bf16[8,64,128]{2,1,0:T(8,128)(2,1)} %get-tuple-element.19), calls=%async_computation | async-start | bytes 262144 | tf_op jit(solution)/shard_map/all_to_all | solution.py:274
  10.4 0.0 copy-start
  10.4 2.6 %collective-permute-start.5 = (s32[3,8,128]{2,1,0:T(8,128)}, s32[3,8,128]{2,1,0:T(8,128)S(1)}, u32[]{:S(2)}, u32[]{:S(2)}) collective-permute-start(s32[3,8,128]{2,1,0:T(8,128)} %get-tuple-element.22.w0.wants_ref), channel_id=1, source_target_pairs={{0,3},{1,0},{2,1},{3,2},{4,7},{5,4},{6,5},{7,6},{8,11},{9,8},{10,9... | collective-permute-start | bytes 36872 | tf_op jit(solution)/shard_map/ppermute | solution.py:26
  13.0 0.5 collective-permute-start.4
  13.5 0.6 collective-permute-start.3
  14.1 4.1 %all-to-all-done.refs_0_ = bf16[8,64,128]{2,1,0:T(8,128)(2,1)S(1)} async-done(((bf16[8,64,128]{2,1,0:T(8,128)(2,1)}), bf16[8,64,128]{2,1,0:T(8,128)(2,1)S(1)}, u32[]{:S(2)}, u32[]{:S(2)}) %all-to-all-start) | async-done | bytes 131104 | tf_op jit(solution)/shard_map/all_to_all | solution.py:274
  18.2 2.7 %collective-permute-start.2 = (bf16[8,64,128]{2,1,0:T(8,128)(2,1)S(1)}, bf16[8,64,128]{2,1,0:T(8,128)(2,1)S(1)}, u32[]{:S(2)}, u32[]{:S(2)}) collective-permute-start(bf16[8,64,128]{2,1,0:T(8,128)(2,1)S(1)} %all-to-all-done.refs_0_), channel_id=1, source_target_pairs={{0,24},{8,0},{16,8},{24,16},{1,25},{9,1},{17,9},{25,17},{2,26},{10... | collective-permute-start | bytes 393224 | tf_op jit(solution)/shard_map/ppermute | solution.py:275
  20.9 0.3 collective-permute-start.1
  21.3 0.0 collective-permute-done.5.w3
  21.3 0.7 collective-permute-start
  22.0 5.9 %prep.1.sw_ref = bf16[8,64,4096]{2,1,0:T(8,128)(2,1)} custom-call(bf16[8,64,4096]{2,1,0:T(8,128)(2,1)} %t_ref.3), custom_call_target="tpu_custom_call" | custom-call | flops 8999999488 | bytes 8388608 | tf_op jit(solution)/shard_map/prep/pallas_call | solution.py:70
  27.9 0.0 collective-permute-done.4.w2
  27.9 3.1 %collective-permute-start.6 = (bf16[8,64,128]{2,1,0:T(8,128)(2,1)S(1)}, bf16[8,64,128]{2,1,0:T(8,128)(2,1)S(1)}, u32[]{:S(2)}, u32[]{:S(2)}) collective-permute-start(bf16[8,64,128]{2,1,0:T(8,128)(2,1)S(1)} %all-to-all-done.refs_0_), channel_id=1, source_target_pairs={{0,4},{4,0},{1,5},{5,1},{2,6},{6,2},{3,7},{7,3},{8,12},{12,8},{9,1... | collective-permute-start | bytes 393224 | tf_op jit(solution)/shard_map/ppermute | solution.py:280
  31.0 0.0 collective-permute-done.3.w1
  31.0 0.0 collective-permute-done.2.refs_3_
  31.0 0.0 collective-permute-done.1.refs_2_
  31.0 0.0 collective-permute-done.refs_1_
  31.0 0.4 collective-permute-start.7
  31.4 0.2 collective-permute-start.8
  31.6 0.3 collective-permute-start.9
  31.9 0.1 collective-permute-done.6.refs_4_
  32.0 0.5 collective-permute-done.7.refs_5_
  32.5 0.3 collective-permute-done.8.refs_6_
  32.7 0.2 collective-permute-done.9.refs_7_
  33.0 0.0 copy-done
  33.0 0.8 %pick.1 = (bf16[2,2,4,16,128]{4,3,2,1,0:T(8,128)(2,1)S(1)}, bf16[2,2,4,16,128]{4,3,2,1,0:T(8,128)(2,1)S(1)}, bf16[2,2,4,16,128]{4,3,2,1,0:T(8,128)(2,1)S(1)}, bf16[2,2,4,16,128]{4,3,2,1,0:T(8,128)(2,1)S(1)}) custom-call(s32[1]{0:T(128)} %bitcast.1.core_ref, s32[1]{0:T(128)} %bitcast.2.y_ref, s32[3,8,128]{2,1,0:T(8,128)S(1)} %copy-done, ...), custom_call_target="tpu_custom_call" | custom-call | tf_op jit(solution)/shard_map/pick/pallas_call | solution.py:259
  33.8 1.3 %collective-permute-start.10 = (bf16[2,2,4,16,128]{4,3,2,1,0:T(8,128)(2,1)S(1)}, bf16[2,2,4,16,128]{4,3,2,1,0:T(8,128)(2,1)S(1)}, u32[]{:S(2)}, u32[]{:S(2)}) collective-permute-start(bf16[2,2,4,16,128]{4,3,2,1,0:T(8,128)(2,1)S(1)} %get-tuple-element.30), channel_id=1, source_target_pairs={{0,1},{1,2},{2,3},{3,0},{4,5},{5,6},{6,7},{7,4},{8,9},{9,10},{10,1... | collective-permute-start | bytes 196616 | tf_op jit(solution)/shard_map/ppermute | solution.py:26
  35.1 2.5 %collective-permute-start.11 = (bf16[2,2,4,16,128]{4,3,2,1,0:T(8,128)(2,1)S(1)}, bf16[2,2,4,16,128]{4,3,2,1,0:T(8,128)(2,1)S(1)}, u32[]{:S(2)}, u32[]{:S(2)}) collective-permute-start(bf16[2,2,4,16,128]{4,3,2,1,0:T(8,128)(2,1)S(1)} %get-tuple-element.31), channel_id=1, source_target_pairs={{0,2},{1,3},{2,0},{3,1},{4,6},{5,7},{6,4},{7,5},{8,10},{9,11},{10,... | collective-permute-start | bytes 196616 | tf_op jit(solution)/shard_map/ppermute | solution.py:26
  37.6 1.2 %collective-permute-start.12 = (bf16[2,2,4,16,128]{4,3,2,1,0:T(8,128)(2,1)S(1)}, bf16[2,2,4,16,128]{4,3,2,1,0:T(8,128)(2,1)S(1)}, u32[]{:S(2)}, u32[]{:S(2)}) collective-permute-start(bf16[2,2,4,16,128]{4,3,2,1,0:T(8,128)(2,1)S(1)} %get-tuple-element.32), channel_id=1, source_target_pairs={{0,3},{1,0},{2,1},{3,2},{4,7},{5,4},{6,5},{7,6},{8,11},{9,8},{10,9... | collective-permute-start | bytes 196616 | tf_op jit(solution)/shard_map/ppermute | solution.py:26
  38.7 0.0 collective-permute-done.10.g1
  38.7 2.2 %collective-permute-done.11.g2 = bf16[2,2,4,16,128]{4,3,2,1,0:T(8,128)(2,1)S(1)} collective-permute-done((bf16[2,2,4,16,128]{4,3,2,1,0:T(8,128)(2,1)S(1)}, bf16[2,2,4,16,128]{4,3,2,1,0:T(8,128)(2,1)S(1)}, u32[]{:S(2)}, u32[]{:S(2)}) %collective-permute-start.11) | collective-permute-done | bytes 65568 | tf_op jit(solution)/shard_map/ppermute | solution.py:26
  40.9 0.1 collective-permute-done.12.g3
  41.0 9.6 %tile_pairs.1 = bf16[8,48,128]{2,1,0:T(8,128)(2,1)S(1)} custom-call(s32[1]{0:T(128)} %bitcast.me_ref, bf16[8,64,4096]{2,1,0:T(8,128)(2,1)} %t_ref.3, bf16[8,64,4096]{2,1,0:T(8,128)(2,1)} %prep.1.sw_ref, s32[3,8,128]{2,1,0:T(8,128)S(1)} %copy-done, bf16[2,2,4,16,128]{4,3,2,1,0:T(8,128)(2,1)S(1)} %get-tuple-element.29.g0, ...), custom_call_target="tpu_custom_call" | custom-call | tf_op jit(solution)/shard_map/tile_pairs/pallas_call | solution.py:208
  50.5 10.4 %all_to_all.20.t_ref = bf16[8,48,128]{2,1,0:T(8,128)(2,1)S(1)} all-to-all(bf16[8,48,128]{2,1,0:T(8,128)(2,1)S(1)} %tile_pairs.1), channel_id=1, replica_groups=mesh['z'=8,'h'=2,'l'=2,'c'=2,'x'=4] {'c','x'}, dimensions={0} | all-to-all | bytes 196608 | tf_op jit(solution)/shard_map/all_to_all | solution.py:287
  61.0 0.3 place.1
  61.3 12.7 %all_to_all.21.s_ref = bf16[32,16,128]{2,1,0:T(8,128)(2,1)S(1)} all-to-all(bf16[32,16,128]{2,1,0:T(8,128)(2,1)S(1)} %place.1), channel_id=1, replica_groups=mesh['z'=8,'h'=2,'l'=2,'c'=2,'x'=4] {'z','h','l'}, dimensions={0} | all-to-all | bytes 262144 | tf_op jit(solution)/shard_map/all_to_all | solution.py:289
  74.0 9.4 %all_to_all.22.p_ref = f32[8,8,128]{2,1,0:T(8,128)S(1)} all-to-all(f32[8,8,128]{2,1,0:T(8,128)S(1)} %sum.1), channel_id=1, replica_groups=mesh['z'=8,'h'=2,'l'=2,'c'=2,'x'=4] {'c','x'}, dimensions={0} | all-to-all | bytes 65536 | tf_op jit(solution)/shard_map/all_to_all | solution.py:291
  83.4 0.7 finish.1
  (1 shorter events, 0.0 us)
Async XLA Ops:
  1.4 16.8 %all-to-all-start = ((bf16[8,64,128]{2,1,0:T(8,128)(2,1)}), bf16[8,64,128]{2,1,0:T(8,128)(2,1)S(1)}, u32[]{:S(2)}, u32[]{:S(2)}) async-start(bf16[8,64,128]{2,1,0:T(8,128)(2,1)} %get-tuple-element.19), calls=%async_computation | async-start | bytes 262144 | tf_op jit(solution)/shard_map/all_to_all | solution.py:274
  10.4 22.5 %copy-start = (s32[3,8,128]{2,1,0:T(8,128)S(1)}, s32[3,8,128]{2,1,0:T(8,128)}, u32[]{:S(2)}) copy-start(s32[3,8,128]{2,1,0:T(8,128)} %get-tuple-element.22.w0.wants_ref) | copy-start | bytes 36868
  10.4 10.9 %collective-permute-start.5 = (s32[3,8,128]{2,1,0:T(8,128)}, s32[3,8,128]{2,1,0:T(8,128)S(1)}, u32[]{:S(2)}, u32[]{:S(2)}) collective-permute-start(s32[3,8,128]{2,1,0:T(8,128)} %get-tuple-element.22.w0.wants_ref), channel_id=1, source_target_pairs={{0,3},{1,0},{2,1},{3,2},{4,7},{5,4},{6,5},{7,6},{8,11},{9,8},{10,9... | collective-permute-start | bytes 36872 | tf_op jit(solution)/shard_map/ppermute | solution.py:26
  13.0 14.9 %collective-permute-start.4 = (s32[3,8,128]{2,1,0:T(8,128)}, s32[3,8,128]{2,1,0:T(8,128)S(1)}, u32[]{:S(2)}, u32[]{:S(2)}) collective-permute-start(s32[3,8,128]{2,1,0:T(8,128)} %get-tuple-element.22.w0.wants_ref), channel_id=1, source_target_pairs={{0,2},{1,3},{2,0},{3,1},{4,6},{5,7},{6,4},{7,5},{8,10},{9,11},{10,... | collective-permute-start | bytes 36872 | tf_op jit(solution)/shard_map/ppermute | solution.py:26
  13.5 17.5 %collective-permute-start.3 = (s32[3,8,128]{2,1,0:T(8,128)}, s32[3,8,128]{2,1,0:T(8,128)S(1)}, u32[]{:S(2)}, u32[]{:S(2)}) collective-permute-start(s32[3,8,128]{2,1,0:T(8,128)} %get-tuple-element.22.w0.wants_ref), channel_id=1, source_target_pairs={{0,1},{1,2},{2,3},{3,0},{4,5},{5,6},{6,7},{7,4},{8,9},{9,10},{10,1... | collective-permute-start | bytes 36872 | tf_op jit(solution)/shard_map/ppermute | solution.py:26
  18.2 12.8 %collective-permute-start.2 = (bf16[8,64,128]{2,1,0:T(8,128)(2,1)S(1)}, bf16[8,64,128]{2,1,0:T(8,128)(2,1)S(1)}, u32[]{:S(2)}, u32[]{:S(2)}) collective-permute-start(bf16[8,64,128]{2,1,0:T(8,128)(2,1)S(1)} %all-to-all-done.refs_0_), channel_id=1, source_target_pairs={{0,24},{8,0},{16,8},{24,16},{1,25},{9,1},{17,9},{25,17},{2,26},{10... | collective-permute-start | bytes 393224 | tf_op jit(solution)/shard_map/ppermute | solution.py:275
  20.9 10.1 %collective-permute-start.1 = (bf16[8,64,128]{2,1,0:T(8,128)(2,1)S(1)}, bf16[8,64,128]{2,1,0:T(8,128)(2,1)S(1)}, u32[]{:S(2)}, u32[]{:S(2)}) collective-permute-start(bf16[8,64,128]{2,1,0:T(8,128)(2,1)S(1)} %all-to-all-done.refs_0_), channel_id=1, source_target_pairs={{0,16},{8,24},{16,0},{24,8},{1,17},{9,25},{17,1},{25,9},{2,18},{10... | collective-permute-start | bytes 393224 | tf_op jit(solution)/shard_map/ppermute | solution.py:275
  21.3 9.7 %collective-permute-start = (bf16[8,64,128]{2,1,0:T(8,128)(2,1)S(1)}, bf16[8,64,128]{2,1,0:T(8,128)(2,1)S(1)}, u32[]{:S(2)}, u32[]{:S(2)}) collective-permute-start(bf16[8,64,128]{2,1,0:T(8,128)(2,1)S(1)} %all-to-all-done.refs_0_), channel_id=1, source_target_pairs={{0,8},{8,16},{16,24},{24,0},{1,9},{9,17},{17,25},{25,1},{2,10},{10... | collective-permute-start | bytes 393224 | tf_op jit(solution)/shard_map/ppermute | solution.py:275
  27.9 4.1 %collective-permute-start.6 = (bf16[8,64,128]{2,1,0:T(8,128)(2,1)S(1)}, bf16[8,64,128]{2,1,0:T(8,128)(2,1)S(1)}, u32[]{:S(2)}, u32[]{:S(2)}) collective-permute-start(bf16[8,64,128]{2,1,0:T(8,128)(2,1)S(1)} %all-to-all-done.refs_0_), channel_id=1, source_target_pairs={{0,4},{4,0},{1,5},{5,1},{2,6},{6,2},{3,7},{7,3},{8,12},{12,8},{9,1... | collective-permute-start | bytes 393224 | tf_op jit(solution)/shard_map/ppermute | solution.py:280
  31.0 1.4 %collective-permute-start.7 = (bf16[8,64,128]{2,1,0:T(8,128)(2,1)S(1)}, bf16[8,64,128]{2,1,0:T(8,128)(2,1)S(1)}, u32[]{:S(2)}, u32[]{:S(2)}) collective-permute-start(bf16[8,64,128]{2,1,0:T(8,128)(2,1)S(1)} %collective-permute-done.refs_1_), channel_id=1, source_target_pairs={{0,4},{4,0},{1,5},{5,1},{2,6},{6,2},{3,7},{7,3},{8,12},{12,8},{9,1... | collective-permute-start | bytes 393224 | tf_op jit(solution)/shard_map/ppermute | solution.py:280
  31.4 1.3 %collective-permute-start.8 = (bf16[8,64,128]{2,1,0:T(8,128)(2,1)S(1)}, bf16[8,64,128]{2,1,0:T(8,128)(2,1)S(1)}, u32[]{:S(2)}, u32[]{:S(2)}) collective-permute-start(bf16[8,64,128]{2,1,0:T(8,128)(2,1)S(1)} %collective-permute-done.1.refs_2_), channel_id=1, source_target_pairs={{0,4},{4,0},{1,5},{5,1},{2,6},{6,2},{3,7},{7,3},{8,12},{12,8},{9,1... | collective-permute-start | bytes 393224 | tf_op jit(solution)/shard_map/ppermute | solution.py:280
  31.6 1.3 %collective-permute-start.9 = (bf16[8,64,128]{2,1,0:T(8,128)(2,1)S(1)}, bf16[8,64,128]{2,1,0:T(8,128)(2,1)S(1)}, u32[]{:S(2)}, u32[]{:S(2)}) collective-permute-start(bf16[8,64,128]{2,1,0:T(8,128)(2,1)S(1)} %collective-permute-done.2.refs_3_), channel_id=1, source_target_pairs={{0,4},{4,0},{1,5},{5,1},{2,6},{6,2},{3,7},{7,3},{8,12},{12,8},{9,1... | collective-permute-start | bytes 393224 | tf_op jit(solution)/shard_map/ppermute | solution.py:280
  33.8 4.9 %collective-permute-start.10 = (bf16[2,2,4,16,128]{4,3,2,1,0:T(8,128)(2,1)S(1)}, bf16[2,2,4,16,128]{4,3,2,1,0:T(8,128)(2,1)S(1)}, u32[]{:S(2)}, u32[]{:S(2)}) collective-permute-start(bf16[2,2,4,16,128]{4,3,2,1,0:T(8,128)(2,1)S(1)} %get-tuple-element.30), channel_id=1, source_target_pairs={{0,1},{1,2},{2,3},{3,0},{4,5},{5,6},{6,7},{7,4},{8,9},{9,10},{10,1... | collective-permute-start | bytes 196616 | tf_op jit(solution)/shard_map/ppermute | solution.py:26
  35.1 5.8 %collective-permute-start.11 = (bf16[2,2,4,16,128]{4,3,2,1,0:T(8,128)(2,1)S(1)}, bf16[2,2,4,16,128]{4,3,2,1,0:T(8,128)(2,1)S(1)}, u32[]{:S(2)}, u32[]{:S(2)}) collective-permute-start(bf16[2,2,4,16,128]{4,3,2,1,0:T(8,128)(2,1)S(1)} %get-tuple-element.31), channel_id=1, source_target_pairs={{0,2},{1,3},{2,0},{3,1},{4,6},{5,7},{6,4},{7,5},{8,10},{9,11},{10,... | collective-permute-start | bytes 196616 | tf_op jit(solution)/shard_map/ppermute | solution.py:26
  37.6 3.4 %collective-permute-start.12 = (bf16[2,2,4,16,128]{4,3,2,1,0:T(8,128)(2,1)S(1)}, bf16[2,2,4,16,128]{4,3,2,1,0:T(8,128)(2,1)S(1)}, u32[]{:S(2)}, u32[]{:S(2)}) collective-permute-start(bf16[2,2,4,16,128]{4,3,2,1,0:T(8,128)(2,1)S(1)} %get-tuple-element.32), channel_id=1, source_target_pairs={{0,3},{1,0},{2,1},{3,2},{4,7},{5,4},{6,5},{7,6},{8,11},{9,8},{10,9... | collective-permute-start | bytes 196616 | tf_op jit(solution)/shard_map/ppermute | solution.py:26

commit v7 on v6

--- a/solution.py
+++ b/solution.py
@@ -30,14 +30,17 @@
     return lax.broadcasted_iota(jnp.int32, (rows, 128), 1) < BS
 
 
-def rows_kernel(row_ref, col_ref, dest_ref, aux_ref, occ_ref, virt_ref, o_ref, wants_ref, scr):
+def rows_kernel(row_ref, col_ref, dest_ref, aux_ref, occ_ref, virt_ref, o_ref, wants_ref, target_ref, scr):
     at = lax.broadcasted_iota(jnp.int32, (8, 128), 0)
     for j in range(3):
         found = jnp.zeros((8, 128), jnp.int32)
         for t in range(8):
             value = row_ref[t] if j == 0 else col_ref[t] if j == 1 else dest_ref[t] * AUX + aux_ref[t]
             found = jnp.where(at == t, value, found)
-        wants_ref[j] = found
+        if j < 2:
+            wants_ref[j] = found
+        else:
+            target_ref[...] = jnp.concatenate([found, found], axis=0).astype(F32).astype(BF16)
     for arr, ref in enumerate((occ_ref, virt_ref)):
         values = ref[...].astype(F32)
         for i in range(4):
@@ -122,7 +125,7 @@
                         o_ref[l, side, ih * 2 + il] = jnp.concatenate([f[cut] for f in found], axis=0).astype(BF16)
 
 
-def tile_kernel(me_ref, t_ref, sw_ref, wants_ref, g0, g1, g2, g3, o_ref, gscr, us, ws, ys, zs, pk):
+def tile_kernel(me_ref, t_ref, sw_ref, target_ref, g0, g1, g2, g3, o_ref, gscr, us, ws, ys, zs, pk):
     step = pl.program_id(0)
 
     @pl.when(step == 0)
@@ -193,8 +196,7 @@
 
     @pl.when(step == pl.num_programs(0) - 1)
     def _():
-        target = wants_ref[2].astype(F32)
-        target = jnp.concatenate([target, target], axis=0).astype(BF16)
+        target = target_ref[...]
         for peer in range(NG):
             for r in (0, 2):
                 rows = [pk[pl.ds(4 * peer + r + i, 8, stride=40), :] for i in range(2)]
@@ -202,7 +204,7 @@
             o_ref[peer, 32:48] = target
 
 
-def tile_pairs(me, tiles, swapped, wants, got):
+def tile_pairs(me, tiles, swapped, target, got):
     count = tiles.shape[0]
     tile = pl.BlockSpec((2, BS, BS * BS), lambda i: (i, 0, 0))
     return pl.pallas_call(
@@ -217,7 +219,7 @@
         ],
         compiler_params=pltpu.CompilerParams(vmem_limit_bytes=MIDDLE),
         name="tile_pairs",
-    )(me, tiles, swapped, wants, *got)
+    )(me, tiles, swapped, target, *got)
 
 
 def place_kernel(t_ref, o_ref):
@@ -268,9 +270,9 @@
 
 def shards(tiles, tile_dest, tile_aux, tile_row, tile_col, green_occ, green_virt):
     me = lax.axis_index("x").reshape(1)
-    own, wants = call(rows_kernel, "rows", [((8, BS, 128), BF16), ((3, 8, 128), jnp.int32)],
+    own, wants, target = call(rows_kernel, "rows", [((8, BS, 128), BF16), ((2, 8, 128), jnp.int32), ((16, 128), BF16)],
                       tile_row, tile_col, tile_dest, tile_aux, green_occ, green_virt,
-                      spaces=[SMEM] * 4 + [VMEM] * 2, limit=LARGE, out_specs=[VMEM] * 2, scratch_shapes=[pltpu.VMEM((BS, 128), F32)])
+                      spaces=[SMEM] * 4 + [VMEM] * 2, limit=LARGE, out_specs=[VMEM] * 3, scratch_shapes=[pltpu.VMEM((BS, 128), F32)])
     rows = lax.all_to_all(own, "z", 0, 0)
     pieces = [rows] + [lax.ppermute(rows, HL, [(i, (i + k) % NY) for i in range(NY)]) for k in range(1, NY)]
     asked = [wants] + [shift(wants, k) for k in range(1, NX)]
@@ -283,7 +285,7 @@
                   spaces=[SMEM] * 2 + [VMEM] * (NX + 2 * NY), out_specs=[VMEM] * NX,
                   scratch_shapes=[pltpu.VMEM((2, NY, 8, BS, 128), BF16)])
     got = [picked[0]] + [shift(picked[NX - k], k) for k in range(1, NX)]
-    pieces = tile_pairs(me, tiles, swapped, wants, got)
+    pieces = tile_pairs(me, tiles, swapped, target, got)
     terms = lax.all_to_all(pieces, CX, 0, 0)
     dense = call(place_kernel, "place", ((32, 16, 128), BF16), terms, out_specs=VMEM)
     spread = lax.all_to_all(dense, ZHL, 0, 0)

time: 84.5 us -> 84.5 us (level)
  no operation moved by 1% of the time
where the time goes in v7:
time: 84.5 us; the launch traced here: 84.1 us
  blocking collectives  32.6 us (39%)
  starting transfers between devices  25.4 us (30%)
  Pallas kernels  18.7 us (22%)
  waiting for transfers between devices  7.41 us (9%)
    all_to_all x1, blocking collectives, shards(): spread = lax.all_to_all(dense, ZHL, 0, 0)  12.7 us
    all_to_all x1, blocking collectives, shards(): terms = lax.all_to_all(pieces, CX, 0, 0)  10.4 us
    pallas_call x1, Pallas kernels, tile_pairs(): pl.pallas_call(tile_kernel, grid=(count // 2,), out_shape=jax.ShapeDtypeS...  9.56 us
    all_to_all x1, blocking collectives, shards(): parts = lax.all_to_all(owned, CX, 0, 0)  9.42 us
    all_to_all x1, starting transfers between devices, shards(): rows = lax.all_to_all(own, 'z', 0, 0)  9.02 us
    ppermute x6, starting transfers between devices, shift(): return lax.ppermute(values, 'x', [(i, (i + k) % NX) for i in range(NX)])  8.58 us
    pallas_call x1, Pallas kernels, prep(): pl.pallas_call(prep_kernel, grid=(count // 2,), out_shape=jax.ShapeDtypeS...  5.87 us
    all_to_all x1, waiting for transfers between devices, shards(): rows = lax.all_to_all(own, 'z', 0, 0)  4.07 us
  transfers between devices with their start and end apart: 14, of which 7 were waited for; matrix products, arithmetic and copies ran while one was open for 0% of the time, Pallas kernels for 7%

profile of v7, /device:TPU:1, one launch (start us, length us, event | category | flops | bytes accessed | tf_op | source)
XLA Modules:
  0.0 84.1 jit_solution(1220556569715540211)
XLA Ops:
  0.0 1.4 %rows.1 = (bf16[8,64,128]{2,1,0:T(8,128)(2,1)}, s32[2,8,128]{2,1,0:T(8,128)}, bf16[16,128]{1,0:T(8,128)(2,1)}) custom-call(s32[8]{0:T(128)} %row_ref.1, s32[8]{0:T(128)} %col_ref.1, s32[8]{0:T(128)} %dest_ref.1, s32[8]{0:T(128)} %aux_ref.1, bf16[4,1024]{1,0:T(4,128)(2,1)} %occ_ref.1, bf16[4,1024]{1,0:T(4,128)(2,1)} %virt_ref.1), custom_call_target="tpu_custom_call" | custom-call | tf_op jit(solution)/shard_map/rows/pallas_call | solution.py:261
  1.4 9.0 %all-to-all-start = ((bf16[8,64,128]{2,1,0:T(8,128)(2,1)}), bf16[8,64,128]{2,1,0:T(8,128)(2,1)S(1)}, u32[]{:S(2)}, u32[]{:S(2)}) async-start(bf16[8,64,128]{2,1,0:T(8,128)(2,1)} %get-tuple-element.20), calls=%async_computation | async-start | bytes 262144 | tf_op jit(solution)/shard_map/all_to_all | solution.py:276
  10.5 0.0 copy-start
  10.5 0.0 copy-start.1
  10.5 2.6 %collective-permute-start.5 = (s32[2,8,128]{2,1,0:T(8,128)}, s32[2,8,128]{2,1,0:T(8,128)S(1)}, u32[]{:S(2)}, u32[]{:S(2)}) collective-permute-start(s32[2,8,128]{2,1,0:T(8,128)} %get-tuple-element.24.w0), channel_id=1, source_target_pairs={{0,3},{1,0},{2,1},{3,2},{4,7},{5,4},{6,5},{7,6},{8,11},{9,8},{10,9... | collective-permute-start | bytes 24584 | tf_op jit(solution)/shard_map/ppermute | solution.py:26
  13.0 0.5 collective-permute-start.4
  13.5 0.6 collective-permute-start.3
  14.2 4.1 %all-to-all-done.refs_0_ = bf16[8,64,128]{2,1,0:T(8,128)(2,1)S(1)} async-done(((bf16[8,64,128]{2,1,0:T(8,128)(2,1)}), bf16[8,64,128]{2,1,0:T(8,128)(2,1)S(1)}, u32[]{:S(2)}, u32[]{:S(2)}) %all-to-all-start) | async-done | bytes 131104 | tf_op jit(solution)/shard_map/all_to_all | solution.py:276
  18.2 2.7 %collective-permute-start.2 = (bf16[8,64,128]{2,1,0:T(8,128)(2,1)S(1)}, bf16[8,64,128]{2,1,0:T(8,128)(2,1)S(1)}, u32[]{:S(2)}, u32[]{:S(2)}) collective-permute-start(bf16[8,64,128]{2,1,0:T(8,128)(2,1)S(1)} %all-to-all-done.refs_0_), channel_id=1, source_target_pairs={{0,24},{8,0},{16,8},{24,16},{1,25},{9,1},{17,9},{25,17},{2,26},{10... | collective-permute-start | bytes 393224 | tf_op jit(solution)/shard_map/ppermute | solution.py:277
  21.0 0.3 collective-permute-start.1
  21.3 0.0 collective-permute-done.5.w3
  21.3 0.7 collective-permute-start
  22.0 5.9 %prep.1.sw_ref = bf16[8,64,4096]{2,1,0:T(8,128)(2,1)} custom-call(bf16[8,64,4096]{2,1,0:T(8,128)(2,1)} %t_ref.3), custom_call_target="tpu_custom_call" | custom-call | flops 8999999488 | bytes 8388608 | tf_op jit(solution)/shard_map/prep/pallas_call | solution.py:73
  27.9 0.0 collective-permute-done.4.w2
  27.9 3.1 %collective-permute-start.6 = (bf16[8,64,128]{2,1,0:T(8,128)(2,1)S(1)}, bf16[8,64,128]{2,1,0:T(8,128)(2,1)S(1)}, u32[]{:S(2)}, u32[]{:S(2)}) collective-permute-start(bf16[8,64,128]{2,1,0:T(8,128)(2,1)S(1)} %all-to-all-done.refs_0_), channel_id=1, source_target_pairs={{0,4},{4,0},{1,5},{5,1},{2,6},{6,2},{3,7},{7,3},{8,12},{12,8},{9,1... | collective-permute-start | bytes 393224 | tf_op jit(solution)/shard_map/ppermute | solution.py:282
  31.0 0.0 collective-permute-done.3.w1
  31.0 0.0 collective-permute-done.2.refs_3_
  31.0 0.0 collective-permute-done.1.refs_2_
  31.0 0.0 collective-permute-done.refs_1_
  31.0 0.4 collective-permute-start.7
  31.4 0.2 collective-permute-start.8
  31.6 0.3 collective-permute-start.9
  31.9 0.1 collective-permute-done.6.refs_4_
  32.0 0.5 collective-permute-done.7.refs_5_
  32.5 0.3 collective-permute-done.8.refs_6_
  32.7 0.2 collective-permute-done.9.refs_7_
  33.0 0.0 copy-done
  33.0 0.8 %pick.1 = (bf16[2,2,4,16,128]{4,3,2,1,0:T(8,128)(2,1)S(1)}, bf16[2,2,4,16,128]{4,3,2,1,0:T(8,128)(2,1)S(1)}, bf16[2,2,4,16,128]{4,3,2,1,0:T(8,128)(2,1)S(1)}, bf16[2,2,4,16,128]{4,3,2,1,0:T(8,128)(2,1)S(1)}) custom-call(s32[1]{0:T(128)} %bitcast.1.core_ref, s32[1]{0:T(128)} %bitcast.2.y_ref, s32[2,8,128]{2,1,0:T(8,128)S(1)} %copy-done, ...), custom_call_target="tpu_custom_call" | custom-call | tf_op jit(solution)/shard_map/pick/pallas_call | solution.py:261
  33.8 1.3 %collective-permute-start.10 = (bf16[2,2,4,16,128]{4,3,2,1,0:T(8,128)(2,1)S(1)}, bf16[2,2,4,16,128]{4,3,2,1,0:T(8,128)(2,1)S(1)}, u32[]{:S(2)}, u32[]{:S(2)}) collective-permute-start(bf16[2,2,4,16,128]{4,3,2,1,0:T(8,128)(2,1)S(1)} %get-tuple-element.32), channel_id=1, source_target_pairs={{0,1},{1,2},{2,3},{3,0},{4,5},{5,6},{6,7},{7,4},{8,9},{9,10},{10,1... | collective-permute-start | bytes 196616 | tf_op jit(solution)/shard_map/ppermute | solution.py:26
  35.1 2.4 %collective-permute-start.11 = (bf16[2,2,4,16,128]{4,3,2,1,0:T(8,128)(2,1)S(1)}, bf16[2,2,4,16,128]{4,3,2,1,0:T(8,128)(2,1)S(1)}, u32[]{:S(2)}, u32[]{:S(2)}) collective-permute-start(bf16[2,2,4,16,128]{4,3,2,1,0:T(8,128)(2,1)S(1)} %get-tuple-element.33), channel_id=1, source_target_pairs={{0,2},{1,3},{2,0},{3,1},{4,6},{5,7},{6,4},{7,5},{8,10},{9,11},{10,... | collective-permute-start | bytes 196616 | tf_op jit(solution)/shard_map/ppermute | solution.py:26
  37.6 1.2 %collective-permute-start.12 = (bf16[2,2,4,16,128]{4,3,2,1,0:T(8,128)(2,1)S(1)}, bf16[2,2,4,16,128]{4,3,2,1,0:T(8,128)(2,1)S(1)}, u32[]{:S(2)}, u32[]{:S(2)}) collective-permute-start(bf16[2,2,4,16,128]{4,3,2,1,0:T(8,128)(2,1)S(1)} %get-tuple-element.34), channel_id=1, source_target_pairs={{0,3},{1,0},{2,1},{3,2},{4,7},{5,4},{6,5},{7,6},{8,11},{9,8},{10,9... | collective-permute-start | bytes 196616 | tf_op jit(solution)/shard_map/ppermute | solution.py:26
  38.7 0.0 collective-permute-done.10.g1
  38.7 1.9 %collective-permute-done.11.g2 = bf16[2,2,4,16,128]{4,3,2,1,0:T(8,128)(2,1)S(1)} collective-permute-done((bf16[2,2,4,16,128]{4,3,2,1,0:T(8,128)(2,1)S(1)}, bf16[2,2,4,16,128]{4,3,2,1,0:T(8,128)(2,1)S(1)}, u32[]{:S(2)}, u32[]{:S(2)}) %collective-permute-start.11) | collective-permute-done | bytes 65568 | tf_op jit(solution)/shard_map/ppermute | solution.py:26
  40.6 0.4 collective-permute-done.12.g3
  41.0 0.0 copy-done.1
  41.0 9.6 %tile_pairs.1 = bf16[8,48,128]{2,1,0:T(8,128)(2,1)S(1)} custom-call(s32[1]{0:T(128)} %bitcast.me_ref, bf16[8,64,4096]{2,1,0:T(8,128)(2,1)} %t_ref.3, bf16[8,64,4096]{2,1,0:T(8,128)(2,1)} %prep.1.sw_ref, bf16[16,128]{1,0:T(8,128)(2,1)S(1)} %copy-done.1, bf16[2,2,4,16,128]{4,3,2,1,0:T(8,128)(2,1)S(1)} %get-tuple-element.31.g0, ...), custom_call_target="tpu_custom_call" | custom-call | tf_op jit(solution)/shard_map/tile_pairs/pallas_call | solution.py:210
  50.5 10.4 %all_to_all.20.t_ref = bf16[8,48,128]{2,1,0:T(8,128)(2,1)S(1)} all-to-all(bf16[8,48,128]{2,1,0:T(8,128)(2,1)S(1)} %tile_pairs.1), channel_id=1, replica_groups=mesh['z'=8,'h'=2,'l'=2,'c'=2,'x'=4] {'c','x'}, dimensions={0} | all-to-all | bytes 196608 | tf_op jit(solution)/shard_map/all_to_all | solution.py:289
  61.0 0.3 place.1
  61.3 12.7 %all_to_all.21.s_ref = bf16[32,16,128]{2,1,0:T(8,128)(2,1)S(1)} all-to-all(bf16[32,16,128]{2,1,0:T(8,128)(2,1)S(1)} %place.1), channel_id=1, replica_groups=mesh['z'=8,'h'=2,'l'=2,'c'=2,'x'=4] {'z','h','l'}, dimensions={0} | all-to-all | bytes 262144 | tf_op jit(solution)/shard_map/all_to_all | solution.py:291
  74.0 9.4 %all_to_all.22.p_ref = f32[8,8,128]{2,1,0:T(8,128)S(1)} all-to-all(f32[8,8,128]{2,1,0:T(8,128)S(1)} %sum.1), channel_id=1, replica_groups=mesh['z'=8,'h'=2,'l'=2,'c'=2,'x'=4] {'c','x'}, dimensions={0} | all-to-all | bytes 65536 | tf_op jit(solution)/shard_map/all_to_all | solution.py:293
  83.4 0.7 finish.1
  (1 shorter events, 0.0 us)
Async XLA Ops:
  1.4 16.8 %all-to-all-start = ((bf16[8,64,128]{2,1,0:T(8,128)(2,1)}), bf16[8,64,128]{2,1,0:T(8,128)(2,1)S(1)}, u32[]{:S(2)}, u32[]{:S(2)}) async-start(bf16[8,64,128]{2,1,0:T(8,128)(2,1)} %get-tuple-element.20), calls=%async_computation | async-start | bytes 262144 | tf_op jit(solution)/shard_map/all_to_all | solution.py:276
  10.5 22.5 %copy-start = (s32[2,8,128]{2,1,0:T(8,128)S(1)}, s32[2,8,128]{2,1,0:T(8,128)}, u32[]{:S(2)}) copy-start(s32[2,8,128]{2,1,0:T(8,128)} %get-tuple-element.24.w0) | copy-start | bytes 24580
  10.5 30.5 %copy-start.1 = (bf16[16,128]{1,0:T(8,128)(2,1)S(1)}, bf16[16,128]{1,0:T(8,128)(2,1)}, u32[]{:S(2)}) copy-start(bf16[16,128]{1,0:T(8,128)(2,1)} %get-tuple-element.23.target_ref) | copy-start | bytes 12292
  10.5 10.8 %collective-permute-start.5 = (s32[2,8,128]{2,1,0:T(8,128)}, s32[2,8,128]{2,1,0:T(8,128)S(1)}, u32[]{:S(2)}, u32[]{:S(2)}) collective-permute-start(s32[2,8,128]{2,1,0:T(8,128)} %get-tuple-element.24.w0), channel_id=1, source_target_pairs={{0,3},{1,0},{2,1},{3,2},{4,7},{5,4},{6,5},{7,6},{8,11},{9,8},{10,9... | collective-permute-start | bytes 24584 | tf_op jit(solution)/shard_map/ppermute | solution.py:26
  13.0 14.9 %collective-permute-start.4 = (s32[2,8,128]{2,1,0:T(8,128)}, s32[2,8,128]{2,1,0:T(8,128)S(1)}, u32[]{:S(2)}, u32[]{:S(2)}) collective-permute-start(s32[2,8,128]{2,1,0:T(8,128)} %get-tuple-element.24.w0), channel_id=1, source_target_pairs={{0,2},{1,3},{2,0},{3,1},{4,6},{5,7},{6,4},{7,5},{8,10},{9,11},{10,... | collective-permute-start | bytes 24584 | tf_op jit(solution)/shard_map/ppermute | solution.py:26
  13.5 17.5 %collective-permute-start.3 = (s32[2,8,128]{2,1,0:T(8,128)}, s32[2,8,128]{2,1,0:T(8,128)S(1)}, u32[]{:S(2)}, u32[]{:S(2)}) collective-permute-start(s32[2,8,128]{2,1,0:T(8,128)} %get-tuple-element.24.w0), channel_id=1, source_target_pairs={{0,1},{1,2},{2,3},{3,0},{4,5},{5,6},{6,7},{7,4},{8,9},{9,10},{10,1... | collective-permute-start | bytes 24584 | tf_op jit(solution)/shard_map/ppermute | solution.py:26
  18.2 12.8 %collective-permute-start.2 = (bf16[8,64,128]{2,1,0:T(8,128)(2,1)S(1)}, bf16[8,64,128]{2,1,0:T(8,128)(2,1)S(1)}, u32[]{:S(2)}, u32[]{:S(2)}) collective-permute-start(bf16[8,64,128]{2,1,0:T(8,128)(2,1)S(1)} %all-to-all-done.refs_0_), channel_id=1, source_target_pairs={{0,24},{8,0},{16,8},{24,16},{1,25},{9,1},{17,9},{25,17},{2,26},{10... | collective-permute-start | bytes 393224 | tf_op jit(solution)/shard_map/ppermute | solution.py:277
  21.0 10.1 %collective-permute-start.1 = (bf16[8,64,128]{2,1,0:T(8,128)(2,1)S(1)}, bf16[8,64,128]{2,1,0:T(8,128)(2,1)S(1)}, u32[]{:S(2)}, u32[]{:S(2)}) collective-permute-start(bf16[8,64,128]{2,1,0:T(8,128)(2,1)S(1)} %all-to-all-done.refs_0_), channel_id=1, source_target_pairs={{0,16},{8,24},{16,0},{24,8},{1,17},{9,25},{17,1},{25,9},{2,18},{10... | collective-permute-start | bytes 393224 | tf_op jit(solution)/shard_map/ppermute | solution.py:277
  21.3 9.7 %collective-permute-start = (bf16[8,64,128]{2,1,0:T(8,128)(2,1)S(1)}, bf16[8,64,128]{2,1,0:T(8,128)(2,1)S(1)}, u32[]{:S(2)}, u32[]{:S(2)}) collective-permute-start(bf16[8,64,128]{2,1,0:T(8,128)(2,1)S(1)} %all-to-all-done.refs_0_), channel_id=1, source_target_pairs={{0,8},{8,16},{16,24},{24,0},{1,9},{9,17},{17,25},{25,1},{2,10},{10... | collective-permute-start | bytes 393224 | tf_op jit(solution)/shard_map/ppermute | solution.py:277
  27.9 4.1 %collective-permute-start.6 = (bf16[8,64,128]{2,1,0:T(8,128)(2,1)S(1)}, bf16[8,64,128]{2,1,0:T(8,128)(2,1)S(1)}, u32[]{:S(2)}, u32[]{:S(2)}) collective-permute-start(bf16[8,64,128]{2,1,0:T(8,128)(2,1)S(1)} %all-to-all-done.refs_0_), channel_id=1, source_target_pairs={{0,4},{4,0},{1,5},{5,1},{2,6},{6,2},{3,7},{7,3},{8,12},{12,8},{9,1... | collective-permute-start | bytes 393224 | tf_op jit(solution)/shard_map/ppermute | solution.py:282
  31.0 1.4 %collective-permute-start.7 = (bf16[8,64,128]{2,1,0:T(8,128)(2,1)S(1)}, bf16[8,64,128]{2,1,0:T(8,128)(2,1)S(1)}, u32[]{:S(2)}, u32[]{:S(2)}) collective-permute-start(bf16[8,64,128]{2,1,0:T(8,128)(2,1)S(1)} %collective-permute-done.refs_1_), channel_id=1, source_target_pairs={{0,4},{4,0},{1,5},{5,1},{2,6},{6,2},{3,7},{7,3},{8,12},{12,8},{9,1... | collective-permute-start | bytes 393224 | tf_op jit(solution)/shard_map/ppermute | solution.py:282
  31.4 1.3 %collective-permute-start.8 = (bf16[8,64,128]{2,1,0:T(8,128)(2,1)S(1)}, bf16[8,64,128]{2,1,0:T(8,128)(2,1)S(1)}, u32[]{:S(2)}, u32[]{:S(2)}) collective-permute-start(bf16[8,64,128]{2,1,0:T(8,128)(2,1)S(1)} %collective-permute-done.1.refs_2_), channel_id=1, source_target_pairs={{0,4},{4,0},{1,5},{5,1},{2,6},{6,2},{3,7},{7,3},{8,12},{12,8},{9,1... | collective-permute-start | bytes 393224 | tf_op jit(solution)/shard_map/ppermute | solution.py:282
  31.6 1.3 %collective-permute-start.9 = (bf16[8,64,128]{2,1,0:T(8,128)(2,1)S(1)}, bf16[8,64,128]{2,1,0:T(8,128)(2,1)S(1)}, u32[]{:S(2)}, u32[]{:S(2)}) collective-permute-start(bf16[8,64,128]{2,1,0:T(8,128)(2,1)S(1)} %collective-permute-done.2.refs_3_), channel_id=1, source_target_pairs={{0,4},{4,0},{1,5},{5,1},{2,6},{6,2},{3,7},{7,3},{8,12},{12,8},{9,1... | collective-permute-start | bytes 393224 | tf_op jit(solution)/shard_map/ppermute | solution.py:282
  33.8 4.9 %collective-permute-start.10 = (bf16[2,2,4,16,128]{4,3,2,1,0:T(8,128)(2,1)S(1)}, bf16[2,2,4,16,128]{4,3,2,1,0:T(8,128)(2,1)S(1)}, u32[]{:S(2)}, u32[]{:S(2)}) collective-permute-start(bf16[2,2,4,16,128]{4,3,2,1,0:T(8,128)(2,1)S(1)} %get-tuple-element.32), channel_id=1, source_target_pairs={{0,1},{1,2},{2,3},{3,0},{4,5},{5,6},{6,7},{7,4},{8,9},{9,10},{10,1... | collective-permute-start | bytes 196616 | tf_op jit(solution)/shard_map/ppermute | solution.py:26
  35.1 5.5 %collective-permute-start.11 = (bf16[2,2,4,16,128]{4,3,2,1,0:T(8,128)(2,1)S(1)}, bf16[2,2,4,16,128]{4,3,2,1,0:T(8,128)(2,1)S(1)}, u32[]{:S(2)}, u32[]{:S(2)}) collective-permute-start(bf16[2,2,4,16,128]{4,3,2,1,0:T(8,128)(2,1)S(1)} %get-tuple-element.33), channel_id=1, source_target_pairs={{0,2},{1,3},{2,0},{3,1},{4,6},{5,7},{6,4},{7,5},{8,10},{9,11},{10,... | collective-permute-start | bytes 196616 | tf_op jit(solution)/shard_map/ppermute | solution.py:26
  37.6 3.4 %collective-permute-start.12 = (bf16[2,2,4,16,128]{4,3,2,1,0:T(8,128)(2,1)S(1)}, bf16[2,2,4,16,128]{4,3,2,1,0:T(8,128)(2,1)S(1)}, u32[]{:S(2)}, u32[]{:S(2)}) collective-permute-start(bf16[2,2,4,16,128]{4,3,2,1,0:T(8,128)(2,1)S(1)} %get-tuple-element.34), channel_id=1, source_target_pairs={{0,3},{1,0},{2,1},{3,2},{4,7},{5,4},{6,5},{7,6},{8,11},{9,8},{10,9... | collective-permute-start | bytes 196616 | tf_op jit(solution)/shard_map/ppermute | solution.py:26
